TPU v7x, 32 devices: a whole 2x2x4 slice. The times are simulated.
32 devices in a mesh: dp: 8 (over y, x, core), section: 4 (over z).
Axes of the slice: x: 2, y: 2, z: 4, core: 2. Of those that a mesh axis runs over, the one named last changes fastest.
Arguments:
- tokens: bfloat16 [32, 1024, 512], P('dp'), may hold values from -6 to 6
- resets: int32 [32, 1024], P('dp'), may hold values 0 or 1
- init_states: float32 [2, 32, 1024], P(None, 'dp'), may hold values from -6 to 6
- cotangent: bfloat16 [32, 1024, 512], P('dp'), may hold values from -6 to 6
- mix_gain: float32 [2, 512], replicated, may hold values from 0.5 to 1.5
- mix_in: bfloat16 [2, 512, 2048], replicated, may hold values from -0.25 to 0.25
- conv_weight: float32 [2, 4, 2048], replicated, may hold values from -3 to 3
- conv_bias: float32 [2, 2048], replicated, may hold values from -4.5 to 1.2
- mix_out: bfloat16 [2, 1024, 512], replicated, may hold values from -0.1875 to 0.1875
- mlp_gain: float32 [2, 512], replicated, may hold values from 0.5 to 1.5
- mlp_up: bfloat16 [2, 512, 2048], replicated, may hold values from -0.25 to 0.25
- up_bias: float32 [2, 2048], replicated, may hold values from -3 to 3
- mlp_down: bfloat16 [2, 2048, 512], replicated, may hold values from -0.125 to 0.125
- down_bias: float32 [2, 512], replicated, may hold values from -3 to 3
Outputs:
- activations: bfloat16 [4, 32, 1024, 512], P('section', 'dp')
- input_grads: bfloat16 [4, 32, 1024, 512], P('section', 'dp')
- final_states: float32 [2, 32, 1024], P(None, 'dp', 'section')
- mix_gain_grad: float32 [2, 512], P(None, ('dp', 'section'))
- mix_in_grad: float32 [2, 512, 2048], P(None, ('dp', 'section'))
- conv_weight_grad: float32 [2, 4, 2048], P(None, None, ('dp', 'section'))
- conv_bias_grad: float32 [2, 2048], P(None, ('dp', 'section'))
- mix_out_grad: float32 [2, 1024, 512], P(None, None, ('dp', 'section'))
- mlp_gain_grad: float32 [2, 512], P(None, ('dp', 'section'))
- mlp_up_grad: float32 [2, 512, 2048], P(None, ('dp', 'section'))
- up_bias_grad: float32 [2, 2048], P(None, ('dp', 'section'))
- mlp_down_grad: float32 [2, 2048, 512], P(None, None, ('dp', 'section'))
- down_bias_grad: float32 [2, 512], P(None, ('dp', 'section'))
All inputs are finite; a program needn't handle non-finite values. No bound on the sum of `resets` on one device may be relied on, other than what follows from the above.
Results may differ from a plain program's by a relative error of at most 0.012.
Values may be sent and summed in bfloat16 or wider, within the bound.
A program may use at most 640 MiB of HBM per device.

v0:
```python
import jax
import jax.numpy as jnp
from jax import lax
from jax.sharding import PartitionSpec as P

MICRO = 4


EPSILON = 1e-06


def for_sending(x):
    return jax.tree.map(lambda a: a.astype(jnp.bfloat16) if a.dtype == jnp.float32 else a, x)


def shifted(x, axis, by):
    count = lax.axis_size(axis)
    pairs = [(i, i + by) for i in range(count) if 0 <= i + by < count]
    return lax.ppermute(x, axis, pairs)


def scaled_norm(values, norm_gain):
    return (
        values * lax.rsqrt(jnp.mean(values * values, axis=-1, keepdims=True) + EPSILON) * norm_gain
    )


def delay(values, amount):
    return jnp.concatenate(
        [jnp.zeros_like(values[..., :amount, :]), values[..., :-amount, :]], axis=-2
    )


def delay_ones(values, amount):
    return jnp.concatenate(
        [jnp.ones_like(values[..., :amount, :]), values[..., :-amount, :]], axis=-2
    )


def linear_chain(earlier, latter):
    return (earlier[0] * latter[0], latter[0] * earlier[1] + latter[1])


def recurrence(projected, kernel, shift_bias, initial, continuing):
    convolved = shift_bias + kernel[0] * projected
    window = continuing
    for offset in range(1, kernel.shape[0]):
        if offset > 1:
            window = window * delay_ones(continuing, offset - 1)
        convolved = convolved + kernel[offset] * window * delay(projected, offset)
    midpoint = projected.shape[-1] // 2
    update = jax.nn.sigmoid(convolved[..., :midpoint])
    candidate = convolved[..., midpoint:]
    retain = (1.0 - update) * continuing
    inject = update * candidate
    opening = inject[..., :1, :] + retain[..., :1, :] * initial[..., None, :]
    inject = jnp.concatenate([opening, inject[..., 1:, :]], axis=-2)
    return lax.associative_scan(linear_chain, (retain, inject), axis=projected.ndim - 2)[1]


def smooth_gate(values):
    return jax.nn.gelu(values, approximate=True)


def flat_rows(values):
    return values.reshape(-1, values.shape[-1])


def inner_rows(left, right):
    return lax.dot_general(
        flat_rows(left),
        flat_rows(right),
        (((0,), (0,)), ((), ())),
        preferred_element_type=jnp.float32,
    )


def times_weight(values, weight):
    out_shape = values.shape[:-1] + (weight.shape[1],)
    return jnp.dot(flat_rows(values), weight, preferred_element_type=jnp.float32).reshape(out_shape)


def times_weight_back(values, weight):
    out_shape = values.shape[:-1] + (weight.shape[0],)
    return lax.dot_general(
        flat_rows(values), weight, (((1,), (1,)), ((), ())), preferred_element_type=jnp.float32
    ).reshape(out_shape)


def mixer_forward(inputs, continuing, initial, weights):
    norm_gain, weight_in, kernel, shift_bias, weight_out = weights
    source = inputs.astype(jnp.float32)
    normed = scaled_norm(source, norm_gain).astype(jnp.bfloat16)
    projected = times_weight(normed, weight_in)
    hidden = recurrence(projected, kernel, shift_bias, initial, continuing)
    branch = times_weight(hidden.astype(jnp.bfloat16), weight_out)
    return ((source + branch).astype(jnp.bfloat16), hidden[:, -1, :])


def mixer_backward(inputs, continuing, initial, weights, upstream):
    norm_gain, weight_in, kernel, shift_bias, weight_out = weights
    source = inputs.astype(jnp.float32)
    normed_full, norm_pull = jax.vjp(scaled_norm, source, norm_gain)
    normed = normed_full.astype(jnp.bfloat16)
    projected = times_weight(normed, weight_in)

    def recur_piece(proj_values, kernel_values, bias_values):
        return recurrence(proj_values, kernel_values, bias_values, initial, continuing)

    hidden, recur_pull = jax.vjp(recur_piece, projected, kernel, shift_bias)
    hidden_low = hidden.astype(jnp.bfloat16)
    grad_out = inner_rows(hidden_low, upstream)
    grad_hidden = times_weight_back(upstream, weight_out)
    grad_proj, grad_kernel, grad_bias = recur_pull(grad_hidden)
    grad_proj_low = grad_proj.astype(jnp.bfloat16)
    grad_in = inner_rows(normed, grad_proj_low)
    grad_normed = times_weight_back(grad_proj_low, weight_in)
    grad_source, grad_gain = norm_pull(grad_normed)
    outgoing = (upstream.astype(jnp.float32) + grad_source).astype(jnp.bfloat16)
    return (outgoing, (grad_gain, grad_in, grad_kernel, grad_bias, grad_out))


def mlp_forward(inputs, weights):
    norm_gain, weight_up, bias_up, weight_down, bias_down = weights
    source = inputs.astype(jnp.float32)
    normed = scaled_norm(source, norm_gain).astype(jnp.bfloat16)
    pre_act = times_weight(normed, weight_up) + bias_up
    active = smooth_gate(pre_act).astype(jnp.bfloat16)
    return (source + times_weight(active, weight_down) + bias_down).astype(jnp.bfloat16)


def mlp_backward(inputs, weights, upstream):
    norm_gain, weight_up, bias_up, weight_down, bias_down = weights
    source = inputs.astype(jnp.float32)
    normed_full, norm_pull = jax.vjp(scaled_norm, source, norm_gain)
    normed = normed_full.astype(jnp.bfloat16)
    pre_act = times_weight(normed, weight_up) + bias_up
    active_full, gate_pull = jax.vjp(smooth_gate, pre_act)
    active = active_full.astype(jnp.bfloat16)
    grad_down = inner_rows(active, upstream)
    grad_bias_down = jnp.sum(flat_rows(upstream), axis=0, dtype=jnp.float32)
    grad_active = times_weight_back(upstream, weight_down)
    grad_pre = gate_pull(grad_active)[0]
    grad_pre_low = grad_pre.astype(jnp.bfloat16)
    grad_bias_up = jnp.sum(flat_rows(grad_pre_low), axis=0, dtype=jnp.float32)
    grad_up = inner_rows(normed, grad_pre_low)
    grad_normed = times_weight_back(grad_pre_low, weight_up)
    grad_source, grad_gain = norm_pull(grad_normed)
    outgoing = (upstream.astype(jnp.float32) + grad_source).astype(jnp.bfloat16)
    return (outgoing, (grad_gain, grad_up, grad_bias_up, grad_down, grad_bias_down))


def reduce_everything(mix_final, mlp_final):
    return (
        lax.psum_scatter(mix_final[0], ("dp", "section"), scatter_dimension=1, tiled=True),
        lax.psum_scatter(mix_final[1], ("dp", "section"), scatter_dimension=1, tiled=True),
        lax.psum_scatter(mix_final[2], ("dp", "section"), scatter_dimension=2, tiled=True),
        lax.psum_scatter(mix_final[3], ("dp", "section"), scatter_dimension=1, tiled=True),
        lax.psum_scatter(mix_final[4], ("dp", "section"), scatter_dimension=2, tiled=True),
        lax.psum_scatter(mlp_final[0], ("dp", "section"), scatter_dimension=1, tiled=True),
        lax.psum_scatter(mlp_final[1], ("dp", "section"), scatter_dimension=1, tiled=True),
        lax.psum_scatter(mlp_final[2], ("dp", "section"), scatter_dimension=1, tiled=True),
        lax.psum_scatter(mlp_final[3], ("dp", "section"), scatter_dimension=2, tiled=True),
        lax.psum_scatter(mlp_final[4], ("dp", "section"), scatter_dimension=1, tiled=True),
    )


def store_slot(buffer, values, slot_index, active):
    previous = lax.dynamic_index_in_dim(buffer, slot_index, 0, keepdims=False)
    chosen = jnp.where(active, values, previous)
    return lax.dynamic_update_index_in_dim(buffer, chosen, slot_index, 0)


def body(
    tokens,
    resets,
    init_states,
    cotangent,
    mix_gain,
    mix_in,
    conv_weight,
    conv_bias,
    mix_out,
    mlp_gain,
    mlp_up,
    up_bias,
    mlp_down,
    down_bias,
):
    sections = lax.axis_size("section")
    section_index = lax.axis_index("section")
    micro_count = MICRO
    local_rows = tokens.shape[0] // micro_count
    block_shape = (local_rows,) + tokens.shape[1:]
    hidden_width = init_states.shape[2]
    continuing_all = (1 - resets).astype(jnp.float32)[..., None]
    mix_stack = (mix_gain, mix_in, conv_weight, conv_bias, mix_out)
    mlp_stack = (mlp_gain, mlp_up, up_bias, mlp_down, down_bias)
    mix_zero = tuple((jnp.zeros(stacked.shape[1:], jnp.float32) for stacked in mix_stack))
    mlp_zero = tuple((jnp.zeros(stacked.shape[1:], jnp.float32) for stacked in mlp_stack))

    def take_rows(values, which, axis_no):
        return lax.dynamic_slice_in_dim(values, which * local_rows, local_rows, axis_no)

    layer_no = section_index // 2
    kind_flag = section_index % 2
    mix_weights = tuple(
        (lax.dynamic_index_in_dim(stacked, layer_no, 0, keepdims=False) for stacked in mix_stack)
    )
    mlp_weights = tuple(
        (lax.dynamic_index_in_dim(stacked, layer_no, 0, keepdims=False) for stacked in mlp_stack)
    )
    initial_all = lax.dynamic_index_in_dim(init_states, layer_no, 0, keepdims=False)
    state_zero = jnp.zeros((local_rows, hidden_width), jnp.float32)

    def spare_forward(incoming, continuing, initial):
        return (jnp.zeros(block_shape, jnp.bfloat16), state_zero)

    def mixer_branch(incoming, continuing, initial):
        return mixer_forward(incoming, continuing, initial, mix_weights)

    def mlp_branch(incoming, continuing, initial):
        return (mlp_forward(incoming, mlp_weights), state_zero)

    def spare_backward(incoming, continuing, initial, upstream):
        return (jnp.zeros(block_shape, jnp.bfloat16), mix_zero, mlp_zero)

    def mixer_back_branch(incoming, continuing, initial, upstream):
        outgoing, terms = mixer_backward(incoming, continuing, initial, mix_weights, upstream)
        return (outgoing, terms, mlp_zero)

    def mlp_back_branch(incoming, continuing, initial, upstream):
        outgoing, terms = mlp_backward(incoming, mlp_weights, upstream)
        return (outgoing, mix_zero, terms)

    tick_total = micro_count + sections - 1
    section_inputs = jnp.zeros((micro_count,) + block_shape, jnp.bfloat16)
    section_outputs = jnp.zeros((micro_count,) + block_shape, jnp.bfloat16)
    finals = jnp.zeros((micro_count, local_rows, hidden_width), jnp.float32)
    received = jnp.zeros(block_shape, jnp.bfloat16)
    for tick_index in range(tick_total):
        batch_index = tick_index - section_index
        active = (batch_index >= 0) & (batch_index < micro_count)
        slot_index = jnp.clip(batch_index, 0, micro_count - 1)
        incoming = jnp.where(section_index == 0, take_rows(tokens, slot_index, 0), received)
        continuing = take_rows(continuing_all, slot_index, 0)
        initial = take_rows(initial_all, slot_index, 0)
        selector = jnp.where(active, 1 + kind_flag, 0)
        result, final_state = lax.switch(
            selector, (spare_forward, mixer_branch, mlp_branch), incoming, continuing, initial
        )
        section_inputs = store_slot(section_inputs, incoming, slot_index, active)
        section_outputs = store_slot(section_outputs, result, slot_index, active)
        finals = store_slot(finals, final_state, slot_index, active)
        if tick_index + 1 < tick_total:
            received = jax.tree.map(
                lambda part, own: part.astype(own.dtype),
                shifted(for_sending(result), "section", 1),
                result,
            )
    grad_inputs = jnp.zeros((micro_count,) + block_shape, jnp.bfloat16)
    mix_totals = mix_zero
    mlp_totals = mlp_zero
    received = jnp.zeros(block_shape, jnp.bfloat16)
    for tick_index in range(tick_total):
        batch_index = tick_index - (sections - 1 - section_index)
        active = (batch_index >= 0) & (batch_index < micro_count)
        slot_index = jnp.clip(batch_index, 0, micro_count - 1)
        upstream = jnp.where(
            section_index == sections - 1, take_rows(cotangent, slot_index, 0), received
        )
        incoming = lax.dynamic_index_in_dim(section_inputs, slot_index, 0, keepdims=False)
        continuing = take_rows(continuing_all, slot_index, 0)
        initial = take_rows(initial_all, slot_index, 0)
        selector = jnp.where(active, 1 + kind_flag, 0)
        outgoing, mix_terms, mlp_terms = lax.switch(
            selector,
            (spare_backward, mixer_back_branch, mlp_back_branch),
            incoming,
            continuing,
            initial,
            upstream,
        )
        mix_totals = tuple((total + term for total, term in zip(mix_totals, mix_terms)))
        mlp_totals = tuple((total + term for total, term in zip(mlp_totals, mlp_terms)))
        grad_inputs = store_slot(grad_inputs, outgoing, slot_index, active)
        if tick_index + 1 < tick_total:
            received = jax.tree.map(
                lambda part, own: part.astype(own.dtype),
                shifted(for_sending(outgoing), "section", -1),
                outgoing,
            )
    activations = section_outputs.reshape((1, micro_count * local_rows) + tokens.shape[1:])
    input_grads = grad_inputs.reshape((1, micro_count * local_rows) + tokens.shape[1:])
    spread_states = lax.all_to_all(
        finals.reshape(1, micro_count * local_rows, hidden_width),
        "section",
        split_axis=2,
        concat_axis=0,
        tiled=True,
    )
    final_states = spread_states[0::2]
    level_mask = (jnp.arange(2) == layer_no).astype(jnp.float32)
    mix_final = tuple(
        (level_mask.reshape((2,) + (1,) * total.ndim) * total[None] for total in mix_totals)
    )
    mlp_final = tuple(
        (level_mask.reshape((2,) + (1,) * total.ndim) * total[None] for total in mlp_totals)
    )
    grads = reduce_everything(mix_final, mlp_final)
    return (activations, input_grads, final_states) + tuple(grads)


def solution(mesh):
    return jax.shard_map(
        body,
        mesh=mesh,
        in_specs=(
            P("dp", None, None),
            P("dp", None),
            P(None, "dp", None),
            P("dp", None, None),
            P(),
            P(),
            P(),
            P(),
            P(),
            P(),
            P(),
            P(),
            P(),
            P(),
        ),
        out_specs=(
            P("section", "dp", None, None),
            P("section", "dp", None, None),
            P(None, "dp", "section"),
            P(None, ("dp", "section")),
            P(None, ("dp", "section"), None),
            P(None, None, ("dp", "section")),
            P(None, ("dp", "section")),
            P(None, None, ("dp", "section")),
            P(None, ("dp", "section")),
            P(None, ("dp", "section"), None),
            P(None, ("dp", "section")),
            P(None, None, ("dp", "section")),
            P(None, ("dp", "section")),
        ),
        check_vma=False,
    )
```

profile of v0, /device:TPU:0, one launch (start us, length us, event | category | flops | bytes accessed | tf_op | source)
XLA Modules:
  0.0 6855.5 jit_solution(17372174832339075758)
XLA Ops:
  23.0 286.8 %conditional.14 = (bf16[1,1024,512]{2,1,0:T(8,128)(2,1)}, f32[1,1024]{1,0:T(1,128)S(1)}) conditional(s32[]{:T(128)} %clamp.154, () %tuple.204, (bf16[1,1024,512]{2,1,0:T(8,128)(2,1)S(1)}, f32[2048]{0:T(1024)S(1)}, f32[4,2048]{1,0:T(4,128)S(1)}, f32[512]{0:T(512)}, bf16[512,2048]{1,0:T(8,128)(2,1)S(1)}, ...), branch_computations={%region_0.1_spmd, %region_1.3_spmd, %region_3.5_spmd} | conditional | flops 4321707008 | bytes 291166656 | solution.py:249
  283.3 16.7 pad.3253
  312.7 22.1 collective-permute-done
  337.5 286.3 %conditional.15 = (bf16[1,1024,512]{2,1,0:T(8,128)(2,1)}, f32[1,1024]{1,0:T(1,128)S(1)}) conditional(s32[]{:T(128)} %clamp.155, () %tuple.207, (bf16[1,1024,512]{2,1,0:T(8,128)(2,1)S(1)}, f32[2048]{0:T(1024)S(1)}, f32[4,2048]{1,0:T(4,128)S(1)}, f32[512]{0:T(512)}, bf16[512,2048]{1,0:T(8,128)(2,1)S(1)}, ...), branch_computations={%region_5.6_spmd, %region_6.8_spmd, %region_8.10_spmd} | conditional | flops 4321707008 | bytes 291166656 | solution.py:249
  597.4 16.6 pad.3273
  626.6 21.5 collective-permute-done.1
  650.8 286.1 %conditional.16 = (bf16[1,1024,512]{2,1,0:T(8,128)(2,1)}, f32[1,1024]{1,0:T(1,128)S(1)}) conditional(s32[]{:T(128)} %clamp.156, () %tuple.210, (bf16[1,1024,512]{2,1,0:T(8,128)(2,1)S(1)}, f32[2048]{0:T(1024)S(1)}, f32[4,2048]{1,0:T(4,128)S(1)}, f32[512]{0:T(512)}, bf16[512,2048]{1,0:T(8,128)(2,1)S(1)}, ...), branch_computations={%region_10.11_spmd, %region_11.13_spmd, %region_13.15_spmd} | conditional | flops 4321707008 | bytes 291166656 | solution.py:249
  910.5 16.8 pad.3293
  939.7 20.9 collective-permute-done.2
  963.3 286.3 %conditional.17 = (bf16[1,1024,512]{2,1,0:T(8,128)(2,1)}, f32[1,1024]{1,0:T(1,128)S(1)}) conditional(s32[]{:T(128)} %clamp.157, () %tuple.213, (bf16[1,1024,512]{2,1,0:T(8,128)(2,1)S(1)}, f32[2048]{0:T(1024)S(1)}, f32[4,2048]{1,0:T(4,128)S(1)}, f32[512]{0:T(512)}, bf16[512,2048]{1,0:T(8,128)(2,1)S(1)}, ...), branch_computations={%region_15.16_spmd, %region_16.18_spmd, %region_18.20_spmd} | conditional | flops 4321707008 | bytes 291166656 | solution.py:249
  1222.9 16.7 pad.3313
  1252.5 20.3 collective-permute-done.3
  1296.2 19.4 collective-permute-done.4
  1372.6 304.2 %collective-permute-done.6 = bf16[1,1024,512]{2,1,0:T(8,128)(2,1)S(1)} collective-permute-done((bf16[1,1024,512]{2,1,0:T(8,128)(2,1)}, bf16[1,1024,512]{2,1,0:T(8,128)(2,1)S(1)}, u32[]{:S(2)}, u32[]{:S(2)}) %collective-permute-start.6) | collective-permute-done | bytes 1048608 | tf_op jit(solution)/shard_map/ppermute | solution.py:19
  1696.1 21.0 collective-permute-done.7
  1734.5 727.8 %collective-permute-done.8 = bf16[1,1024,512]{2,1,0:T(8,128)(2,1)S(1)} collective-permute-done((bf16[1,1024,512]{2,1,0:T(8,128)(2,1)}, bf16[1,1024,512]{2,1,0:T(8,128)(2,1)S(1)}, u32[]{:S(2)}, u32[]{:S(2)}) %collective-permute-start.8) | collective-permute-done | bytes 1048608 | tf_op jit(solution)/shard_map/ppermute | solution.py:19
  2464.7 668.5 %conditional.24 = (bf16[1,1024,512]{2,1,0:T(8,128)(2,1)}, f32[512]{0:T(512)}, f32[512,2048]{1,0:T(8,128)}, f32[4,2048]{1,0:T(4,128)S(1)}, f32[2048]{0:T(1024)}, ...) conditional(s32[]{:T(128)} %clamp.164, () %tuple.234, ...), branch_computations={%region_83.84_spmd, %region_84.93_spmd, %region_93.99_spmd} | conditional | flops 10821832704 | bytes 994280896 | solution.py:276
  2902.3 16.7 pad.3821
  2935.5 16.7 pad.3757
  2978.4 16.9 pad.3843
  3049.4 17.2 fusion.719
  3134.5 63.8 collective-permute-done.9
  3200.7 709.4 %conditional.25 = (bf16[1,1024,512]{2,1,0:T(8,128)(2,1)}, f32[512]{0:T(512)S(1)}, f32[512,2048]{1,0:T(8,128)}, f32[4,2048]{1,0:T(4,128)S(1)}, f32[2048]{0:T(1024...) conditional(s32[]{:T(128)} %clamp.165, () %tuple.237, ...), branch_computations={%region_99.100_spmd, %region_100.109_spmd, %region_109.115_spmd} | conditional | flops 10821832704 | bytes 997426560 | solution.py:276
  3696.4 16.7 pad.3948
  3722.2 16.8 pad.3884
  3774.3 16.6 pad.3996
  3858.2 16.6 pad.4007
  3911.4 18.9 collective-permute-done.10
  3932.7 668.9 %conditional.26 = (bf16[1,1024,512]{2,1,0:T(8,128)(2,1)}, f32[512]{0:T(512)}, f32[512,2048]{1,0:T(8,128)}, f32[4,2048]{1,0:T(4,128)S(1)}, f32[2048]{0:T(1024)}, ...) conditional(s32[]{:T(128)} %clamp.166, () %tuple.240, ...), branch_computations={%region_115.116_spmd, %region_116.125_spmd, %region_125.131_spmd} | conditional | flops 10821832704 | bytes 994280896 | solution.py:276
  4404.2 16.7 pad.4011
  4447.1 16.7 pad.4097
  4517.9 17.3 fusion.891
  4549.1 16.7 pad.4134
  4603.5 17.5 collective-permute-done.11
  4623.3 717.3 %conditional.27 = (bf16[1,1024,512]{2,1,0:T(8,128)(2,1)}, f32[512]{0:T(512)S(1)}, f32[512,2048]{1,0:T(8,128)}, f32[4,2048]{1,0:T(4,128)}, f32[2048]{0:T(1024)}, ...) conditional(s32[]{:T(128)} %clamp.167, () %tuple.243, ...), branch_computations={%region_131.132_spmd, %region_132.141_spmd, %region_141.147_spmd} | conditional | flops 10821832704 | bytes 997426560 | solution.py:276
  5119.8 16.7 pad.4202
  5145.5 16.8 pad.4138
  5252.1 17.2 fusion.977
  5304.0 16.8 pad.4262
  5485.4 86.4 %dynamic_update_slice.116 = f32[1,4,1024]{1,0,2:T(1,128)S(1)} dynamic-update-slice(f32[1,4,1024]{1,0,2:T(1,128)S(1)} %bitcast.1150, f32[1,1,1024]{1,0,2:T(1,128)S(1)} %copy.94, s32[]{:T(128)} %constant.1341.clone.1, s32[]{:T(128)} %min.77, s32[]{:T(128)} %constant.1341.clone.1) | dynamic-update-slice | bytes 8196 | tf_op jit(solution)/shard_map/jit(dynamic_update_index_in_dim)/dynamic_update_slice | solution.py:171
  5612.0 127.0 %reduce-scatter.41.cloned.1.call-done = f32[16,2]{1,0:T(8,128)} async-done(((f32[512,2]{1,0:T(8,128)}), f32[16,2]{1,0:T(8,128)}) %reduce-scatter.41.cloned.1.call-update) | async-done | bytes 144
  5740.3 132.6 %reduce-scatter.35.cloned.1.call-done = f32[64,2]{1,0:T(8,128)} async-done(((f32[2048,2]{1,0:T(8,128)}), f32[64,2]{1,0:T(8,128)}) %reduce-scatter.35.cloned.1.call-update) | async-done | bytes 528
  5874.3 132.6 %reduce-scatter.39.cloned.1.call-done = f32[64,2]{1,0:T(8,128)} async-done(((f32[2048,2]{1,0:T(8,128)}), f32[64,2]{1,0:T(8,128)}) %reduce-scatter.39.cloned.1.call-update) | async-done | bytes 528
  6008.2 132.7 %reduce-scatter.33.cloned.1.call-done = f32[64,8]{1,0:T(8,128)} async-done(((f32[2048,8]{1,0:T(8,128)}), f32[64,8]{1,0:T(8,128)}) %reduce-scatter.33.cloned.1.call-update) | async-done | bytes 2064
  6142.5 145.8 %reduce-scatter.25.cloned.1.call-done = f32[2,1024,16]{1,2,0:T(8,128)} async-done(((f32[2,1024,512]{1,2,0:T(8,128)}), f32[2,1024,16]{1,2,0:T(8,128)}) %reduce-scatter.25.cloned.1.call-update) | async-done | bytes 131088 | tf_op jit(solution)/shard_map/reduce_scatter | solution.py:159
  6288.3 187.4 %reduce-scatter.23.cloned.1.call-done = f32[2,16,2048]{2,1,0:T(8,128)} async-done(((f32[2,512,2048]{2,1,0:T(8,128)}), f32[2,16,2048]{2,1,0:T(8,128)}) %reduce-scatter.23.cloned.1.call-update) | async-done | bytes 262160 | tf_op jit(solution)/shard_map/reduce_scatter | solution.py:156
  6475.6 186.4 %reduce-scatter.27.cloned.1.call-done = f32[2,16,2048]{2,1,0:T(8,128)} async-done(((f32[2,512,2048]{2,1,0:T(8,128)}), f32[2,16,2048]{2,1,0:T(8,128)}) %reduce-scatter.27.cloned.1.call-update) | async-done | bytes 262160 | tf_op jit(solution)/shard_map/reduce_scatter | solution.py:161
  6662.1 186.2 %reduce-scatter.29.cloned.1.call-done = f32[2,2048,16]{1,2,0:T(8,128)} async-done(((f32[2,2048,512]{1,2,0:T(8,128)}), f32[2,2048,16]{1,2,0:T(8,128)}) %reduce-scatter.29.cloned.1.call-update) | async-done | bytes 262160 | tf_op jit(solution)/shard_map/reduce_scatter | solution.py:163
  (2764 shorter events, 3926.8 us)
Async XLA Ops:
  7.2 5602.1 %reduce-scatter.31.cloned.1.call-start = ((), (), s32[]{:S(2)}) async-start(), calls=%async_computation.15 | async-start | bytes 270336
  10.2 1346.9 %copy-start.35 = (bf16[1024,512]{1,0:T(8,128)(2,1)}, bf16[1024,512]{1,0:T(8,128)(2,1)S(1)}, u32[]{:S(2)}) copy-start(bf16[1024,512]{1,0:T(8,128)(2,1)S(1)} %dynamic-slice_bitcast_fusion.10) | copy-start | bytes 3145732
  154.9 53.9 copy-start.280
  309.9 24.9 collective-permute-start
  469.4 53.8 copy-start.281
  623.8 24.3 collective-permute-start.1
  782.8 53.8 copy-start.282
  936.9 23.8 collective-permute-start.2
  1249.7 23.1 collective-permute-start.3
  1279.4 36.1 collective-permute-start.4
  1323.6 27.9 collective-permute-start.5
  1371.3 307.9 %copy-start.588 = (f32[4,2048]{1,0:T(4,128)}, f32[4,2048]{1,0:T(4,128)S(1)}, u32[]{:S(2)}) copy-start(f32[4,2048]{1,0:T(4,128)S(1)} %get-tuple-element.1420) | copy-start | bytes 98308
  1371.3 307.9 %copy-start.728 = (f32[2048]{0:T(1024)}, f32[2048]{0:T(1024)S(1)}, u32[]{:S(2)}) copy-start(f32[2048]{0:T(1024)S(1)} %get-tuple-element.1427) | copy-start | bytes 24580
  1371.3 307.9 %copy-start.729 = (f32[2048]{0:T(1024)}, f32[2048]{0:T(1024)S(1)}, u32[]{:S(2)}) copy-start(f32[2048]{0:T(1024)S(1)} %get-tuple-element.1455) | copy-start | bytes 24580
  1371.3 307.9 %copy-start.757 = (f32[512]{0:T(512)}, f32[512]{0:T(512)S(1)}, u32[]{:S(2)}) copy-start(f32[512]{0:T(512)S(1)} %get-tuple-element.1406) | copy-start | bytes 6148
  1371.3 307.9 %copy-start.758 = (f32[512]{0:T(512)}, f32[512]{0:T(512)S(1)}, u32[]{:S(2)}) copy-start(f32[512]{0:T(512)S(1)} %get-tuple-element.1469) | copy-start | bytes 6148
  1371.3 305.5 %collective-permute-start.6 = (bf16[1,1024,512]{2,1,0:T(8,128)(2,1)}, bf16[1,1024,512]{2,1,0:T(8,128)(2,1)S(1)}, u32[]{:S(2)}, u32[]{:S(2)}) collective-permute-start(bf16[1,1024,512]{2,1,0:T(8,128)(2,1)} %get-tuple-element.1392), channel_id=1, source_target_pairs={{1,0},{2,1},{3,2},{5,4},{6,5},{7,6},{9,8},{10,9},{11,10},{13,12},{... | collective-permute-start | bytes 3145736 | tf_op jit(solution)/shard_map/ppermute | solution.py:19
  1694.8 22.3 collective-permute-start.7
  1733.1 731.5 %copy-start.592 = (f32[4,2048]{1,0:T(4,128)}, f32[4,2048]{1,0:T(4,128)S(1)}, u32[]{:S(2)}) copy-start(f32[4,2048]{1,0:T(4,128)S(1)} %get-tuple-element.1422) | copy-start | bytes 98308
  1733.1 731.5 %copy-start.731 = (f32[2048]{0:T(1024)}, f32[2048]{0:T(1024)S(1)}, u32[]{:S(2)}) copy-start(f32[2048]{0:T(1024)S(1)} %get-tuple-element.1429) | copy-start | bytes 24580
  1733.2 731.5 %copy-start.732 = (f32[2048]{0:T(1024)}, f32[2048]{0:T(1024)S(1)}, u32[]{:S(2)}) copy-start(f32[2048]{0:T(1024)S(1)} %get-tuple-element.1457) | copy-start | bytes 24580
  1733.2 731.5 %copy-start.760 = (f32[512]{0:T(512)}, f32[512]{0:T(512)S(1)}, u32[]{:S(2)}) copy-start(f32[512]{0:T(512)S(1)} %get-tuple-element.1408) | copy-start | bytes 6148
  1733.2 731.5 %copy-start.761 = (f32[512]{0:T(512)}, f32[512]{0:T(512)S(1)}, u32[]{:S(2)}) copy-start(f32[512]{0:T(512)S(1)} %get-tuple-element.1443) | copy-start | bytes 6148
  1733.2 731.5 %copy-start.762 = (f32[512]{0:T(512)}, f32[512]{0:T(512)S(1)}, u32[]{:S(2)}) copy-start(f32[512]{0:T(512)S(1)} %get-tuple-element.1471) | copy-start | bytes 6148
  1733.2 729.2 %collective-permute-start.8 = (bf16[1,1024,512]{2,1,0:T(8,128)(2,1)}, bf16[1,1024,512]{2,1,0:T(8,128)(2,1)S(1)}, u32[]{:S(2)}, u32[]{:S(2)}) collective-permute-start(bf16[1,1024,512]{2,1,0:T(8,128)(2,1)} %get-tuple-element.1394), channel_id=1, source_target_pairs={{1,0},{2,1},{3,2},{5,4},{6,5},{7,6},{9,8},{10,9},{11,10},{13,12},{... | collective-permute-start | bytes 3145736 | tf_op jit(solution)/shard_map/ppermute | solution.py:19
  2464.7 736.0 %copy-start.23 = (bf16[1,1024,512]{2,1,0:T(8,128)(2,1)S(1)}, bf16[1,1024,512]{2,1,0:T(8,128)(2,1)}, u32[]{:S(2)}) copy-start(bf16[1,1024,512]{2,1,0:T(8,128)(2,1)} %get-tuple-element.2595) | copy-start | bytes 3145732
  3133.2 67.5 copy-start.594
  3133.2 67.5 copy-start.733
  3133.2 67.5 copy-start.763
  3133.2 65.1 collective-permute-start.9
  3512.1 55.6 copy-start.487
  3515.7 54.2 copy-start.265
  3910.1 20.2 collective-permute-start.10
  3932.7 690.6 %copy-start.18 = (bf16[1,1024,512]{2,1,0:T(8,128)(2,1)S(1)}, bf16[1,1024,512]{2,1,0:T(8,128)(2,1)}, u32[]{:S(2)}) copy-start(bf16[1,1024,512]{2,1,0:T(8,128)(2,1)} %get-tuple-element.2593) | copy-start | bytes 3145732
  4601.6 19.3 collective-permute-start.11
  4935.5 55.6 copy-start.488
  4939.1 54.3 copy-start.269
  5344.4 266.2 %reduce-scatter.37.cloned.1.call-start = ((), (), s32[]{:S(2)}) async-start(), calls=%async_computation.18 | async-start | bytes 270336
  5345.4 393.6 %reduce-scatter.41.cloned.1.call-start = ((), (), s32[]{:S(2)}) async-start(), calls=%async_computation.20 | async-start | bytes 270336
  5346.3 526.5 %reduce-scatter.35.cloned.1.call-start = ((), (), s32[]{:S(2)}) async-start(), calls=%async_computation.17 | async-start | bytes 1081344
  5350.1 656.8 %reduce-scatter.39.cloned.1.call-start = ((), (), s32[]{:S(2)}) async-start(), calls=%async_computation.19 | async-start | bytes 1081344
  5351.5 789.4 %reduce-scatter.33.cloned.1.call-start = ((), (), s32[]{:S(2)}) async-start(), calls=%async_computation.16 | async-start | bytes 1081344
  5366.2 922.1 %reduce-scatter.25.cloned.1.call-start = ((), (), s32[]{:S(2)}) async-start(), calls=%async_computation.12 | async-start | bytes 4325376 | tf_op jit(solution)/shard_map/reduce_scatter | solution.py:159
  5368.9 1106.7 %reduce-scatter.23.cloned.1.call-start = ((), (), s32[]{:S(2)}) async-start(), calls=%async_computation.11 | async-start | bytes 8650752 | tf_op jit(solution)/shard_map/reduce_scatter | solution.py:156
  5408.0 1254.0 %reduce-scatter.27.cloned.1.call-start = ((), (), s32[]{:S(2)}) async-start(), calls=%async_computation.13 | async-start | bytes 8650752 | tf_op jit(solution)/shard_map/reduce_scatter | solution.py:161
  5408.8 1439.5 %reduce-scatter.29.cloned.1.call-start = ((), (), s32[]{:S(2)}) async-start(), calls=%async_computation.14 | async-start | bytes 8650752 | tf_op jit(solution)/shard_map/reduce_scatter | solution.py:163
  5575.2 8.8 all-to-all-start
  5601.9 1246.4 %copy-start.1 = (bf16[2,1024,512]{2,1,0:T(8,128)(2,1)S(1)}, bf16[2,1024,512]{2,1,0:T(8,128)(2,1)}, u32[]{:S(2)}) copy-start(bf16[2,1024,512]{2,1,0:T(8,128)(2,1)} %param.64) | copy-start | bytes 6291460
  (463 other events, 4762.3 us)
Sparse Core Ops, SparseCore 0:
  5344.6 129.2 reduce-scatter.30
  5476.2 130.6 reduce-scatter.36
  5609.1 129.8 reduce-scatter.40
  5741.2 131.6 reduce-scatter.34
  5874.9 131.8 reduce-scatter.38
  6009.0 131.8 reduce-scatter.32
  6143.8 144.4 reduce-scatter.24
  6291.1 184.4 reduce-scatter.22
  6478.5 183.4 reduce-scatter.26
  6664.8 183.4 reduce-scatter.28
where the time goes:
time: 6920 us; the launch traced here: 6860 us
  local copies, waits for them, and re-layouts  2920 us (42%)
  waiting for transfers between devices  2510 us (36%)
  other arithmetic  1180 us (17%)
  matrix products  131 us (2%)
    pad x388, local copies, waits for them, and re-layouts, recurrence(): lax.associative_scan(linear_chain, (retain, inject), axis=projected.ndim...  1330 us
    ppermute x12, waiting for transfers between devices, shifted(): return lax.ppermute(x, axis, pairs)  1270 us
    slice x544, local copies, waits for them, and re-layouts, recurrence(): lax.associative_scan(linear_chain, (retain, inject), axis=projected.ndim...  1240 us
    unnamed x16, waiting for transfers between devices  526 us
    reduce_scatter x1, waiting for transfers between devices, reduce_everything(): lax.psum_scatter(mix_final[1], ('dp', 'section'), scatter_dimension=1, ti...  187 us
    reduce_scatter x1, waiting for transfers between devices, reduce_everything(): lax.psum_scatter(mlp_final[1], ('dp', 'section'), scatter_dimension=1, ti...  186 us
    reduce_scatter x1, waiting for transfers between devices, reduce_everything(): lax.psum_scatter(mlp_final[3], ('dp', 'section'), scatter_dimension=2, ti...  186 us
    add x104, other arithmetic, linear_chain(): return (earlier[0] * latter[0], latter[0] * earlier[1] + latter[1])  182 us
  transfers between devices with their start and end apart: 23, of which 21 were waited for; matrix products, arithmetic and copies ran while one was open for 4% of the time, Pallas kernels for 0%

commit v1 on v0

v1 whole, which is shorter than its diff:
```python
import functools

import jax
import jax.numpy as jnp
from jax import lax
from jax.experimental import pallas as pl
from jax.experimental.pallas import tpu as pltpu
from jax.sharding import PartitionSpec as P

EPSILON = 1e-06
LANES = 128
GROUP = 8
TILE_C = 256
TILE_F = 512
BIG = 256
F32 = jnp.float32
BF16 = jnp.bfloat16
ROOT_2_PI = 0.7978845608028654
CUBIC = 0.044715


def dot_nn(left, right):
    return jnp.dot(left, right, preferred_element_type=F32)


def dot_nt(left, right):
    return lax.dot_general(left, right, (((1,), (1,)), ((), ())), preferred_element_type=F32)


def rows_loop(total, step, fn):
    def at(index, carry):
        fn(pl.ds(pl.multiple_of(index * step, step), step))
        return carry

    lax.fori_loop(0, total // step, at, 0)


def to_chunks(natural, target):
    stride = natural.shape[1] // GROUP

    def at(index, carry):
        for tile in range(natural.shape[0]):
            first = natural[tile, pl.ds(2 * index, GROUP, stride=stride), :]
            second = natural[tile, pl.ds(2 * index + 1, GROUP, stride=stride), :]
            both = jnp.concatenate([first, second], axis=0).astype(BF16)
            target[pl.ds(pl.multiple_of(index * 16, 16), 16), pl.ds(tile * LANES, LANES)] = both
        return carry

    lax.fori_loop(0, stride // 2, at, 0)


def to_tokens(chunked, natural):
    stride = natural.shape[1] // GROUP

    def at(index, carry):
        for tile in range(natural.shape[0]):
            rows = pl.ds(pl.multiple_of(index * GROUP, GROUP), GROUP)
            natural[tile, pl.ds(index, GROUP, stride=stride), :] = chunked[rows, pl.ds(tile * LANES, LANES)]
        return carry

    lax.fori_loop(0, stride, at, 0)


def transpose_into(source, target):
    def at(index, carry):
        rows = pl.ds(pl.multiple_of(index * LANES, LANES), LANES)
        target[:, rows] = source[rows, :].astype(F32).T.astype(BF16)
        return carry

    lax.fori_loop(0, source.shape[0] // LANES, at, 0)


def inverse_rms(values):
    return lax.rsqrt(jnp.mean(values * values, axis=-1, keepdims=True) + EPSILON)


def put_tiles(natural, rows, values):
    for tile in range(natural.shape[0]):
        natural[tile, rows, :] = values[:, tile * LANES : (tile + 1) * LANES]


def get_tiles(natural, rows):
    return jnp.concatenate([natural[tile, rows, :] for tile in range(natural.shape[0])], axis=1)


def norm_into(x_ref, gain_ref, target):
    def at(rows):
        source = x_ref[rows, :].astype(F32)
        result = source * inverse_rms(source) * gain_ref[...]
        if len(target.shape) == 3:
            put_tiles(target, rows, result)
        else:
            target[rows, :] = result.astype(target.dtype)

    rows_loop(x_ref.shape[0], 128, at)


def previous_chunk(values, first_row):
    rolled = pltpu.roll(values, 1, 0)
    position = lax.broadcasted_iota(jnp.int32, values.shape, 0)
    return jnp.where(position == 0, first_row, rolled)


def following_chunk(values):
    rolled = pltpu.roll(values, GROUP - 1, 0)
    position = lax.broadcasted_iota(jnp.int32, values.shape, 0)
    return jnp.where(position == GROUP - 1, 0.0, rolled)


def sigmoid(values):
    return 0.5 * jnp.tanh(0.5 * values) + 0.5


def repeat_rows(values, rows):
    return jnp.concatenate([values] * (rows // values.shape[0]), axis=0)


STEP = 32
SPLIT = 64
HALO = 24


def mixer_forward_kernel(
    x_ref, gain_ref, wg_ref, wc_ref, kg_ref, kc_ref, bg_ref, bc_ref, wo_ref, mask_ref, init_ref,
    y_ref, p_ref, z_ref, cand_ref, h_ref, final_ref,
    normed, natural, total, proj, local, decay,
):
    step = pl.program_id(0)
    seq = x_ref.shape[0]
    width = wg_ref.shape[1]

    @pl.when(step == 0)
    def _():
        norm_into(x_ref, gain_ref, natural)
        to_chunks(natural, normed)
        total[...] = jnp.zeros_like(total)

    def project(index, carry):
        rows = pl.ds(pl.multiple_of(index * BIG, BIG), BIG)
        out_rows = pl.ds(pl.multiple_of(index * BIG + HALO, GROUP), BIG)
        block = normed[rows, :]
        for side, weight in enumerate((wg_ref, wc_ref)):
            lanes = pl.ds(side * width, width)
            piece = dot_nn(block, weight[...])
            proj[out_rows, lanes] = piece
            p_ref[0, rows, lanes] = piece.astype(BF16)
        return carry

    lax.fori_loop(0, seq // BIG, project, 0)
    for offset in range(3):
        last = proj[pl.ds(seq + GROUP * offset, GROUP), :]
        proj[pl.ds(GROUP * offset, GROUP), :] = previous_chunk(last, 0.0)

    def scan_step(index, carry):
        base = pl.multiple_of(index * STEP, STEP)
        rows = pl.ds(base, STEP)
        masks = [None] + [mask_ref[k, rows, :] for k in range(3)]
        updated = []
        for tile in range(width // LANES):
            lanes = pl.ds(tile * LANES, LANES)

            def convolve(shift, taps, bias):
                value = bias[0:1, lanes]
                for k in range(4):
                    at = pl.ds(pl.multiple_of(base + HALO - GROUP * k, GROUP), STEP)
                    term = proj[at, pl.ds(shift + tile * LANES, LANES)]
                    if k:
                        term = term * masks[k]
                    value = value + taps[k : k + 1, lanes] * term
                return value

            update = sigmoid(convolve(0, kg_ref, bg_ref))
            candidate = convolve(width, kc_ref, bc_ref)
            z_ref[rows, lanes] = update.astype(BF16)
            cand_ref[rows, lanes] = candidate.astype(BF16)
            retain = (1.0 - update) * masks[1]
            inject = update * candidate
            state, product = carry[tile]
            states, products = [], []
            for g in range(STEP // GROUP):
                here = slice(g * GROUP, (g + 1) * GROUP)
                state = retain[here] * state + inject[here]
                product = retain[here] * product
                states.append(state)
                products.append(product)
            local[rows, lanes] = jnp.concatenate(states, axis=0)
            decay[rows, lanes] = jnp.concatenate(products, axis=0)
            updated.append((state, product))
        return tuple(updated)

    zero = jnp.zeros((GROUP, LANES), F32)
    one = jnp.ones((GROUP, LANES), F32)
    ends = lax.fori_loop(0, seq // STEP, scan_step, ((zero, one),) * (width // LANES))
    entries = []
    for tile, (state, product) in enumerate(ends):
        lanes = pl.ds(tile * LANES, LANES)
        current = init_ref[0:1, lanes]
        starts = []
        for g in range(GROUP):
            starts.append(current)
            current = product[g : g + 1] * current + state[g : g + 1]
        final_ref[0:1, lanes] = current
        entries.append(jnp.concatenate(starts, axis=0))
    entry = repeat_rows(jnp.concatenate(entries, axis=1), STEP)

    def fix(index, carry):
        rows = pl.ds(pl.multiple_of(index * STEP, STEP), STEP)
        h_ref[rows, :] = (local[rows, :] + decay[rows, :] * entry).astype(BF16)
        return carry

    lax.fori_loop(0, seq // STEP, fix, 0)

    def output(rows):
        total[rows, :] += dot_nn(h_ref[rows, :], wo_ref[...])

    rows_loop(seq, BIG, output)

    @pl.when(step == pl.num_programs(0) - 1)
    def _():
        to_tokens(total, natural)

        def finish(rows):
            y_ref[rows, :] = (x_ref[rows, :].astype(F32) + get_tiles(natural, rows)).astype(BF16)

        rows_loop(seq, 128, finish)


def norm_backward(x_ref, g_ref, gain_ref, grad_normed, dx_ref, dgain_ref):
    gain = gain_ref[...]

    def at(index, carry):
        rows = pl.ds(pl.multiple_of(index * 64, 64), 64)
        source = x_ref[rows, :].astype(F32)
        upstream = g_ref[rows, :].astype(F32)
        incoming = get_tiles(grad_normed, rows) if len(grad_normed.shape) == 3 else grad_normed[rows, :]
        scale = inverse_rms(source)
        scaled = gain * incoming
        mean = jnp.mean(source * scaled, axis=-1, keepdims=True)
        result = upstream + scale * scaled - source * (scale * scale * scale * mean)
        dx_ref[rows, :] = result.astype(BF16)
        return carry + jnp.sum(incoming * source * scale, axis=0, keepdims=True)

    dgain_ref[...] = lax.fori_loop(0, x_ref.shape[0] // 64, at, jnp.zeros(gain.shape, F32))


def put_halves(keep_ref, send_ref, bit_ref, index, lanes, values):
    low = values[:SPLIT].astype(BF16)
    high = values[SPLIT:].astype(BF16)
    mine = bit_ref[0] == 1
    rows = pl.ds(pl.multiple_of(index * SPLIT, SPLIT), SPLIT)
    keep_ref[0, rows, lanes] = jnp.where(mine, high, low)
    send_ref[0, rows, lanes] = jnp.where(mine, low, high)


def mixer_backward_kernel(
    x_ref, g_ref, gain_ref, wg_ref, wc_ref, kg_ref, kc_ref, wo_ref, mask_ref, init_ref,
    p_ref, z_ref, cand_ref, h_ref, bit_ref,
    dx_ref, keep_ref, send_ref, small_ref, dgain_ref,
    normed_t, upstream, upstream_t, natural, total, local, decay, dconv, dproj,
):
    step = pl.program_id(0)
    seq = x_ref.shape[0]
    width = wg_ref.shape[1]
    tiles = width // LANES

    @pl.when(step == 0)
    def _():
        norm_into(x_ref, gain_ref, natural)
        to_chunks(natural, upstream)
        transpose_into(upstream, normed_t)

        def widen(rows):
            put_tiles(natural, rows, g_ref[rows, :].astype(F32))

        rows_loop(seq, 128, widen)
        to_chunks(natural, upstream)
        transpose_into(upstream, upstream_t)
        total[...] = jnp.zeros_like(total)

    def back_hidden(rows):
        local[rows, :] = dot_nt(upstream[rows, :], wo_ref[...])

    rows_loop(seq, BIG, back_hidden)

    def scan_step(index, carry):
        rows = pl.ds(pl.multiple_of(seq - STEP - index * STEP, STEP), STEP)
        keep = mask_ref[0, rows, :]
        updated = []
        for tile in range(tiles):
            lanes = pl.ds(tile * LANES, LANES)
            retain = (1.0 - z_ref[rows, lanes].astype(F32)) * keep
            grads = local[rows, lanes]
            chain, product = carry[tile]
            chains, products = [], []
            for g in reversed(range(STEP // GROUP)):
                here = slice(g * GROUP, (g + 1) * GROUP)
                value = grads[here] + chain
                chains.append(value)
                products.append(product)
                chain = retain[here] * value
                product = retain[here] * product
            local[rows, lanes] = jnp.concatenate(chains[::-1], axis=0)
            decay[rows, lanes] = jnp.concatenate(products[::-1], axis=0)
            updated.append((chain, product))
        return tuple(updated)

    zero = jnp.zeros((GROUP, LANES), F32)
    one = jnp.ones((GROUP, LANES), F32)
    ends = lax.fori_loop(0, seq // STEP, scan_step, ((zero, one),) * tiles)
    entries = []
    for chain, product in ends:
        current = jnp.zeros((1, LANES), F32)
        starts = [current]
        for g in reversed(range(1, GROUP)):
            current = chain[g : g + 1] + product[g : g + 1] * current
            starts.append(current)
        entries.append(jnp.concatenate(starts[::-1], axis=0))

    last_rows = h_ref[pl.ds(seq - 16, 16), :].astype(F32)[GROUP:]
    before = previous_chunk(last_rows, init_ref[0:1, :])

    def gates(index, carry):
        base = pl.multiple_of(index * STEP, STEP)
        rows = pl.ds(base, STEP)
        keep = mask_ref[0, rows, :]
        updated = []
        for tile in range(tiles):
            lanes = pl.ds(tile * LANES, LANES)
            hidden = h_ref[rows, lanes].astype(F32)
            delayed = jnp.concatenate([carry[tile], hidden[: STEP - GROUP]], axis=0)
            error = local[rows, lanes] + decay[rows, lanes] * repeat_rows(entries[tile], STEP)
            update = z_ref[rows, lanes].astype(F32)
            candidate = cand_ref[rows, lanes].astype(F32)
            slope = error * (candidate - keep * delayed)
            dconv[rows, lanes] = slope * (update * (1.0 - update))
            dconv[rows, pl.ds(width + tile * LANES, LANES)] = update * error
            updated.append(hidden[STEP - GROUP :])
        return tuple(updated)

    starting = tuple(before[:, tile * LANES : (tile + 1) * LANES] for tile in range(tiles))
    lax.fori_loop(0, seq // STEP, gates, starting)
    for offset in range(3):
        first = dconv[pl.ds(GROUP * offset, GROUP), :]
        dconv[pl.ds(seq + GROUP * offset, GROUP), :] = following_chunk(first)

    def fold(values):
        result = values[0:GROUP]
        for g in range(1, STEP // GROUP):
            result = result + values[g * GROUP : (g + 1) * GROUP]
        return result

    for side, taps in enumerate((kg_ref, kc_ref)):

        def spread(index, carry):
            base = pl.multiple_of(index * STEP, STEP)
            rows = pl.ds(base, STEP)
            updated = []
            for tile in range(tiles):
                lanes = pl.ds(side * width + tile * LANES, LANES)
                weights = pl.ds(tile * LANES, LANES)
                projected = p_ref[0, rows, lanes].astype(F32)
                sums = carry[tile]
                fresh = []
                value = None
                for k in range(4):
                    at = pl.ds(pl.multiple_of(base + GROUP * k, GROUP), STEP)
                    moved = dconv[at, lanes]
                    if k == 0:
                        bias_sum = sums[4] + fold(moved)
                    else:
                        moved = moved * mask_ref[k - 1, at, :]
                    fresh.append(sums[k] + fold(moved * projected))
                    term = taps[k : k + 1, weights] * moved
                    value = term if value is None else value + term
                fresh.append(bias_sum)
                dproj[rows, lanes] = value.astype(BF16)
                updated.append(tuple(fresh))
            return tuple(updated)

        sums = lax.fori_loop(0, seq // STEP, spread, ((zero,) * 5,) * tiles)
        for tile in range(tiles):
            lanes = pl.ds(side * width + tile * LANES, LANES)
            for k in range(5):
                small_ref[0, k : k + 1, lanes] = jnp.sum(sums[tile][k], axis=0, keepdims=True)
            small_ref[0, 5:8, lanes] = jnp.zeros((3, LANES), F32)

    def weight_grads(index, carry):
        rows = pl.ds(pl.multiple_of(index * 128, 128), 128)
        put_halves(keep_ref, send_ref, bit_ref, index, pl.ds(0, 2 * width), dot_nn(normed_t[rows, :], dproj[...]))
        put_halves(
            keep_ref, send_ref, bit_ref, index, pl.ds(2 * width, width), dot_nn(upstream_t[rows, :], h_ref[...])
        )
        return carry

    lax.fori_loop(0, normed_t.shape[0] // 128, weight_grads, 0)

    def back_normed(rows):
        total[rows, :] += dot_nt(dproj[rows, pl.ds(0, width)], wg_ref[...]) + dot_nt(
            dproj[rows, pl.ds(width, width)], wc_ref[...]
        )

    rows_loop(seq, BIG, back_normed)

    @pl.when(step == pl.num_programs(0) - 1)
    def _():
        to_tokens(total, natural)
        norm_backward(x_ref, g_ref, gain_ref, natural, dx_ref, dgain_ref)


def mlp_forward_kernel(
    x_ref, gain_ref, wu_ref, bu_ref, wd_ref, bd_ref, y_ref, u_ref, normed, total
):
    step = pl.program_id(0)
    seq = x_ref.shape[0]

    @pl.when(step == 0)
    def _():
        norm_into(x_ref, gain_ref, normed)

        def start(rows):
            total[rows, :] = x_ref[rows, :].astype(F32) + bd_ref[...]

        rows_loop(seq, 128, start)

    def at(rows):
        pre = dot_nn(normed[rows, :], wu_ref[...]) + bu_ref[...]
        u_ref[rows, :] = pre.astype(BF16)
        inner = ROOT_2_PI * (pre + CUBIC * (pre * pre * pre))
        active = (0.5 * pre * (1.0 + jnp.tanh(inner))).astype(BF16)
        total[rows, :] += dot_nn(active, wd_ref[...])

    rows_loop(seq, BIG, at)

    @pl.when(step == pl.num_programs(0) - 1)
    def _():
        def finish(rows):
            y_ref[rows, :] = total[rows, :].astype(BF16)

        rows_loop(seq, 128, finish)


def mlp_backward_kernel(
    x_ref, g_ref, gain_ref, wu_ref, wd_ref, u_ref, bit_ref,
    dx_ref, keep_ref, send_ref, dbu_ref, dbd_ref, dgain_ref,
    normed_t, upstream_t, total, active, dpre,
):
    step = pl.program_id(0)
    seq = x_ref.shape[0]
    width = wu_ref.shape[1]

    @pl.when(step == 0)
    def _():
        norm_into(x_ref, gain_ref, active)
        transpose_into(active, normed_t)
        transpose_into(g_ref, upstream_t)

        def at(index, carry):
            rows = pl.ds(pl.multiple_of(index * 64, 64), 64)
            return carry + jnp.sum(g_ref[rows, :].astype(F32), axis=0, keepdims=True)

        dbd_ref[...] = lax.fori_loop(0, seq // 64, at, jnp.zeros(dbd_ref.shape, F32))
        total[...] = jnp.zeros_like(total)

    def at(index, carry):
        rows = pl.ds(pl.multiple_of(index * BIG, BIG), BIG)
        pre = u_ref[rows, :].astype(F32)
        square = pre * pre
        bent = jnp.tanh(pre * (ROOT_2_PI + (ROOT_2_PI * CUBIC) * square))
        half = 0.5 * pre
        active[rows, :] = (half + half * bent).astype(BF16)
        slope = 0.5 + 0.5 * bent + half * (1.0 - bent * bent) * (
            ROOT_2_PI + (3.0 * ROOT_2_PI * CUBIC) * square
        )
        low = (dot_nt(g_ref[rows, :], wd_ref[...]) * slope).astype(BF16)
        dpre[rows, :] = low
        total[rows, :] += dot_nt(low, wu_ref[...])
        return carry + jnp.sum(low.astype(F32), axis=0, keepdims=True)

    dbu_ref[...] = lax.fori_loop(0, seq // BIG, at, jnp.zeros(dbu_ref.shape, F32))

    def weight_grads(index, carry):
        rows = pl.ds(pl.multiple_of(index * 128, 128), 128)
        put_halves(keep_ref, send_ref, bit_ref, index, pl.ds(0, width), dot_nn(normed_t[rows, :], dpre[...]))
        put_halves(
            keep_ref, send_ref, bit_ref, index, pl.ds(width, width), dot_nn(upstream_t[rows, :], active[...])
        )
        return carry

    lax.fori_loop(0, normed_t.shape[0] // 128, weight_grads, 0)

    @pl.when(step == pl.num_programs(0) - 1)
    def _():
        norm_backward(x_ref, g_ref, gain_ref, total, dx_ref, dgain_ref)


def shape(dims, kind):
    return jax.ShapeDtypeStruct(dims, kind)


PARAMS = pltpu.CompilerParams(
    dimension_semantics=("arbitrary",), vmem_limit_bytes=56 * 1024 * 1024
)


SCALAR = pl.BlockSpec(memory_space=pltpu.SMEM)


def cost(seq, microseconds):
    return pl.CostEstimate(
        flops=int(microseconds * 1.1e9), bytes_accessed=seq * 4096, transcendentals=0
    )


def whole(dims):
    return pl.BlockSpec(dims, lambda i: (0,) * len(dims))


def mixer_specs(layer, width, hidden, tile):
    count = hidden // tile
    return dict(
        gate=pl.BlockSpec((None, width, tile), lambda i: (layer, 0, i)),
        cand=pl.BlockSpec((None, width, tile), lambda i: (layer, 0, count + i)),
        tap_gate=pl.BlockSpec((None, 4, tile), lambda i: (layer, 0, i)),
        tap_cand=pl.BlockSpec((None, 4, tile), lambda i: (layer, 0, count + i)),
        bias_gate=pl.BlockSpec((None, 1, tile), lambda i: (layer, 0, i)),
        bias_cand=pl.BlockSpec((None, 1, tile), lambda i: (layer, 0, count + i)),
        out=pl.BlockSpec((None, tile, width), lambda i: (layer, i, 0)),
        gain=pl.BlockSpec((None, 1, width), lambda i: (layer, 0, 0)),
        init=pl.BlockSpec((None, 1, tile), lambda i: (layer, 0, i)),
    )


def mixer_forward(layer, x, masks, init, gain, weight_in, taps, bias, weight_out):
    seq, width = x.shape
    hidden = init.shape[2]
    tile = TILE_C
    count = hidden // tile
    spec = mixer_specs(layer, width, hidden, tile)
    column = pl.BlockSpec((seq, tile), lambda i: (0, i))
    return pl.pallas_call(
        mixer_forward_kernel,
        grid=(count,),
        in_specs=[
            whole(x.shape), spec["gain"], spec["gate"], spec["cand"], spec["tap_gate"], spec["tap_cand"],
            spec["bias_gate"], spec["bias_cand"], spec["out"], whole(masks.shape), spec["init"],
        ],
        out_specs=[
            whole(x.shape), pl.BlockSpec((1, seq, 2 * tile), lambda i: (i, 0, 0)), column, column, column,
            pl.BlockSpec((1, tile), lambda i: (0, i)),
        ],
        out_shape=[
            shape(x.shape, BF16), shape((count, seq, 2 * tile), BF16), shape((seq, hidden), BF16),
            shape((seq, hidden), BF16), shape((seq, hidden), BF16), shape((1, hidden), F32),
        ],
        scratch_shapes=[
            pltpu.VMEM((seq, width), BF16), pltpu.VMEM((width // LANES, seq, LANES), F32), pltpu.VMEM((seq, width), F32),
            pltpu.VMEM((seq + HALO, 2 * tile), F32), pltpu.VMEM((seq, tile), F32), pltpu.VMEM((seq, tile), F32),
        ],
        compiler_params=PARAMS,
        cost_estimate=cost(seq, 15),
        name="mixer_forward",
    )(x, gain, weight_in, weight_in, taps, taps, bias, bias, weight_out, masks, init)


def mixer_backward(layer, x, g, stash, masks, init, gain, weight_in, taps, weight_out, bit):
    seq, width = x.shape
    hidden = init.shape[2]
    tile = TILE_C
    count = hidden // tile
    spec = mixer_specs(layer, width, hidden, tile)
    column = pl.BlockSpec((seq, tile), lambda i: (0, i))
    return pl.pallas_call(
        mixer_backward_kernel,
        grid=(count,),
        in_specs=[
            whole(x.shape), whole(x.shape), spec["gain"], spec["gate"], spec["cand"], spec["tap_gate"],
            spec["tap_cand"], spec["out"], whole(masks.shape), spec["init"],
            pl.BlockSpec((1, seq, 2 * tile), lambda i: (i, 0, 0)), column, column, column, SCALAR,
        ],
        out_specs=[
            whole(x.shape), pl.BlockSpec((1, width // 2, 3 * tile), lambda i: (i, 0, 0)),
            pl.BlockSpec((1, width // 2, 3 * tile), lambda i: (i, 0, 0)),
            pl.BlockSpec((1, 8, 2 * tile), lambda i: (i, 0, 0)), whole((1, width)),
        ],
        out_shape=[
            shape(x.shape, BF16), shape((count, width // 2, 3 * tile), BF16),
            shape((count, width // 2, 3 * tile), BF16), shape((count, 8, 2 * tile), F32),
            shape((1, width), F32),
        ],
        scratch_shapes=[
            pltpu.VMEM((width, seq), BF16), pltpu.VMEM((seq, width), BF16), pltpu.VMEM((width, seq), BF16),
            pltpu.VMEM((width // LANES, seq, LANES), F32), pltpu.VMEM((seq, width), F32), pltpu.VMEM((seq, tile), F32),
            pltpu.VMEM((seq, tile), F32), pltpu.VMEM((seq + HALO, 2 * tile), F32),
            pltpu.VMEM((seq, 2 * tile), BF16),
        ],
        compiler_params=PARAMS,
        cost_estimate=cost(seq, 30),
        name="mixer_backward",
    )(x, g, gain, weight_in, weight_in, taps, taps, weight_out, masks, init, *stash, bit)


def mlp_forward(layer, x, gain, weight_up, bias_up, weight_down, bias_down):
    seq, width = x.shape
    inner = weight_up.shape[2]
    tile = TILE_F
    return pl.pallas_call(
        mlp_forward_kernel,
        grid=(inner // tile,),
        in_specs=[
            whole(x.shape), pl.BlockSpec((None, 1, width), lambda i: (layer, 0, 0)),
            pl.BlockSpec((None, width, tile), lambda i: (layer, 0, i)),
            pl.BlockSpec((None, 1, tile), lambda i: (layer, 0, i)),
            pl.BlockSpec((None, tile, width), lambda i: (layer, i, 0)),
            pl.BlockSpec((None, 1, width), lambda i: (layer, 0, 0)),
        ],
        out_specs=[whole(x.shape), pl.BlockSpec((seq, tile), lambda i: (0, i))],
        out_shape=[shape(x.shape, BF16), shape((seq, inner), BF16)],
        scratch_shapes=[pltpu.VMEM((seq, width), BF16), pltpu.VMEM((seq, width), F32)],
        compiler_params=PARAMS,
        cost_estimate=cost(seq, 10),
        name="mlp_forward",
    )(x, gain, weight_up, bias_up, weight_down, bias_down)


def mlp_backward(layer, x, g, pre, gain, weight_up, weight_down, bit):
    seq, width = x.shape
    inner = weight_up.shape[2]
    tile = TILE_F
    return pl.pallas_call(
        mlp_backward_kernel,
        grid=(inner // tile,),
        in_specs=[
            whole(x.shape), whole(x.shape), pl.BlockSpec((None, 1, width), lambda i: (layer, 0, 0)),
            pl.BlockSpec((None, width, tile), lambda i: (layer, 0, i)),
            pl.BlockSpec((None, tile, width), lambda i: (layer, i, 0)),
            pl.BlockSpec((seq, tile), lambda i: (0, i)), SCALAR,
        ],
        out_specs=[
            whole(x.shape), pl.BlockSpec((1, width // 2, 2 * tile), lambda i: (i, 0, 0)),
            pl.BlockSpec((1, width // 2, 2 * tile), lambda i: (i, 0, 0)),
            pl.BlockSpec((1, tile), lambda i: (0, i)), whole((1, width)), whole((1, width)),
        ],
        out_shape=[
            shape(x.shape, BF16), shape((inner // tile, width // 2, 2 * tile), BF16),
            shape((inner // tile, width // 2, 2 * tile), BF16), shape((1, inner), F32),
            shape((1, width), F32), shape((1, width), F32),
        ],
        scratch_shapes=[
            pltpu.VMEM((width, seq), BF16), pltpu.VMEM((width, seq), BF16), pltpu.VMEM((seq, width), F32),
            pltpu.VMEM((seq, tile), BF16), pltpu.VMEM((seq, tile), BF16),
        ],
        compiler_params=PARAMS,
        cost_estimate=cost(seq, 20),
        name="mlp_backward",
    )(x, g, gain, weight_up, weight_down, pre, bit)


def chunk_masks(resets):
    seq = resets.shape[0]
    keep = (1 - resets).astype(F32)
    windows = [keep]
    for k in (1, 2):
        windows.append(windows[-1] * jnp.concatenate([jnp.ones((k,), F32), keep[:-k]]))
    stacked = jnp.stack(windows)
    cut = stacked.reshape(3, GROUP, seq // GROUP).transpose(0, 2, 1)
    ahead = jnp.concatenate([cut[:, :4, 1:], jnp.zeros((3, 4, 1), F32)], axis=2)
    rows = jnp.concatenate([cut, ahead], axis=1).reshape(3, seq + 4 * GROUP, 1)
    return jnp.broadcast_to(rows, (3, seq + 4 * GROUP, LANES))


def permute(x, axis, pairs):
    return lax.ppermute(x, axis, pairs)


def assemble_kernel(own0, own1, own2, own3, left1, left2, left3, right1, right2, right3, out, sems):
    section = lax.axis_index("section")
    lefts = (left1, left2, left3)
    rights = (right1, right2, right3)
    for which, own in enumerate((own0, own1, own2, own3)):

        @pl.when(section == which)
        def _():
            pltpu.make_async_copy(own, out.at[which], sems.at[0]).start()

    for k in (1, 2, 3):

        @pl.when(section < 2)
        def _():
            pltpu.make_async_copy(lefts[k - 1], out.at[section ^ k], sems.at[k]).start()

        @pl.when(section >= 2)
        def _():
            pltpu.make_async_copy(rights[k - 1], out.at[section ^ k], sems.at[k]).start()

    for k in range(4):
        pltpu.make_async_copy(own0, out.at[0], sems.at[k]).wait()


def assemble(owns, lefts, rights):
    dims = owns[0].shape
    anywhere = pl.BlockSpec(memory_space=pl.ANY)
    return pl.pallas_call(
        assemble_kernel,
        in_specs=[anywhere] * 10,
        out_specs=pl.BlockSpec(memory_space=pltpu.VMEM),
        out_shape=shape((4,) + dims, owns[0].dtype),
        scratch_shapes=[pltpu.SemaphoreType.DMA((4,))],
        compiler_params=pltpu.CompilerParams(vmem_limit_bytes=32 * 1024 * 1024),
        name="assemble",
    )(*owns, *lefts, *rights)[None]


def after(value, *others):
    return lax.optimization_barrier((value,) + others)


def send_low(first, second, odd):
    one = jnp.where(odd, first, second)
    two = jnp.where(odd, second, first)
    return (
        permute(one, "section", [(0, 1), (1, 0)]),
        permute(two, "section", [(2, 0), (3, 1)]),
        permute(one, "section", [(3, 0), (2, 1)]),
    )


def send_high(third, fourth, odd):
    one = jnp.where(odd, third, fourth)
    two = jnp.where(odd, fourth, third)
    return (
        permute(one, "section", [(2, 3), (3, 2)]),
        permute(two, "section", [(0, 2), (1, 3)]),
        permute(one, "section", [(1, 2), (0, 3)]),
    )


def swap_pairs(size, step):
    return [(i, i ^ step) for i in range(size)]


def halve(addends, dim, axis, size, step):
    bit = (lax.axis_index(axis) // step) % 2

    def part(which):
        pieces = [
            lax.dynamic_index_in_dim(a, which, dim, keepdims=False).astype(F32) for a in addends
        ]
        return functools.reduce(jnp.add, pieces).astype(addends[0].dtype)

    got = permute(part(1 - bit), axis, swap_pairs(size, step))
    return [part(bit), got]


def bits_of(size):
    return [1 << k for k in range(size.bit_length() - 1)]


def first_step(dp, width):
    return SPLIT // (width // dp)


def sum_rows(keep, send, dp, sections, width, reverse=False):
    split = first_step(dp, width)
    got = permute(send, "dp", swap_pairs(dp, split))
    rest = [step for step in bits_of(dp) if step != split]
    share = width // (dp * sections)
    tiles, _, count = keep.shape
    names = [("dp", dp, step) for step in rest[::-1]]
    names += [("section", sections, step) for step in bits_of(sections)[::-1]]
    dims = (tiles,) + (2,) * len(names) + (share, count)
    addends = [keep.reshape(dims), got.reshape(dims)]
    order = [("dp", dp, step) for step in (rest[::-1] if reverse else rest)]
    order += [("section", sections, step) for step in bits_of(sections)]
    left = list(names)
    for item in order:
        addends = halve(addends, 1 + left.index(item), *item)
        left.remove(item)
    return addends[0].astype(F32) + addends[1].astype(F32)


def sum_small(packed, dp, sections):
    names = [("dp", dp, step) for step in bits_of(dp)[::-1]]
    names += [("section", sections, step) for step in bits_of(sections)[::-1]]
    addends = [packed.reshape((2,) * len(names) + packed.shape[1:])]
    order = [("dp", dp, step) for step in bits_of(dp)]
    order += [("section", sections, step) for step in bits_of(sections)]
    left = list(names)
    for item in order:
        addends = halve(addends, left.index(item), *item)
        left.remove(item)
    return addends[0] + addends[1]


def body(
    tokens, resets, init_states, cotangent, mix_gain, mix_in, conv_weight, conv_bias, mix_out,
    mlp_gain, mlp_up, up_bias, mlp_down, down_bias,
):
    dp = lax.axis_size("dp")
    sections = lax.axis_size("section")
    section = lax.axis_index("section")
    width = tokens.shape[2]
    odd = section % 2 == 1
    bit = ((lax.axis_index("dp") // first_step(dp, width)) % 2).astype(jnp.int32).reshape(1)

    def own(values, axis):
        return lax.dynamic_index_in_dim(values, section, axis, keepdims=False)

    x0 = own(tokens, 0)
    g4 = own(cotangent, 0)
    masks = chunk_masks(own(resets, 0))
    init = own(init_states, 1)[:, None, :]
    mix_gain = mix_gain[:, None, :]
    mlp_gain = mlp_gain[:, None, :]
    conv_bias = conv_bias[:, None, :]
    up_bias = up_bias[:, None, :]
    down_bias = down_bias[:, None, :]

    def mixer(layer, x):
        y, *stash, final = mixer_forward(
            layer, x, masks, init, mix_gain, mix_in, conv_weight, conv_bias, mix_out
        )
        return y, stash, final

    def mlp(layer, x):
        return mlp_forward(layer, x, mlp_gain, mlp_up, up_bias, mlp_down, down_bias)

    x1, stash0, final0 = mixer(0, x0)
    x2, pre0 = mlp(0, x1)
    act_low = send_low(x1, x2, odd)
    x3, stash1, final1 = mixer(1, x2)
    x4, pre1 = mlp(1, x3)
    act_high = send_high(x3, x4, odd)
    final = jnp.concatenate([final0, final1], axis=0)[:, None, :]
    final_states = lax.all_to_all(final, "section", split_axis=2, concat_axis=1, tiled=True)

    g3, up1_keep, up1_send, dbu1, dbd1, dgain_mlp1 = mlp_backward(
        1, x3, g4, pre1, mlp_gain, mlp_up, mlp_down, bit
    )
    mlp1 = sum_rows(up1_keep, up1_send, dp, sections, width)
    act_low = list(act_low)
    g3, act_low[0], act_low[1] = after(g3, act_low[0], act_low[1])
    g2, in1_keep, in1_send, small1, dgain_mix1 = mixer_backward(
        1, x2, g3, stash1, masks, init, mix_gain, mix_in, conv_weight, mix_out, bit
    )
    g2, act_low[2] = after(g2, act_low[2])
    dx_high = send_high(g2, g3, odd)
    mix1 = sum_rows(in1_keep, in1_send, dp, sections, width)
    g1, up0_keep, up0_send, dbu0, dbd0, dgain_mlp0 = mlp_backward(
        0, x1, g2, pre0, mlp_gain, mlp_up, mlp_down, bit
    )
    act_high = list(act_high)
    g1, act_high[0], act_high[1], act_high[2] = after(g1, *act_high)
    mlp0 = sum_rows(up0_keep, up0_send, dp, sections, width)
    g0, in0_keep, in0_send, small0, dgain_mix0 = mixer_backward(
        0, x0, g1, stash0, masks, init, mix_gain, mix_in, conv_weight, mix_out, bit
    )
    dx_high = list(dx_high)
    g0, dx_high[0], dx_high[1], mlp1 = after(g0, dx_high[0], dx_high[1], mlp1)
    dx_low = send_low(g0, g1, odd)
    half = in0_keep.shape[0] // 2
    mix0 = jnp.concatenate(
        [
            sum_rows(in0_keep[:half], in0_send[:half], dp, sections, width),
            sum_rows(in0_keep[half:], in0_send[half:], dp, sections, width, True),
        ]
    )
    activations = assemble((x1, x2, x3, x4), act_low, act_high)
    input_grads = assemble((g0, g1, g2, g3), dx_low, dx_high)

    devices = dp * sections
    mix_small = jnp.stack([small0, small1])
    count, tile = mix_small.shape[1], mix_small.shape[3] // 2
    mix_small = mix_small.reshape(2, count, 8, 2, tile).transpose(0, 2, 3, 1, 4).reshape(2, 8, -1)
    lines = [
        jnp.stack([dgain_mix0[0], dgain_mix1[0]]),
        jnp.stack([dgain_mlp0[0], dgain_mlp1[0]]),
        jnp.stack([dbd0[0], dbd1[0]]),
        jnp.stack([dbu0[0], dbu1[0]]),
        mix_small[:, :5].reshape(10, -1),
    ]
    packed = jnp.concatenate(
        [a.reshape(a.shape[0], devices, -1).transpose(1, 0, 2).reshape(devices, -1) for a in lines],
        axis=1,
    )
    summed = sum_small(packed, dp, sections)
    pieces, at = [], 0
    for a in lines:
        size = a.size // devices
        pieces.append(summed[at : at + size].reshape(a.shape[0], -1))
        at += size
    mix_gain_grad, mlp_gain_grad, down_bias_grad, up_bias_grad, conv = pieces
    conv = conv.reshape(2, 5, -1)

    mix_big = jnp.stack([mix0, mix1])
    mlp_big = jnp.stack([mlp0, mlp1])
    share = mix_big.shape[2]
    mix_in_grad = (
        mix_big[..., : 2 * tile].reshape(2, count, share, 2, tile).transpose(0, 2, 3, 1, 4)
        .reshape(2, share, -1)
    )
    mix_out_grad = mix_big[..., 2 * tile :].transpose(0, 1, 3, 2).reshape(2, -1, share)
    wide = mlp_big.shape[3] // 2
    mlp_up_grad = mlp_big[..., :wide].transpose(0, 2, 1, 3).reshape(2, share, -1)
    mlp_down_grad = mlp_big[..., wide:].transpose(0, 1, 3, 2).reshape(2, -1, share)
    return (
        activations, input_grads, final_states, mix_gain_grad, mix_in_grad, conv[:, :4], conv[:, 4],
        mix_out_grad, mlp_gain_grad, mlp_up_grad, up_bias_grad, mlp_down_grad, down_bias_grad,
    )


def solution(mesh):
    both = ("dp", "section")
    return jax.shard_map(
        body,
        mesh=mesh,
        in_specs=(
            P("dp", None, None), P("dp", None), P(None, "dp", None), P("dp", None, None),
            P(), P(), P(), P(), P(), P(), P(), P(), P(), P(),
        ),
        out_specs=(
            P("section", "dp", None, None), P("section", "dp", None, None), P(None, "dp", "section"),
            P(None, both), P(None, both, None), P(None, None, both), P(None, both), P(None, None, both),
            P(None, both), P(None, both, None), P(None, both), P(None, None, both), P(None, both),
        ),
        check_vma=False,
    )
```

time: 6920 us -> 622 us (0.09)
  local copies, waits for them, and re-layouts: 2920 us -> 51.4 us
  waiting for transfers between devices: 2510 us -> 139 us
  other arithmetic: 1180 us -> 27 us
  Pallas kernels: 0 us -> 233 us
  matrix products: 131 us -> 0 us
  starting transfers between devices: 40.7 us -> 169 us
    pad x388 -> x0, local copies, waits for them, and re-layouts: 1330 us -> none  [recurrence(): lax.associative_scan(linear_chain, (retain, inject), axis=projected.ndim...]
    slice x561 -> x11, local copies, waits for them, and re-layouts: 1280 us -> 5.61 us  [the longest x6 2.14 us: body(): pieces.append(summed[at:at + size].reshape(a.shape[0], -1))]
    ppermute x12 -> x42, waiting for transfers between devices: 1270 us -> 136 us  [permute(): return lax.ppermute(x, axis, pairs)]
    reduce_scatter x4 -> x0, waiting for transfers between devices: 706 us -> none  [the longest x1 187 us: reduce_everything(): lax.psum_scatter(mix_final[1], ('dp', 'section'), scatter_dimension=1, ti...]
    unnamed x16 -> x0, waiting for transfers between devices: 526 us -> none
    mul x122 -> x1, other arithmetic: 376 us -> 0.8 us  [chunk_masks(): windows[-1] * jnp.concatenate([jnp.ones((k,), F32), keep[:-k]])]
    add x198 -> x8, other arithmetic: 351 us -> 0.94 us  [the longest x3 0.83 us: sum_rows(): return addends[0].astype(F32) + addends[1].astype(F32)]
    pallas_call x0 -> x10, Pallas kernels: none -> 233 us  [the longest x2 87.9 us: mixer_backward(): pl.pallas_call(mixer_backward_kernel, grid=(count,), in_specs=[whole(x.sh...]
  transfers between devices with their start and end apart: 23 -> 43, of which waited for: 21 -> 16; matrix products, arithmetic and copies ran while one was open for 4% -> 10% of each run, Pallas kernels for 0% -> 31%
where the time goes in v1:
time: 622 us; the launch traced here: 620 us
  Pallas kernels  233 us (37%)
  starting transfers between devices  169 us (27%)
  waiting for transfers between devices  139 us (22%)
  local copies, waits for them, and re-layouts  51.4 us (8%)
  other arithmetic  27 us (4%)
    ppermute x42, starting transfers between devices, permute(): return lax.ppermute(x, axis, pairs)  162 us
    ppermute x42, waiting for transfers between devices, permute(): return lax.ppermute(x, axis, pairs)  136 us
    pallas_call x2, Pallas kernels, mixer_backward(): pl.pallas_call(mixer_backward_kernel, grid=(count,), in_specs=[whole(x.sh...  87.9 us
    pallas_call x2, Pallas kernels, mlp_backward(): pl.pallas_call(mlp_backward_kernel, grid=(inner // tile,), in_specs=[whol...  58.6 us
    pallas_call x2, Pallas kernels, mixer_forward(): pl.pallas_call(mixer_forward_kernel, grid=(count,), in_specs=[whole(x.sha...  50.9 us
    pallas_call x2, Pallas kernels, mlp_forward(): pl.pallas_call(mlp_forward_kernel, grid=(inner // tile,), in_specs=[whole...  27.8 us
  transfers between devices with their start and end apart: 43, of which 16 were waited for; matrix products, arithmetic and copies ran while one was open for 10% of the time, Pallas kernels for 31%

profile of v1, /device:TPU:0, one launch (start us, length us, event | category | flops | bytes accessed | tf_op | source)
XLA Modules:
  0.0 620.2 jit_solution(13939552219175944546)
XLA Ops:
  9.7 3.0 dynamic-slice_bitcast_fusion
  12.7 1.7 broadcast_in_dim.35.mask_ref
  14.4 25.4 %mixer_forward.2 = (bf16[1024,512]{1,0:T(8,128)(2,1)}, bf16[4,1024,512]{2,1,0:T(8,128)(2,1)}, bf16[1024,1024]{1,0:T(8,128)(2,1)}, bf16[1024,1024]{1,0:T(8,128)(2...) custom-call(bf16[1024,512]{1,0:T(8,128)(2,1)} %get-tuple-element.178.x_ref, f32[2,1,512]{2,1,0:T(1,128)} %broadcast_in_dim.32.gain_ref, ...), custom_call_target="tpu_custom_call" | custom-call | flops 16499999744 | bytes 4194304 | tf_op jit(solution)/shard_map/mixer_forward/pallas_call | solution.py:540
  39.8 13.9 %mlp_forward.2 = (bf16[1024,512]{1,0:T(8,128)(2,1)}, bf16[1024,2048]{1,0:T(8,128)(2,1)}) custom-call(bf16[1024,512]{1,0:T(8,128)(2,1)} %get-tuple-element.64.x_ref.own0, f32[2,1,512]{2,1,0:T(1,128)} %broadcast_in_dim.36.gain_ref, bf16[2,512,2048]{2,1,0:T(8,128)(2,1)} %wu_ref.7, f32[2,1,2048]{2,1,0:T(1,128)} %broadcast_in_dim.37.bu_ref, ...), custom_call_target="tpu_custom_call" | custom-call | flops 11000000512 | bytes 4194304 | tf_op jit(solution)/shard_map/mlp_forward/pallas_call | solution.py:606
  53.6 2.8 broadcast_select_fusion.6
  56.4 4.9 collective-permute-start
  62.6 25.5 %mixer_forward.3 = (bf16[1024,512]{1,0:T(8,128)(2,1)}, bf16[4,1024,512]{2,1,0:T(8,128)(2,1)}, bf16[1024,1024]{1,0:T(8,128)(2,1)}, bf16[1024,1024]{1,0:T(8,128)(2...) custom-call(bf16[1024,512]{1,0:T(8,128)(2,1)} %get-tuple-element.65.x_ref.own1, ...), custom_call_target="tpu_custom_call" | custom-call | flops 16499999744 | bytes 4194304 | tf_op jit(solution)/shard_map/mixer_forward/pallas_call | solution.py:540
  88.1 13.9 %mlp_forward.3 = (bf16[1024,512]{1,0:T(8,128)(2,1)}, bf16[1024,2048]{1,0:T(8,128)(2,1)}) custom-call(bf16[1024,512]{1,0:T(8,128)(2,1)} %get-tuple-element.66.x_ref.own2, f32[2,1,512]{2,1,0:T(1,128)} %broadcast_in_dim.36.gain_ref, bf16[2,512,2048]{2,1,0:T(8,128)(2,1)} %wu_ref.7, f32[2,1,2048]{2,1,0:T(1,128)} %broadcast_in_dim.37.bu_ref, ...), custom_call_target="tpu_custom_call" | custom-call | flops 11000000512 | bytes 4194304 | tf_op jit(solution)/shard_map/mlp_forward/pallas_call | solution.py:606
  102.0 2.8 broadcast_select_fusion.4
  105.5 8.6 %collective-permute-start.5 = (bf16[1024,512]{1,0:T(8,128)(2,1)}, bf16[1024,512]{1,0:T(8,128)(2,1)}, u32[]{:S(2)}, u32[]{:S(2)}) collective-permute-start(bf16[1024,512]{1,0:T(8,128)(2,1)} %get-tuple-element.141), channel_id=1, source_target_pairs={{1,2},{0,3},{5,6},{4,7},{9,10},{8,11},{13,14},{12,15},{17,18},{16,... | collective-permute-start | bytes 3145736 | tf_op jit(solution)/shard_map/ppermute | solution.py:672
  117.0 3.8 reduce.4
  120.8 2.0 reshape.491
  122.7 6.3 %all-to-all-start = ((f32[4,1,512]{2,1,0:T(1,128)}), f32[4,1,512]{2,1,0:T(1,128)S(1)}, u32[]{:S(2)}, u32[]{:S(2)}) async-start(f32[4,1,512]{2,1,0:T(1,128)} %reshape.491), calls=%async_computation | async-start | bytes 16384 | tf_op jit(solution)/shard_map/all_to_all | solution.py:834
  129.0 29.1 %mlp_backward.2 = (bf16[1024,512]{1,0:T(8,128)(2,1)}, bf16[4,256,1024]{2,1,0:T(8,128)(2,1)}, bf16[4,256,1024]{2,1,0:T(8,128)(2,1)}, f32[1,2048]{1,0:T(1,128)}, f32[1,512]{1,0:T(1,128)}, /*index=5*/f32[1,512]{1,0:T(1,128)}) custom-call(bf16[1024,512]{1,0:T(8,128)(2,1)} %get-tuple-element.66.x_ref.own2, bf16[1024,512]{1,0:T(8,128)(2,1)} %get-tuple-element.177.g_ref, ...), custom_call_target="tpu_custom_call" | custom-call | flops 22000001024 | bytes 4194304 | tf_op jit(solution)/shard_map/mlp_backward/pallas_call | solution.py:629
  158.2 3.2 constant_dynamic-slice_fusion.31
  161.4 2.5 all-to-all-done
  164.6 1.7 reshape.492
  166.3 1.8 copy.206
  168.1 2.6 collective-permute-start.4
  170.8 43.9 %mixer_backward.2 = (bf16[1024,512]{1,0:T(8,128)(2,1)}, bf16[4,256,768]{2,1,0:T(8,128)(2,1)}, bf16[4,256,768]{2,1,0:T(8,128)(2,1)}, f32[4,8,512]{2,1,0:T(8,128)}, f32[1,512]{1,0:T(1,128)}) custom-call(bf16[1024,512]{1,0:T(8,128)(2,1)} %get-tuple-element.65.x_ref.own1, bf16[1024,512]{1,0:T(8,128)(2,1)} %get-tuple-element.72.g_ref.own3, ...), custom_call_target="tpu_custom_call" | custom-call | flops 32999999488 | bytes 4194304 | tf_op jit(solution)/shard_map/mixer_backward/pallas_call | solution.py:572
  214.6 29.5 %mlp_backward.3 = (bf16[1024,512]{1,0:T(8,128)(2,1)}, bf16[4,256,1024]{2,1,0:T(8,128)(2,1)}, bf16[4,256,1024]{2,1,0:T(8,128)(2,1)}, f32[1,2048]{1,0:T(1,128)}, f32[1,512]{1,0:T(1,128)}, /*index=5*/f32[1,512]{1,0:T(1,128)}) custom-call(bf16[1024,512]{1,0:T(8,128)(2,1)} %get-tuple-element.64.x_ref.own0, bf16[1024,512]{1,0:T(8,128)(2,1)} %get-tuple-element.79.g_ref.own2, ...), custom_call_target="tpu_custom_call" | custom-call | flops 22000001024 | bytes 4194304 | tf_op jit(solution)/shard_map/mlp_backward/pallas_call | solution.py:629
  244.3 44.1 %mixer_backward.3 = (bf16[1024,512]{1,0:T(8,128)(2,1)}, bf16[4,256,768]{2,1,0:T(8,128)(2,1)}, bf16[4,256,768]{2,1,0:T(8,128)(2,1)}, f32[4,8,512]{2,1,0:T(8,128)}, f32[1,512]{1,0:T(1,128)}) custom-call(bf16[1024,512]{1,0:T(8,128)(2,1)} %get-tuple-element.178.x_ref, bf16[1024,512]{1,0:T(8,128)(2,1)} %get-tuple-element.85.g_ref.own1, ...), custom_call_target="tpu_custom_call" | custom-call | flops 32999999488 | bytes 4194304 | tf_op jit(solution)/shard_map/mixer_backward/pallas_call | solution.py:572
  296.8 1.8 collective-permute-start.6
  310.2 13.6 %collective-permute-start.21 = (f32[864]{0:T(1024)S(1)}, f32[864]{0:T(1024)S(1)}, u32[]{:S(2)}, u32[]{:S(2)}) collective-permute-start(f32[864]{0:T(1024)S(1)} %get-tuple-element.128), channel_id=1, source_target_pairs={{0,2},{1,3},{2,0},{3,1},{4,6},{5,7},{6,4},{7,5},{8,10},{9,11},{10,... | collective-permute-start | bytes 10376 | tf_op jit(solution)/shard_map/ppermute | solution.py:672
  324.8 3.5 assemble.2
  340.0 1.8 constant_dynamic-slice_fusion.30
  343.5 3.0 collective-permute-done.28
  348.1 2.2 collective-permute-done.23
  351.9 24.1 %collective-permute-done.29 = bf16[2,2,2,16,768]{4,3,2,1,0:T(8,128)(2,1)S(1)} collective-permute-done((bf16[2,2,2,16,768]{4,3,2,1,0:T(8,128)(2,1)S(1)}, bf16[2,2,2,16,768]{4,3,2,1,0:T(8,128)(2,1)S(1)}, u32[]{:S(2)}, u32[]{:S(2)}) %collective-permute-start.29) | collective-permute-done | bytes 196640 | tf_op jit(solution)/shard_map/ppermute | solution.py:672
  376.6 5.3 collective-permute-done.24
  383.4 3.5 collective-permute-done.30
  394.0 3.0 collective-permute-start.7
  399.5 9.7 %collective-permute-done.33 = bf16[4,2,2,2,16,768]{5,4,0,2,3,1:T(8,128)(2,1)S(1)} collective-permute-done((bf16[4,2,2,2,16,768]{5,4,0,2,3,1:T(8,128)(2,1)S(1)}, bf16[4,2,2,2,16,768]{5,4,0,2,3,1:T(8,128)(2,1)S(1)}, u32[]{:S(2)}, u32[]{:S(2)}) %collective-permute-start.33) | collective-permute-done | bytes 786464 | tf_op jit(solution)/shard_map/ppermute | solution.py:672
  410.9 5.3 collective-permute-done.26
  416.5 24.1 %collective-permute-start.11 = (bf16[4,2,16,1024]{3,2,0,1:T(8,128)(2,1)S(1)}, bf16[4,2,16,1024]{3,2,0,1:T(8,128)(2,1)S(1)}, u32[]{:S(2)}, u32[]{:S(2)}) collective-permute-start(bf16[4,2,16,1024]{3,2,0,1:T(8,128)(2,1)S(1)} %get-tuple-element.155), channel_id=1, source_target_pairs={{0,1},{1,0},{2,3},{3,2},{4,5},{5,4},{6,7},{7,6},{8,9},{9,8},{10,11... | collective-permute-start | bytes 786440 | tf_op jit(solution)/shard_map/ppermute | solution.py:672
  440.8 9.8 %collective-permute-start.35 = (bf16[4,2,16,768]{3,2,0,1:T(8,128)(2,1)S(1)}, bf16[4,2,16,768]{3,2,0,1:T(8,128)(2,1)S(1)}, u32[]{:S(2)}, u32[]{:S(2)}) collective-permute-start(bf16[4,2,16,768]{3,2,0,1:T(8,128)(2,1)S(1)} %get-tuple-element.157), channel_id=1, source_target_pairs={{0,1},{1,0},{2,3},{3,2},{4,5},{5,4},{6,7},{7,6},{8,9},{9,8},{10,11... | collective-permute-start | bytes 589832 | tf_op jit(solution)/shard_map/ppermute | solution.py:672
  451.1 5.9 collective-permute-start.16
  457.0 19.9 %collective-permute-start.12 = (bf16[4,16,1024]{2,1,0:T(8,128)(2,1)S(1)}, bf16[4,16,1024]{2,1,0:T(8,128)(2,1)S(1)}, u32[]{:S(2)}, u32[]{:S(2)}) collective-permute-start(bf16[4,16,1024]{2,1,0:T(8,128)(2,1)S(1)} %fusion.46), channel_id=1, source_target_pairs={{0,2},{1,3},{2,0},{3,1},{4,6},{5,7},{6,4},{7,5},{8,10},{9,11},{10,... | collective-permute-start | bytes 393224 | tf_op jit(solution)/shard_map/ppermute | solution.py:672
  477.2 3.5 collective-permute-done.12
  484.6 29.8 %collective-permute-start.13 = (bf16[1024,512]{1,0:T(8,128)(2,1)}, bf16[1024,512]{1,0:T(8,128)(2,1)}, u32[]{:S(2)}, u32[]{:S(2)}) collective-permute-start(bf16[1024,512]{1,0:T(8,128)(2,1)} %get-tuple-element.131), channel_id=1, source_target_pairs={{0,1},{1,0},{4,5},{5,4},{8,9},{9,8},{12,13},{13,12},{16,17},{17,16... | collective-permute-start | bytes 3145736 | tf_op jit(solution)/shard_map/ppermute | solution.py:672
  517.3 5.1 collective-permute-start.40
  522.6 41.7 %collective-permute-done.40 = bf16[4,2,16,1024]{3,2,1,0:T(8,128)(2,1)S(1)} collective-permute-done((bf16[4,2,16,1024]{3,2,1,0:T(8,128)(2,1)S(1)}, bf16[4,2,16,1024]{3,2,1,0:T(8,128)(2,1)S(1)}, u32[]{:S(2)}, u32[]{:S(2)}) %collective-permute-start.40) | collective-permute-done | bytes 262176 | tf_op jit(solution)/shard_map/ppermute | solution.py:672
  565.0 7.2 %collective-permute-start.41 = (bf16[4,16,1024]{2,1,0:T(8,128)(2,1)S(1)}, bf16[4,16,1024]{2,1,0:T(8,128)(2,1)}, u32[]{:S(2)}, u32[]{:S(2)}) collective-permute-start(bf16[4,16,1024]{2,1,0:T(8,128)(2,1)S(1)} %fusion.48), channel_id=1, source_target_pairs={{0,2},{1,3},{2,0},{3,1},{4,6},{5,7},{6,4},{7,5},{8,10},{9,11},{10,... | collective-permute-start | bytes 393224 | tf_op jit(solution)/shard_map/ppermute | solution.py:672
  572.9 1.8 reshape.446
  574.7 1.8 copy.276
  576.5 1.8 reshape.447
  580.0 32.4 %collective-permute-done.41 = bf16[4,16,1024]{2,1,0:T(8,128)(2,1)} collective-permute-done((bf16[4,16,1024]{2,1,0:T(8,128)(2,1)S(1)}, bf16[4,16,1024]{2,1,0:T(8,128)(2,1)}, u32[]{:S(2)}, u32[]{:S(2)}) %collective-permute-start.41) | collective-permute-done | bytes 131104 | tf_op jit(solution)/shard_map/ppermute | solution.py:672
  616.0 4.0 assemble.3
  (262 shorter events, 79.9 us)
Async XLA Ops:
  56.4 111.7 %collective-permute-start = (bf16[1024,512]{1,0:T(8,128)(2,1)}, bf16[1024,512]{1,0:T(8,128)(2,1)S(1)}, u32[]{:S(2)}, u32[]{:S(2)}) collective-permute-start(bf16[1024,512]{1,0:T(8,128)(2,1)} %get-tuple-element.143), channel_id=1, source_target_pairs={{0,1},{1,0},{4,5},{5,4},{8,9},{9,8},{12,13},{13,12},{16,17},{17,16... | collective-permute-start | bytes 3145736 | tf_op jit(solution)/shard_map/ppermute | solution.py:672
  61.3 153.3 %collective-permute-start.2 = (bf16[1024,512]{1,0:T(8,128)(2,1)}, bf16[1024,512]{1,0:T(8,128)(2,1)S(1)}, u32[]{:S(2)}, u32[]{:S(2)}) collective-permute-start(bf16[1024,512]{1,0:T(8,128)(2,1)} %get-tuple-element.143), channel_id=1, source_target_pairs={{3,0},{2,1},{7,4},{6,5},{11,8},{10,9},{15,12},{14,13},{19,16},{18,... | collective-permute-start | bytes 3145736 | tf_op jit(solution)/shard_map/ppermute | solution.py:672
  104.8 139.4 %collective-permute-start.3 = (bf16[1024,512]{1,0:T(8,128)(2,1)}, bf16[1024,512]{1,0:T(8,128)(2,1)S(1)}, u32[]{:S(2)}, u32[]{:S(2)}) collective-permute-start(bf16[1024,512]{1,0:T(8,128)(2,1)} %get-tuple-element.141), channel_id=1, source_target_pairs={{2,3},{3,2},{6,7},{7,6},{10,11},{11,10},{14,15},{15,14},{18,19},{1... | collective-permute-start | bytes 3145736 | tf_op jit(solution)/shard_map/ppermute | solution.py:672
  105.5 138.7 %collective-permute-start.5 = (bf16[1024,512]{1,0:T(8,128)(2,1)}, bf16[1024,512]{1,0:T(8,128)(2,1)}, u32[]{:S(2)}, u32[]{:S(2)}) collective-permute-start(bf16[1024,512]{1,0:T(8,128)(2,1)} %get-tuple-element.141), channel_id=1, source_target_pairs={{1,2},{0,3},{5,6},{4,7},{9,10},{8,11},{13,14},{12,15},{17,18},{16,... | collective-permute-start | bytes 3145736 | tf_op jit(solution)/shard_map/ppermute | solution.py:672
  114.1 56.6 %collective-permute-start.1 = (bf16[1024,512]{1,0:T(8,128)(2,1)}, bf16[1024,512]{1,0:T(8,128)(2,1)}, u32[]{:S(2)}, u32[]{:S(2)}) collective-permute-start(bf16[1024,512]{1,0:T(8,128)(2,1)} %get-tuple-element.142), channel_id=1, source_target_pairs={{2,0},{3,1},{6,4},{7,5},{10,8},{11,9},{14,12},{15,13},{18,16},{19,... | collective-permute-start | bytes 3145736 | tf_op jit(solution)/shard_map/ppermute | solution.py:672
  122.7 41.2 %all-to-all-start = ((f32[4,1,512]{2,1,0:T(1,128)}), f32[4,1,512]{2,1,0:T(1,128)S(1)}, u32[]{:S(2)}, u32[]{:S(2)}) async-start(f32[4,1,512]{2,1,0:T(1,128)} %reshape.491), calls=%async_computation | async-start | bytes 16384 | tf_op jit(solution)/shard_map/all_to_all | solution.py:834
  168.1 46.5 %copy-start.13 = (bf16[1024,512]{1,0:T(8,128)(2,1)}, bf16[1024,512]{1,0:T(8,128)(2,1)S(1)}, u32[]{:S(2)}) copy-start(bf16[1024,512]{1,0:T(8,128)(2,1)S(1)} %collective-permute-done.left1) | copy-start | bytes 3145732
  168.1 76.1 %collective-permute-start.4 = (bf16[1024,512]{1,0:T(8,128)(2,1)}, bf16[1024,512]{1,0:T(8,128)(2,1)S(1)}, u32[]{:S(2)}, u32[]{:S(2)}) collective-permute-start(bf16[1024,512]{1,0:T(8,128)(2,1)} %get-tuple-element.140), channel_id=1, source_target_pairs={{0,2},{1,3},{4,6},{5,7},{8,10},{9,11},{12,14},{13,15},{16,18},{17,... | collective-permute-start | bytes 3145736 | tf_op jit(solution)/shard_map/ppermute | solution.py:672
  170.7 167.8 %collective-permute-start.8 = (bf16[4,256,1024]{2,1,0:T(8,128)(2,1)}, bf16[4,256,1024]{2,1,0:T(8,128)(2,1)}, u32[]{:S(2)}, u32[]{:S(2)}) collective-permute-start(bf16[4,256,1024]{2,1,0:T(8,128)(2,1)} %get-tuple-element.92), channel_id=1, source_target_pairs={{0,4},{4,0},{8,12},{12,8},{16,20},{20,16},{24,28},{28,24},{1,5},{5... | collective-permute-start | bytes 6291464 | tf_op jit(solution)/shard_map/ppermute | solution.py:672
  244.3 46.3 %copy-start.36 = (f32[1,2048]{1,0:T(1,128)S(1)}, f32[1,2048]{1,0:T(1,128)}, u32[]{:S(2)}) copy-start(f32[1,2048]{1,0:T(1,128)} %get-tuple-element.105) | copy-start | bytes 24580
  244.3 46.3 %copy-start.37 = (f32[1,2048]{1,0:T(1,128)S(1)}, f32[1,2048]{1,0:T(1,128)}, u32[]{:S(2)}) copy-start(f32[1,2048]{1,0:T(1,128)} %get-tuple-element.104) | copy-start | bytes 24580
  244.3 46.5 %copy-start.35 = (f32[4,8,512]{2,1,0:T(8,128)S(1)}, f32[4,8,512]{2,1,0:T(8,128)}, u32[]{:S(2)}) copy-start(f32[4,8,512]{2,1,0:T(8,128)} %get-tuple-element.107) | copy-start | bytes 196612
  294.8 3.8 collective-permute-start.17
  296.8 185.3 %collective-permute-start.6 = (bf16[1024,512]{1,0:T(8,128)(2,1)}, bf16[1024,512]{1,0:T(8,128)(2,1)}, u32[]{:S(2)}, u32[]{:S(2)}) collective-permute-start(bf16[1024,512]{1,0:T(8,128)(2,1)} %get-tuple-element.139), channel_id=1, source_target_pairs={{2,3},{3,2},{6,7},{7,6},{10,11},{11,10},{14,15},{15,14},{18,19},{1... | collective-permute-start | bytes 3145736 | tf_op jit(solution)/shard_map/ppermute | solution.py:672
  298.6 3.9 collective-permute-start.18
  301.5 30.9 %collective-permute-start.27 = (bf16[2,256,768]{2,1,0:T(8,128)(2,1)}, bf16[2,256,768]{2,1,0:T(8,128)(2,1)}, u32[]{:S(2)}, u32[]{:S(2)}) collective-permute-start(bf16[2,256,768]{2,1,0:T(8,128)(2,1)} %get-tuple-element.153), channel_id=1, source_target_pairs={{0,4},{4,0},{8,12},{12,8},{16,20},{20,16},{24,28},{28,24},{1,5},{5... | collective-permute-start | bytes 2359304 | tf_op jit(solution)/shard_map/ppermute | solution.py:672
  302.6 3.8 collective-permute-start.19
  305.2 30.1 %collective-permute-start.22 = (bf16[2,256,768]{2,1,0:T(8,128)(2,1)}, bf16[2,256,768]{2,1,0:T(8,128)(2,1)}, u32[]{:S(2)}, u32[]{:S(2)}) collective-permute-start(bf16[2,256,768]{2,1,0:T(8,128)(2,1)} %get-tuple-element.152), channel_id=1, source_target_pairs={{0,4},{4,0},{8,12},{12,8},{16,20},{20,16},{24,28},{28,24},{1,5},{5... | collective-permute-start | bytes 2359304 | tf_op jit(solution)/shard_map/ppermute | solution.py:672
  306.4 3.7 collective-permute-start.20
  310.2 18.1 %collective-permute-start.21 = (f32[864]{0:T(1024)S(1)}, f32[864]{0:T(1024)S(1)}, u32[]{:S(2)}, u32[]{:S(2)}) collective-permute-start(f32[864]{0:T(1024)S(1)} %get-tuple-element.128), channel_id=1, source_target_pairs={{0,2},{1,3},{2,0},{3,1},{4,6},{5,7},{6,4},{7,5},{8,10},{9,11},{10,... | collective-permute-start | bytes 10376 | tf_op jit(solution)/shard_map/ppermute | solution.py:672
  328.3 60.1 %collective-permute-start.32 = (bf16[4,256,768]{2,1,0:T(8,128)(2,1)}, bf16[4,256,768]{2,1,0:T(8,128)(2,1)}, u32[]{:S(2)}, u32[]{:S(2)}) collective-permute-start(bf16[4,256,768]{2,1,0:T(8,128)(2,1)} %get-tuple-element.111), channel_id=1, source_target_pairs={{0,4},{4,0},{8,12},{12,8},{16,20},{20,16},{24,28},{28,24},{1,5},{5... | collective-permute-start | bytes 4718600 | tf_op jit(solution)/shard_map/ppermute | solution.py:672
  332.4 66.2 %collective-permute-start.37 = (bf16[4,256,1024]{2,1,0:T(8,128)(2,1)}, bf16[4,256,1024]{2,1,0:T(8,128)(2,1)S(1)}, u32[]{:S(2)}, u32[]{:S(2)}) collective-permute-start(bf16[4,256,1024]{2,1,0:T(8,128)(2,1)} %get-tuple-element.113), channel_id=1, source_target_pairs={{0,4},{4,0},{8,12},{12,8},{16,20},{20,16},{24,28},{28,24},{1,5},{5... | collective-permute-start | bytes 6291464 | tf_op jit(solution)/shard_map/ppermute | solution.py:672
  335.4 11.1 %collective-permute-start.28 = (bf16[2,2,2,2,16,768]{5,4,3,2,1,0:T(8,128)(2,1)S(1)}, bf16[2,2,2,2,16,768]{5,4,3,2,1,0:T(8,128)(2,1)S(1)}, u32[]{:S(2)}, u32[]{:S(2)}) collective-permute-start(bf16[2,2,2,2,16,768]{5,4,3,2,1,0:T(8,128)(2,1)S(1)} %fusion.16), channel_id=1, source_target_pairs={{0,16},{4,20},{8,24},{12,28},{16,0},{20,4},{24,8},{28,12},{1,17},{... | collective-permute-start | bytes 1179656 | tf_op jit(solution)/shard_map/ppermute | solution.py:672
  338.5 11.8 %collective-permute-start.23 = (bf16[2,2,2,2,16,768]{5,4,0,2,3,1:T(8,128)(2,1)S(1)}, bf16[2,2,2,2,16,768]{5,4,0,2,3,1:T(8,128)(2,1)S(1)}, u32[]{:S(2)}, u32[]{:S(2)}) collective-permute-start(bf16[2,2,2,2,16,768]{5,4,0,2,3,1:T(8,128)(2,1)S(1)} %fusion.15), channel_id=1, source_target_pairs={{0,8},{4,12},{8,0},{12,4},{16,24},{20,28},{24,16},{28,20},{1,9},{5... | collective-permute-start | bytes 1179656 | tf_op jit(solution)/shard_map/ppermute | solution.py:672
  346.5 50.5 %collective-permute-start.9 = (bf16[4,2,2,2,16,1024]{5,4,0,2,3,1:T(8,128)(2,1)S(1)}, bf16[4,2,2,2,16,1024]{5,4,0,2,3,1:T(8,128)(2,1)S(1)}, u32[]{:S(2)}, u32[]{:S(2)}) collective-permute-start(bf16[4,2,2,2,16,1024]{5,4,0,2,3,1:T(8,128)(2,1)S(1)} %fusion), channel_id=1, source_target_pairs={{0,8},{4,12},{8,0},{12,4},{16,24},{20,28},{24,16},{28,20},{1,9},{5... | collective-permute-start | bytes 3145736 | tf_op jit(solution)/shard_map/ppermute | solution.py:672
  350.2 25.7 %collective-permute-start.29 = (bf16[2,2,2,16,768]{4,3,2,1,0:T(8,128)(2,1)S(1)}, bf16[2,2,2,16,768]{4,3,2,1,0:T(8,128)(2,1)S(1)}, u32[]{:S(2)}, u32[]{:S(2)}) collective-permute-start(bf16[2,2,2,16,768]{4,3,2,1,0:T(8,128)(2,1)S(1)} %fusion.35), channel_id=1, source_target_pairs={{0,8},{4,12},{8,0},{12,4},{16,24},{20,28},{24,16},{28,20},{1,9},{5... | collective-permute-start | bytes 589832 | tf_op jit(solution)/shard_map/ppermute | solution.py:672
  376.0 6.0 collective-permute-start.24
  381.9 5.0 collective-permute-start.30
  386.9 4.6 collective-permute-start.25
  388.4 5.6 collective-permute-start.31
  391.5 17.7 %collective-permute-start.33 = (bf16[4,2,2,2,16,768]{5,4,0,2,3,1:T(8,128)(2,1)S(1)}, bf16[4,2,2,2,16,768]{5,4,0,2,3,1:T(8,128)(2,1)S(1)}, u32[]{:S(2)}, u32[]{:S(2)}) collective-permute-start(bf16[4,2,2,2,16,768]{5,4,0,2,3,1:T(8,128)(2,1)S(1)} %fusion.6), channel_id=1, source_target_pairs={{0,8},{4,12},{8,0},{12,4},{16,24},{20,28},{24,16},{28,20},{1,9},{5... | collective-permute-start | bytes 2359304 | tf_op jit(solution)/shard_map/ppermute | solution.py:672
  394.0 88.1 %collective-permute-start.7 = (bf16[1024,512]{1,0:T(8,128)(2,1)S(1)}, bf16[1024,512]{1,0:T(8,128)(2,1)S(1)}, u32[]{:S(2)}, u32[]{:S(2)}) collective-permute-start(bf16[1024,512]{1,0:T(8,128)(2,1)S(1)} %copy-done.32), channel_id=1, source_target_pairs={{0,2},{1,3},{4,6},{5,7},{8,10},{9,11},{12,14},{13,15},{16,18},{17,... | collective-permute-start | bytes 3145736 | tf_op jit(solution)/shard_map/ppermute | solution.py:672
  397.5 18.8 %collective-permute-start.10 = (bf16[4,2,2,16,1024]{4,3,0,2,1:T(8,128)(2,1)S(1)}, bf16[4,2,2,16,1024]{4,3,0,2,1:T(8,128)(2,1)S(1)}, u32[]{:S(2)}, u32[]{:S(2)}) collective-permute-start(bf16[4,2,2,16,1024]{4,3,0,2,1:T(8,128)(2,1)S(1)} %copy.164), channel_id=1, source_target_pairs={{0,16},{4,20},{8,24},{12,28},{16,0},{20,4},{24,8},{28,12},{1,17},{... | collective-permute-start | bytes 1572872 | tf_op jit(solution)/shard_map/ppermute | solution.py:672
  398.6 17.7 %collective-permute-start.26 = (bf16[2,16,768]{2,1,0:T(8,128)(2,1)S(1)}, bf16[2,16,768]{2,1,0:T(8,128)(2,1)S(1)}, u32[]{:S(2)}, u32[]{:S(2)}) collective-permute-start(bf16[2,16,768]{2,1,0:T(8,128)(2,1)S(1)} %fusion.59), channel_id=1, source_target_pairs={{0,2},{1,3},{2,0},{3,1},{4,6},{5,7},{6,4},{7,5},{8,10},{9,11},{10,... | collective-permute-start | bytes 147464 | tf_op jit(solution)/shard_map/ppermute | solution.py:672
  409.2 67.7 %collective-permute-start.38 = (bf16[4,2,2,2,16,1024]{5,4,3,2,1,0:T(8,128)(2,1)S(1)}, bf16[4,2,2,2,16,1024]{5,4,3,2,1,0:T(8,128)(2,1)S(1)}, u32[]{:S(2)}, u32[]{:S(2)}) collective-permute-start(bf16[4,2,2,2,16,1024]{5,4,3,2,1,0:T(8,128)(2,1)S(1)} %fusion.1), channel_id=1, source_target_pairs={{0,8},{4,12},{8,0},{12,4},{16,24},{20,28},{24,16},{28,20},{1,9},{5... | collective-permute-start | bytes 3145736 | tf_op jit(solution)/shard_map/ppermute | solution.py:672
  416.3 24.4 %collective-permute-start.34 = (bf16[4,2,2,16,768]{4,3,0,2,1:T(8,128)(2,1)S(1)}, bf16[4,2,2,16,768]{4,3,0,2,1:T(8,128)(2,1)S(1)}, u32[]{:S(2)}, u32[]{:S(2)}) collective-permute-start(bf16[4,2,2,16,768]{4,3,0,2,1:T(8,128)(2,1)S(1)} %copy.192), channel_id=1, source_target_pairs={{0,16},{4,20},{8,24},{12,28},{16,0},{20,4},{24,8},{28,12},{1,17},{... | collective-permute-start | bytes 1179656 | tf_op jit(solution)/shard_map/ppermute | solution.py:672
  416.5 34.5 %collective-permute-start.11 = (bf16[4,2,16,1024]{3,2,0,1:T(8,128)(2,1)S(1)}, bf16[4,2,16,1024]{3,2,0,1:T(8,128)(2,1)S(1)}, u32[]{:S(2)}, u32[]{:S(2)}) collective-permute-start(bf16[4,2,16,1024]{3,2,0,1:T(8,128)(2,1)S(1)} %get-tuple-element.155), channel_id=1, source_target_pairs={{0,1},{1,0},{2,3},{3,2},{4,5},{5,4},{6,7},{7,6},{8,9},{9,8},{10,11... | collective-permute-start | bytes 786440 | tf_op jit(solution)/shard_map/ppermute | solution.py:672
  440.8 16.2 %collective-permute-start.35 = (bf16[4,2,16,768]{3,2,0,1:T(8,128)(2,1)S(1)}, bf16[4,2,16,768]{3,2,0,1:T(8,128)(2,1)S(1)}, u32[]{:S(2)}, u32[]{:S(2)}) collective-permute-start(bf16[4,2,16,768]{3,2,0,1:T(8,128)(2,1)S(1)} %get-tuple-element.157), channel_id=1, source_target_pairs={{0,1},{1,0},{2,3},{3,2},{4,5},{5,4},{6,7},{7,6},{8,9},{9,8},{10,11... | collective-permute-start | bytes 589832 | tf_op jit(solution)/shard_map/ppermute | solution.py:672
  451.1 164.9 %collective-permute-start.16 = (bf16[1024,512]{1,0:T(8,128)(2,1)}, bf16[1024,512]{1,0:T(8,128)(2,1)}, u32[]{:S(2)}, u32[]{:S(2)}) collective-permute-start(bf16[1024,512]{1,0:T(8,128)(2,1)} %get-tuple-element.139), channel_id=1, source_target_pairs={{1,2},{0,3},{5,6},{4,7},{9,10},{8,11},{13,14},{12,15},{17,18},{16,... | collective-permute-start | bytes 3145736 | tf_op jit(solution)/shard_map/ppermute | solution.py:672
  457.0 23.8 %collective-permute-start.12 = (bf16[4,16,1024]{2,1,0:T(8,128)(2,1)S(1)}, bf16[4,16,1024]{2,1,0:T(8,128)(2,1)S(1)}, u32[]{:S(2)}, u32[]{:S(2)}) collective-permute-start(bf16[4,16,1024]{2,1,0:T(8,128)(2,1)S(1)} %fusion.46), channel_id=1, source_target_pairs={{0,2},{1,3},{2,0},{3,1},{4,6},{5,7},{6,4},{7,5},{8,10},{9,11},{10,... | collective-permute-start | bytes 393224 | tf_op jit(solution)/shard_map/ppermute | solution.py:672
  476.9 40.4 %collective-permute-start.36 = (bf16[4,16,768]{2,1,0:T(8,128)(2,1)S(1)}, bf16[4,16,768]{2,1,0:T(8,128)(2,1)S(1)}, u32[]{:S(2)}, u32[]{:S(2)}) collective-permute-start(bf16[4,16,768]{2,1,0:T(8,128)(2,1)S(1)} %fusion.53), channel_id=1, source_target_pairs={{0,2},{1,3},{2,0},{3,1},{4,6},{5,7},{6,4},{7,5},{8,10},{9,11},{10,... | collective-permute-start | bytes 294920 | tf_op jit(solution)/shard_map/ppermute | solution.py:672
  480.8 35.2 %collective-permute-start.39 = (bf16[4,2,2,16,1024]{4,3,2,1,0:T(8,128)(2,1)S(1)}, bf16[4,2,2,16,1024]{4,3,2,1,0:T(8,128)(2,1)S(1)}, u32[]{:S(2)}, u32[]{:S(2)}) collective-permute-start(bf16[4,2,2,16,1024]{4,3,2,1,0:T(8,128)(2,1)S(1)} %fusion.9), channel_id=1, source_target_pairs={{0,16},{4,20},{8,24},{12,28},{16,0},{20,4},{24,8},{28,12},{1,17},{... | collective-permute-start | bytes 1572872 | tf_op jit(solution)/shard_map/ppermute | solution.py:672
  484.6 131.3 %collective-permute-start.13 = (bf16[1024,512]{1,0:T(8,128)(2,1)}, bf16[1024,512]{1,0:T(8,128)(2,1)}, u32[]{:S(2)}, u32[]{:S(2)}) collective-permute-start(bf16[1024,512]{1,0:T(8,128)(2,1)} %get-tuple-element.131), channel_id=1, source_target_pairs={{0,1},{1,0},{4,5},{5,4},{8,9},{9,8},{12,13},{13,12},{16,17},{17,16... | collective-permute-start | bytes 3145736 | tf_op jit(solution)/shard_map/ppermute | solution.py:672
  514.4 101.5 %collective-permute-start.15 = (bf16[1024,512]{1,0:T(8,128)(2,1)}, bf16[1024,512]{1,0:T(8,128)(2,1)}, u32[]{:S(2)}, u32[]{:S(2)}) collective-permute-start(bf16[1024,512]{1,0:T(8,128)(2,1)} %get-tuple-element.131), channel_id=1, source_target_pairs={{3,0},{2,1},{7,4},{6,5},{11,8},{10,9},{15,12},{14,13},{19,16},{18,... | collective-permute-start | bytes 3145736 | tf_op jit(solution)/shard_map/ppermute | solution.py:672
  515.9 100.0 %collective-permute-start.14 = (bf16[1024,512]{1,0:T(8,128)(2,1)}, bf16[1024,512]{1,0:T(8,128)(2,1)}, u32[]{:S(2)}, u32[]{:S(2)}) collective-permute-start(bf16[1024,512]{1,0:T(8,128)(2,1)} %get-tuple-element.130), channel_id=1, source_target_pairs={{2,0},{3,1},{6,4},{7,5},{10,8},{11,9},{14,12},{15,13},{18,16},{19,... | collective-permute-start | bytes 3145736 | tf_op jit(solution)/shard_map/ppermute | solution.py:672
  517.3 46.9 %collective-permute-start.40 = (bf16[4,2,16,1024]{3,2,1,0:T(8,128)(2,1)S(1)}, bf16[4,2,16,1024]{3,2,1,0:T(8,128)(2,1)S(1)}, u32[]{:S(2)}, u32[]{:S(2)}) collective-permute-start(bf16[4,2,16,1024]{3,2,1,0:T(8,128)(2,1)S(1)} %fusion.25), channel_id=1, source_target_pairs={{0,1},{1,0},{2,3},{3,2},{4,5},{5,4},{6,7},{7,6},{8,9},{9,8},{10,11... | collective-permute-start | bytes 786440 | tf_op jit(solution)/shard_map/ppermute | solution.py:672
  522.5 49.7 %copy-start.26 = (f32[1,4,16,768]{3,2,1,0:T(8,128)}, f32[1,4,16,768]{3,2,1,0:T(8,128)S(1)}, u32[]{:S(2)}) copy-start(f32[1,4,16,768]{3,2,1,0:T(8,128)S(1)} %fusion.39) | copy-start | bytes 589828
  565.0 47.4 %collective-permute-start.41 = (bf16[4,16,1024]{2,1,0:T(8,128)(2,1)S(1)}, bf16[4,16,1024]{2,1,0:T(8,128)(2,1)}, u32[]{:S(2)}, u32[]{:S(2)}) collective-permute-start(bf16[4,16,1024]{2,1,0:T(8,128)(2,1)S(1)} %fusion.48), channel_id=1, source_target_pairs={{0,2},{1,3},{2,0},{3,1},{4,6},{5,7},{6,4},{7,5},{8,10},{9,11},{10,... | collective-permute-start | bytes 393224 | tf_op jit(solution)/shard_map/ppermute | solution.py:672
  (40 other events, 747.8 us)

commit v2 on v1

--- a/solution.py
+++ b/solution.py
@@ -12,7 +12,7 @@
 GROUP = 8
 TILE_C = 256
 TILE_F = 512
-BIG = 256
+BIG = 1024
 F32 = jnp.float32
 BF16 = jnp.bfloat16
 ROOT_2_PI = 0.7978845608028654
@@ -243,21 +243,25 @@
     dgain_ref[...] = lax.fori_loop(0, x_ref.shape[0] // 64, at, jnp.zeros(gain.shape, F32))
 
 
-def put_halves(keep_ref, send_ref, bit_ref, index, lanes, values):
-    low = values[:SPLIT].astype(BF16)
-    high = values[SPLIT:].astype(BF16)
+def put_grad(refs, bit_ref, lanes, values):
+    if len(refs) == 1:
+        refs[0][:, lanes] = values.astype(BF16)
+        return
     mine = bit_ref[0] == 1
-    rows = pl.ds(pl.multiple_of(index * SPLIT, SPLIT), SPLIT)
-    keep_ref[0, rows, lanes] = jnp.where(mine, high, low)
-    send_ref[0, rows, lanes] = jnp.where(mine, low, high)
+    for pair in range(values.shape[0] // (2 * SPLIT)):
+        low = values[2 * pair * SPLIT : (2 * pair + 1) * SPLIT].astype(BF16)
+        high = values[(2 * pair + 1) * SPLIT : (2 * pair + 2) * SPLIT].astype(BF16)
+        rows = pl.ds(pair * SPLIT, SPLIT)
+        refs[0][rows, lanes] = jnp.where(mine, high, low)
+        refs[1][rows, lanes] = jnp.where(mine, low, high)
 
 
 def mixer_backward_kernel(
     x_ref, g_ref, gain_ref, wg_ref, wc_ref, kg_ref, kc_ref, wo_ref, mask_ref, init_ref,
-    p_ref, z_ref, cand_ref, h_ref, bit_ref,
-    dx_ref, keep_ref, send_ref, small_ref, dgain_ref,
-    normed_t, upstream, upstream_t, natural, total, local, decay, dconv, dproj,
+    p_ref, z_ref, cand_ref, h_ref, bit_ref, *rest,
 ):
+    *dw, dx_ref, small_ref, dgain_ref = rest[:-9]
+    (normed_t, upstream, upstream_t, natural, total, local, decay, dconv, dproj) = rest[-9:]
     step = pl.program_id(0)
     seq = x_ref.shape[0]
     width = wg_ref.shape[1]
@@ -384,15 +388,8 @@
                 small_ref[0, k : k + 1, lanes] = jnp.sum(sums[tile][k], axis=0, keepdims=True)
             small_ref[0, 5:8, lanes] = jnp.zeros((3, LANES), F32)
 
-    def weight_grads(index, carry):
-        rows = pl.ds(pl.multiple_of(index * 128, 128), 128)
-        put_halves(keep_ref, send_ref, bit_ref, index, pl.ds(0, 2 * width), dot_nn(normed_t[rows, :], dproj[...]))
-        put_halves(
-            keep_ref, send_ref, bit_ref, index, pl.ds(2 * width, width), dot_nn(upstream_t[rows, :], h_ref[...])
-        )
-        return carry
-
-    lax.fori_loop(0, normed_t.shape[0] // 128, weight_grads, 0)
+    put_grad(dw, bit_ref, pl.ds(0, 2 * width), dot_nn(normed_t[...], dproj[...]))
+    put_grad(dw, bit_ref, pl.ds(2 * width, width), dot_nn(upstream_t[...], h_ref[...]))
 
     def back_normed(rows):
         total[rows, :] += dot_nt(dproj[rows, pl.ds(0, width)], wg_ref[...]) + dot_nt(
@@ -440,10 +437,10 @@
 
 
 def mlp_backward_kernel(
-    x_ref, g_ref, gain_ref, wu_ref, wd_ref, u_ref, bit_ref,
-    dx_ref, keep_ref, send_ref, dbu_ref, dbd_ref, dgain_ref,
-    normed_t, upstream_t, total, active, dpre,
+    x_ref, g_ref, gain_ref, wu_ref, wd_ref, u_ref, bit_ref, *rest,
 ):
+    *dw, dx_ref, dbu_ref, dbd_ref, dgain_ref = rest[:-5]
+    normed_t, upstream_t, total, active, dpre = rest[-5:]
     step = pl.program_id(0)
     seq = x_ref.shape[0]
     width = wu_ref.shape[1]
@@ -478,15 +475,8 @@
 
     dbu_ref[...] = lax.fori_loop(0, seq // BIG, at, jnp.zeros(dbu_ref.shape, F32))
 
-    def weight_grads(index, carry):
-        rows = pl.ds(pl.multiple_of(index * 128, 128), 128)
-        put_halves(keep_ref, send_ref, bit_ref, index, pl.ds(0, width), dot_nn(normed_t[rows, :], dpre[...]))
-        put_halves(
-            keep_ref, send_ref, bit_ref, index, pl.ds(width, width), dot_nn(upstream_t[rows, :], active[...])
-        )
-        return carry
-
-    lax.fori_loop(0, normed_t.shape[0] // 128, weight_grads, 0)
+    put_grad(dw, bit_ref, pl.ds(0, width), dot_nn(normed_t[...], dpre[...]))
+    put_grad(dw, bit_ref, pl.ds(width, width), dot_nn(upstream_t[...], active[...]))
 
     @pl.when(step == pl.num_programs(0) - 1)
     def _():
@@ -503,6 +493,123 @@
 
 
 SCALAR = pl.BlockSpec(memory_space=pltpu.SMEM)
+ANYWHERE = pl.BlockSpec(memory_space=pl.ANY)
+MESH = pl.DeviceIdType.MESH
+SECTIONS = 4
+
+
+def meet_sections(section):
+    barrier = pltpu.get_barrier_semaphore()
+    for by in range(1, SECTIONS):
+        other = (section + by) % SECTIONS
+        pl.semaphore_signal(barrier, inc=1, device_id={"section": other}, device_id_type=MESH)
+    pl.semaphore_wait(barrier, SECTIONS - 1)
+
+
+def delivery(jobs, sources, buffers, send_sems, recv_sems):
+    section = lax.axis_index("section")
+
+    def copy(number, sender):
+        source, part, first, count, buffer = jobs[number]
+        rows = pl.ds(first, count)
+        return pltpu.make_async_remote_copy(
+            src_ref=sources[source][0].at[sources[source][1], rows] if sources[source][1] is not None
+            else sources[source][0].at[rows],
+            dst_ref=buffers[buffer].at[sender, rows],
+            send_sem=send_sems.at[number],
+            recv_sem=recv_sems.at[number, sender],
+            device_id={"section": part},
+            device_id_type=MESH,
+        )
+
+    def start():
+        for number, job in enumerate(jobs):
+
+            @pl.when(section != job[1])
+            def _(number=number):
+                copy(number, section).start()
+
+    def wait():
+        for number, job in enumerate(jobs):
+
+            @pl.when(section != job[1])
+            def _(number=number):
+                copy(number, section).wait_send()
+
+            @pl.when(section == job[1])
+            def _(number=number, job=job):
+                for sender in range(SECTIONS):
+                    if sender != job[1]:
+                        copy(number, sender).wait_recv()
+
+    return start, wait
+
+
+class Cargo:
+    def __init__(self, collective_id, arrays, sources, buffers, jobs, dims):
+        self.collective_id = collective_id
+        self.arrays = list(arrays)
+        self.sources = sources
+        self.old = [b for b in buffers if b is not None]
+        self.buffers = buffers
+        self.jobs = jobs
+        self.dims = dims
+
+
+def call(kernel, cargo, *, grid, in_specs, out_specs, out_shape, scratch_shapes, cost_estimate, name, args, aliases=None):
+    aliases = dict(aliases or {})
+    if cargo is None:
+        return pl.pallas_call(
+            kernel, grid=grid, in_specs=in_specs, out_specs=out_specs, out_shape=out_shape,
+            scratch_shapes=scratch_shapes, compiler_params=PARAMS, cost_estimate=cost_estimate, name=name,
+            input_output_aliases=aliases,
+        )(*args)
+    n_in, n_out = len(in_specs), len(out_specs)
+    n_array, n_old, n_buffer = len(cargo.arrays), len(cargo.old), len(cargo.buffers)
+
+    def carrying(*refs):
+        ins, refs = refs[:n_in], refs[n_in:]
+        arrays, refs = refs[:n_array], refs[n_array + n_old :]
+        outs, refs = refs[:n_out], refs[n_out:]
+        buffers, refs = refs[:n_buffer], refs[n_buffer:]
+        own, (send_sems, recv_sems) = refs[:-2], refs[-2:]
+        sources = [(arrays[a], at) for a, at in cargo.sources]
+        start, wait = delivery(cargo.jobs, sources, buffers, send_sems, recv_sems)
+        step = pl.program_id(0)
+
+        @pl.when(step == 0)
+        def _():
+            meet_sections(lax.axis_index("section"))
+            start()
+
+        kernel(*ins, *outs, *own)
+
+        @pl.when(step == pl.num_programs(0) - 1)
+        def _():
+            wait()
+
+    old = 0
+    for number, buffer in enumerate(cargo.buffers):
+        if buffer is not None:
+            aliases[n_in + n_array + old] = n_out + number
+            old += 1
+    jobs = len(cargo.jobs)
+    return pl.pallas_call(
+        carrying,
+        grid=grid,
+        in_specs=list(in_specs) + [ANYWHERE] * (n_array + n_old),
+        out_specs=list(out_specs) + [ANYWHERE] * n_buffer,
+        out_shape=list(out_shape) + [shape(cargo.dims, BF16)] * n_buffer,
+        scratch_shapes=list(scratch_shapes)
+        + [pltpu.SemaphoreType.DMA((jobs,)), pltpu.SemaphoreType.DMA((jobs, SECTIONS))],
+        compiler_params=pltpu.CompilerParams(
+            dimension_semantics=("arbitrary",), vmem_limit_bytes=56 * 1024 * 1024,
+            collective_id=cargo.collective_id, has_side_effects=True,
+        ),
+        cost_estimate=cost_estimate,
+        name=name,
+        input_output_aliases=aliases,
+    )(*args, *cargo.arrays, *cargo.old)
 
 
 def cost(seq, microseconds):
@@ -513,6 +620,12 @@
 
 def whole(dims):
     return pl.BlockSpec(dims, lambda i: (0,) * len(dims))
+
+
+def source_spec(stack, at):
+    if at is None:
+        return whole(stack.shape)
+    return pl.BlockSpec((None,) + stack.shape[1:], lambda i: (at, 0, 0))
 
 
 def mixer_specs(layer, width, hidden, tile):
@@ -530,8 +643,8 @@
     )
 
 
-def mixer_forward(layer, x, masks, init, gain, weight_in, taps, bias, weight_out):
-    seq, width = x.shape
+def mixer_forward(layer, stack, at, masks, init, gain, weight_in, taps, bias, weight_out):
+    seq, width = stack.shape[-2:]
     hidden = init.shape[2]
     tile = TILE_C
     count = hidden // tile
@@ -541,15 +654,15 @@
         mixer_forward_kernel,
         grid=(count,),
         in_specs=[
-            whole(x.shape), spec["gain"], spec["gate"], spec["cand"], spec["tap_gate"], spec["tap_cand"],
+            source_spec(stack, at), spec["gain"], spec["gate"], spec["cand"], spec["tap_gate"], spec["tap_cand"],
             spec["bias_gate"], spec["bias_cand"], spec["out"], whole(masks.shape), spec["init"],
         ],
         out_specs=[
-            whole(x.shape), pl.BlockSpec((1, seq, 2 * tile), lambda i: (i, 0, 0)), column, column, column,
+            pl.BlockSpec((None, seq, width), lambda i: (2 * layer, 0, 0)), pl.BlockSpec((1, seq, 2 * tile), lambda i: (i, 0, 0)), column, column, column,
             pl.BlockSpec((1, tile), lambda i: (0, i)),
         ],
         out_shape=[
-            shape(x.shape, BF16), shape((count, seq, 2 * tile), BF16), shape((seq, hidden), BF16),
+            shape((4, seq, width), BF16), shape((count, seq, 2 * tile), BF16), shape((seq, hidden), BF16),
             shape((seq, hidden), BF16), shape((seq, hidden), BF16), shape((1, hidden), F32),
         ],
         scratch_shapes=[
@@ -558,33 +671,42 @@
         ],
         compiler_params=PARAMS,
         cost_estimate=cost(seq, 15),
+        input_output_aliases={} if at is None else {0: 0},
         name="mixer_forward",
-    )(x, gain, weight_in, weight_in, taps, taps, bias, bias, weight_out, masks, init)
-
-
-def mixer_backward(layer, x, g, stash, masks, init, gain, weight_in, taps, weight_out, bit):
-    seq, width = x.shape
+    )(stack, gain, weight_in, weight_in, taps, taps, bias, bias, weight_out, masks, init)
+
+
+def grad_outputs(width, tile, total, split):
+    rows = width // 2 if split else width
+    parts = 2 if split else 1
+    return (
+        [pl.BlockSpec((rows, tile), lambda i: (0, i))] * parts,
+        [shape((rows, total), BF16)] * parts,
+    )
+
+
+def mixer_backward(layer, stack, at, g, stash, masks, init, gain, weight_in, taps, weight_out, bit, split, cargo):
+    seq, width = g.shape
     hidden = init.shape[2]
     tile = TILE_C
     count = hidden // tile
     spec = mixer_specs(layer, width, hidden, tile)
     column = pl.BlockSpec((seq, tile), lambda i: (0, i))
-    return pl.pallas_call(
+    dw_specs, dw_shapes = grad_outputs(width, 3 * tile, 3 * hidden, split)
+    return call(
         mixer_backward_kernel,
+        cargo,
         grid=(count,),
         in_specs=[
-            whole(x.shape), whole(x.shape), spec["gain"], spec["gate"], spec["cand"], spec["tap_gate"],
+            source_spec(stack, at), whole(g.shape), spec["gain"], spec["gate"], spec["cand"], spec["tap_gate"],
             spec["tap_cand"], spec["out"], whole(masks.shape), spec["init"],
             pl.BlockSpec((1, seq, 2 * tile), lambda i: (i, 0, 0)), column, column, column, SCALAR,
         ],
         out_specs=[
-            whole(x.shape), pl.BlockSpec((1, width // 2, 3 * tile), lambda i: (i, 0, 0)),
-            pl.BlockSpec((1, width // 2, 3 * tile), lambda i: (i, 0, 0)),
-            pl.BlockSpec((1, 8, 2 * tile), lambda i: (i, 0, 0)), whole((1, width)),
+            *dw_specs, whole(g.shape), pl.BlockSpec((1, 8, 2 * tile), lambda i: (i, 0, 0)), whole((1, width)),
         ],
         out_shape=[
-            shape(x.shape, BF16), shape((count, width // 2, 3 * tile), BF16),
-            shape((count, width // 2, 3 * tile), BF16), shape((count, 8, 2 * tile), F32),
+            *dw_shapes, shape(g.shape, BF16), shape((count, 8, 2 * tile), F32),
             shape((1, width), F32),
         ],
         scratch_shapes=[
@@ -593,66 +715,69 @@
             pltpu.VMEM((seq, tile), F32), pltpu.VMEM((seq + HALO, 2 * tile), F32),
             pltpu.VMEM((seq, 2 * tile), BF16),
         ],
-        compiler_params=PARAMS,
         cost_estimate=cost(seq, 30),
         name="mixer_backward",
-    )(x, g, gain, weight_in, weight_in, taps, taps, weight_out, masks, init, *stash, bit)
-
-
-def mlp_forward(layer, x, gain, weight_up, bias_up, weight_down, bias_down):
-    seq, width = x.shape
+        args=(stack, g, gain, weight_in, weight_in, taps, taps, weight_out, masks, init, *stash, bit),
+    )
+
+
+def mlp_forward(layer, stack, at, gain, weight_up, bias_up, weight_down, bias_down):
+    seq, width = stack.shape[-2:]
     inner = weight_up.shape[2]
     tile = TILE_F
     return pl.pallas_call(
         mlp_forward_kernel,
         grid=(inner // tile,),
         in_specs=[
-            whole(x.shape), pl.BlockSpec((None, 1, width), lambda i: (layer, 0, 0)),
+            source_spec(stack, at), pl.BlockSpec((None, 1, width), lambda i: (layer, 0, 0)),
             pl.BlockSpec((None, width, tile), lambda i: (layer, 0, i)),
             pl.BlockSpec((None, 1, tile), lambda i: (layer, 0, i)),
             pl.BlockSpec((None, tile, width), lambda i: (layer, i, 0)),
             pl.BlockSpec((None, 1, width), lambda i: (layer, 0, 0)),
         ],
-        out_specs=[whole(x.shape), pl.BlockSpec((seq, tile), lambda i: (0, i))],
-        out_shape=[shape(x.shape, BF16), shape((seq, inner), BF16)],
+        out_specs=[
+            pl.BlockSpec((None, seq, width), lambda i: (2 * layer + 1, 0, 0)),
+            pl.BlockSpec((seq, tile), lambda i: (0, i)),
+        ],
+        out_shape=[shape(stack.shape, BF16), shape((seq, inner), BF16)],
         scratch_shapes=[pltpu.VMEM((seq, width), BF16), pltpu.VMEM((seq, width), F32)],
         compiler_params=PARAMS,
         cost_estimate=cost(seq, 10),
+        input_output_aliases={0: 0},
         name="mlp_forward",
-    )(x, gain, weight_up, bias_up, weight_down, bias_down)
-
-
-def mlp_backward(layer, x, g, pre, gain, weight_up, weight_down, bit):
-    seq, width = x.shape
+    )(stack, gain, weight_up, bias_up, weight_down, bias_down)
+
+
+def mlp_backward(layer, stack, at, g, pre, gain, weight_up, weight_down, bit, split, cargo):
+    seq, width = g.shape
     inner = weight_up.shape[2]
     tile = TILE_F
-    return pl.pallas_call(
+    dw_specs, dw_shapes = grad_outputs(width, 2 * tile, 2 * inner, split)
+    return call(
         mlp_backward_kernel,
+        cargo,
         grid=(inner // tile,),
         in_specs=[
-            whole(x.shape), whole(x.shape), pl.BlockSpec((None, 1, width), lambda i: (layer, 0, 0)),
+            source_spec(stack, at), whole(g.shape), pl.BlockSpec((None, 1, width), lambda i: (layer, 0, 0)),
             pl.BlockSpec((None, width, tile), lambda i: (layer, 0, i)),
             pl.BlockSpec((None, tile, width), lambda i: (layer, i, 0)),
             pl.BlockSpec((seq, tile), lambda i: (0, i)), SCALAR,
         ],
         out_specs=[
-            whole(x.shape), pl.BlockSpec((1, width // 2, 2 * tile), lambda i: (i, 0, 0)),
-            pl.BlockSpec((1, width // 2, 2 * tile), lambda i: (i, 0, 0)),
-            pl.BlockSpec((1, tile), lambda i: (0, i)), whole((1, width)), whole((1, width)),
+            *dw_specs, whole(g.shape), pl.BlockSpec((1, tile), lambda i: (0, i)), whole((1, width)), whole((1, width)),
         ],
         out_shape=[
-            shape(x.shape, BF16), shape((inner // tile, width // 2, 2 * tile), BF16),
-            shape((inner // tile, width // 2, 2 * tile), BF16), shape((1, inner), F32),
+            *dw_shapes, shape(g.shape, BF16), shape((1, inner), F32),
             shape((1, width), F32), shape((1, width), F32),
         ],
         scratch_shapes=[
             pltpu.VMEM((width, seq), BF16), pltpu.VMEM((width, seq), BF16), pltpu.VMEM((seq, width), F32),
             pltpu.VMEM((seq, tile), BF16), pltpu.VMEM((seq, tile), BF16),
         ],
-        compiler_params=PARAMS,
         cost_estimate=cost(seq, 20),
         name="mlp_backward",
-    )(x, g, gain, weight_up, weight_down, pre, bit)
+        args=(stack, g, gain, weight_up, weight_down, pre, bit),
+    )
 
 
 def chunk_masks(resets):
@@ -672,83 +797,122 @@
     return lax.ppermute(x, axis, pairs)
 
 
-def assemble_kernel(own0, own1, own2, own3, left1, left2, left3, right1, right2, right3, out, sems):
+def last_kernel(jobs, split, dp, n_array, *refs):
+    arrays, refs = refs[:n_array], refs[n_array:]
+    (keeps, sends), refs = (refs[0:2], refs[2:4]), refs[5:]
+    buffer, outs, refs = refs[0], refs[1:3], refs[3:]
+    kept, got, parts, landed, sums = refs[0:2], refs[2:4], refs[4:6], refs[6:8], refs[8:10]
+    send_sems, recv_sems, local_sems, core_sems, part_sems = refs[10:]
     section = lax.axis_index("section")
-    lefts = (left1, left2, left3)
-    rights = (right1, right2, right3)
-    for which, own in enumerate((own0, own1, own2, own3)):
-
-        @pl.when(section == which)
-        def _():
-            pltpu.make_async_copy(own, out.at[which], sems.at[0]).start()
-
-    for k in (1, 2, 3):
-
-        @pl.when(section < 2)
-        def _():
-            pltpu.make_async_copy(lefts[k - 1], out.at[section ^ k], sems.at[k]).start()
-
-        @pl.when(section >= 2)
-        def _():
-            pltpu.make_async_copy(rights[k - 1], out.at[section ^ k], sems.at[k]).start()
-
-    for k in range(4):
-        pltpu.make_async_copy(own0, out.at[0], sems.at[k]).wait()
-
-
-def assemble(owns, lefts, rights):
-    dims = owns[0].shape
-    anywhere = pl.BlockSpec(memory_space=pl.ANY)
+    where = lax.axis_index("dp")
+    bit = (where // split) % 2
+    partner = where + split * (1 - 2 * bit)
+    top = dp // 4 if split * 4 < dp else 0
+    steps = [step for step in bits_of(dp) if step != split][-2:]
+    low_bit, high_bit = (where // steps[0]) % 2, (where // steps[1]) % 2
+    mine = low_bit + 2 * high_bit
+
+    def flipped(mask):
+        low, high = mask % 2, mask // 2
+        new_low = low_bit + low * (1 - 2 * low_bit)
+        new_high = high_bit + high * (1 - 2 * high_bit)
+        device = where + steps[0] * (new_low - low_bit) + steps[1] * (new_high - high_bit)
+        return new_low + 2 * new_high, device
+
+    barrier = pltpu.get_barrier_semaphore()
+    for by in range(1, SECTIONS):
+        other = (section + by) % SECTIONS
+        pl.semaphore_signal(barrier, inc=1, device_id={"section": other}, device_id_type=MESH)
+    pl.semaphore_signal(barrier, inc=1, device_id={"dp": partner}, device_id_type=MESH)
+    for mask in (1, 2, 3):
+        pl.semaphore_signal(barrier, inc=1, device_id={"dp": flipped(mask)[1]}, device_id_type=MESH)
+    pl.semaphore_wait(barrier, SECTIONS + 3)
+
+    start, wait = delivery(jobs, [(a, None) for a in arrays], [buffer], send_sems, recv_sems)
+    swaps, loads = [], []
+    for n in range(2):
+        swap = pltpu.make_async_remote_copy(
+            src_ref=sends[n], dst_ref=got[n], send_sem=core_sems.at[0, n], recv_sem=core_sems.at[1, n],
+            device_id={"dp": partner}, device_id_type=MESH,
+        )
+        swap.start()
+        load = pltpu.make_async_copy(keeps[n], kept[n], local_sems.at[n])
+        load.start()
+        swaps.append(swap)
+        loads.append(load)
+    start()
+    moves = []
+    for n in range(2):
+        loads[n].wait()
+        swaps[n].wait()
+        rows = kept[n].shape[0] // 4
+        for mask in (1, 2, 3):
+            quarter, device = flipped(mask)
+            taken = pl.ds(pl.multiple_of(quarter * rows, rows), rows)
+            parts[n][mask - 1] = (kept[n][taken, :].astype(F32) + got[n][taken, :].astype(F32)).astype(BF16)
+            move = pltpu.make_async_remote_copy(
+                src_ref=parts[n].at[mask - 1], dst_ref=landed[n].at[mask - 1],
+                send_sem=part_sems.at[0, n, mask - 1], recv_sem=part_sems.at[1, n, mask - 1],
+                device_id={"dp": device}, device_id_type=MESH,
+            )
+            move.start()
+            moves.append(move)
+    for n in range(2):
+        rows = kept[n].shape[0] // 4
+        taken = pl.ds(pl.multiple_of(mine * rows, rows), rows)
+        total = kept[n][taken, :].astype(F32) + got[n][taken, :].astype(F32)
+        for mask in (1, 2, 3):
+            moves[3 * n + mask - 1].wait()
+            total = total + landed[n][mask - 1].astype(F32)
+        sums[n][...] = total.astype(BF16)
+        store = pltpu.make_async_copy(sums[n], outs[n], local_sems.at[n])
+        store.start()
+        store.wait()
+    wait()
+
+
+def finish(cargo, keeps, sends, dp, width):
+    quarters = [(k.shape[0] // 4, k.shape[1]) for k in keeps]
+    n_array = len(cargo.arrays)
+    jobs = len(cargo.jobs)
     return pl.pallas_call(
-        assemble_kernel,
-        in_specs=[anywhere] * 10,
-        out_specs=pl.BlockSpec(memory_space=pltpu.VMEM),
-        out_shape=shape((4,) + dims, owns[0].dtype),
-        scratch_shapes=[pltpu.SemaphoreType.DMA((4,))],
-        compiler_params=pltpu.CompilerParams(vmem_limit_bytes=32 * 1024 * 1024),
-        name="assemble",
-    )(*owns, *lefts, *rights)[None]
-
-
-def after(value, *others):
-    return lax.optimization_barrier((value,) + others)
-
-
-def send_low(first, second, odd):
-    one = jnp.where(odd, first, second)
-    two = jnp.where(odd, second, first)
-    return (
-        permute(one, "section", [(0, 1), (1, 0)]),
-        permute(two, "section", [(2, 0), (3, 1)]),
-        permute(one, "section", [(3, 0), (2, 1)]),
-    )
-
-
-def send_high(third, fourth, odd):
-    one = jnp.where(odd, third, fourth)
-    two = jnp.where(odd, fourth, third)
-    return (
-        permute(one, "section", [(2, 3), (3, 2)]),
-        permute(two, "section", [(0, 2), (1, 3)]),
-        permute(one, "section", [(1, 2), (0, 3)]),
-    )
-
-
-def swap_pairs(size, step):
-    return [(i, i ^ step) for i in range(size)]
-
-
-def halve(addends, dim, axis, size, step):
-    bit = (lax.axis_index(axis) // step) % 2
+        functools.partial(last_kernel, cargo.jobs, first_step(dp, width), dp, n_array),
+        in_specs=[ANYWHERE] * (n_array + 5),
+        out_specs=[ANYWHERE] * 3,
+        out_shape=[shape(cargo.dims, BF16)] + [shape(q, BF16) for q in quarters],
+        scratch_shapes=[pltpu.VMEM(k.shape, BF16) for k in keeps] * 2
+        + [pltpu.VMEM((3,) + q, BF16) for q in quarters] * 2
+        + [pltpu.VMEM(q, BF16) for q in quarters]
+        + [
+            pltpu.SemaphoreType.DMA((jobs,)), pltpu.SemaphoreType.DMA((jobs, SECTIONS)),
+            pltpu.SemaphoreType.DMA((2,)), pltpu.SemaphoreType.DMA((2, 2)), pltpu.SemaphoreType.DMA((2, 2, 3)),
+        ],
+        compiler_params=pltpu.CompilerParams(
+            vmem_limit_bytes=56 * 1024 * 1024, collective_id=cargo.collective_id, has_side_effects=True
+        ),
+        input_output_aliases={n_array + 4: 0},
+        name="finish",
+    )(*cargo.arrays, *keeps, *sends, cargo.old[0])
+
+
+def add_up(pieces):
+    return functools.reduce(jnp.add, [piece.astype(F32) for piece in pieces])
+
+
+def exchange(addends, axis, size, steps):
+    where = lax.axis_index(axis)
+    own = sum(((where // step) % 2) << k for k, step in enumerate(steps))
+    blocks = [a.reshape((1 << len(steps), -1) + a.shape[-1:]) for a in addends]
 
     def part(which):
-        pieces = [
-            lax.dynamic_index_in_dim(a, which, dim, keepdims=False).astype(F32) for a in addends
-        ]
-        return functools.reduce(jnp.add, pieces).astype(addends[0].dtype)
-
-    got = permute(part(1 - bit), axis, swap_pairs(size, step))
-    return [part(bit), got]
+        taken = [lax.dynamic_index_in_dim(b, which, 0, keepdims=False) for b in blocks]
+        return add_up(taken).astype(BF16)
+
+    result = [part(own)]
+    for mask in range(1, 1 << len(steps)):
+        flip = sum(step for k, step in enumerate(steps) if mask >> k & 1)
+        result.append(permute(part(own ^ mask), axis, [(i, i ^ flip) for i in range(size)]))
+    return result
 
 
 def bits_of(size):
@@ -759,36 +923,16 @@
     return SPLIT // (width // dp)
 
 
-def sum_rows(keep, send, dp, sections, width, reverse=False):
-    split = first_step(dp, width)
-    got = permute(send, "dp", swap_pairs(dp, split))
-    rest = [step for step in bits_of(dp) if step != split]
-    share = width // (dp * sections)
-    tiles, _, count = keep.shape
-    names = [("dp", dp, step) for step in rest[::-1]]
-    names += [("section", sections, step) for step in bits_of(sections)[::-1]]
-    dims = (tiles,) + (2,) * len(names) + (share, count)
-    addends = [keep.reshape(dims), got.reshape(dims)]
-    order = [("dp", dp, step) for step in (rest[::-1] if reverse else rest)]
-    order += [("section", sections, step) for step in bits_of(sections)]
-    left = list(names)
-    for item in order:
-        addends = halve(addends, 1 + left.index(item), *item)
-        left.remove(item)
-    return addends[0].astype(F32) + addends[1].astype(F32)
-
-
-def sum_small(packed, dp, sections):
-    names = [("dp", dp, step) for step in bits_of(dp)[::-1]]
-    names += [("section", sections, step) for step in bits_of(sections)[::-1]]
-    addends = [packed.reshape((2,) * len(names) + packed.shape[1:])]
-    order = [("dp", dp, step) for step in bits_of(dp)]
-    order += [("section", sections, step) for step in bits_of(sections)]
-    left = list(names)
-    for item in order:
-        addends = halve(addends, left.index(item), *item)
-        left.remove(item)
-    return addends[0] + addends[1]
+def sum_rest(addends, dp, width):
+    rest = [step for step in bits_of(dp) if step != first_step(dp, width)][:-2]
+    while rest:
+        top, rest = rest[-2:], rest[:-2]
+        addends = exchange(addends, "dp", dp, top)
+    return addends
+
+
+def sum_section(addends, sections):
+    return add_up(exchange(addends, "section", sections, bits_of(sections)))
 
 
 def body(
@@ -799,7 +943,6 @@
     sections = lax.axis_size("section")
     section = lax.axis_index("section")
     width = tokens.shape[2]
-    odd = section % 2 == 1
     bit = ((lax.axis_index("dp") // first_step(dp, width)) % 2).astype(jnp.int32).reshape(1)
 
     def own(values, axis):
@@ -814,58 +957,59 @@
     conv_bias = conv_bias[:, None, :]
     up_bias = up_bias[:, None, :]
     down_bias = down_bias[:, None, :]
-
-    def mixer(layer, x):
-        y, *stash, final = mixer_forward(
-            layer, x, masks, init, mix_gain, mix_in, conv_weight, conv_bias, mix_out
-        )
-        return y, stash, final
-
-    def mlp(layer, x):
-        return mlp_forward(layer, x, mlp_gain, mlp_up, up_bias, mlp_down, down_bias)
-
-    x1, stash0, final0 = mixer(0, x0)
-    x2, pre0 = mlp(0, x1)
-    act_low = send_low(x1, x2, odd)
-    x3, stash1, final1 = mixer(1, x2)
-    x4, pre1 = mlp(1, x3)
-    act_high = send_high(x3, x4, odd)
-    final = jnp.concatenate([final0, final1], axis=0)[:, None, :]
-    final_states = lax.all_to_all(final, "section", split_axis=2, concat_axis=1, tiled=True)
-
-    g3, up1_keep, up1_send, dbu1, dbd1, dgain_mlp1 = mlp_backward(
-        1, x3, g4, pre1, mlp_gain, mlp_up, mlp_down, bit
-    )
-    mlp1 = sum_rows(up1_keep, up1_send, dp, sections, width)
-    act_low = list(act_low)
-    g3, act_low[0], act_low[1] = after(g3, act_low[0], act_low[1])
-    g2, in1_keep, in1_send, small1, dgain_mix1 = mixer_backward(
-        1, x2, g3, stash1, masks, init, mix_gain, mix_in, conv_weight, mix_out, bit
-    )
-    g2, act_low[2] = after(g2, act_low[2])
-    dx_high = send_high(g2, g3, odd)
-    mix1 = sum_rows(in1_keep, in1_send, dp, sections, width)
-    g1, up0_keep, up0_send, dbu0, dbd0, dgain_mlp0 = mlp_backward(
-        0, x1, g2, pre0, mlp_gain, mlp_up, mlp_down, bit
-    )
-    act_high = list(act_high)
-    g1, act_high[0], act_high[1], act_high[2] = after(g1, *act_high)
-    mlp0 = sum_rows(up0_keep, up0_send, dp, sections, width)
-    g0, in0_keep, in0_send, small0, dgain_mix0 = mixer_backward(
-        0, x0, g1, stash0, masks, init, mix_gain, mix_in, conv_weight, mix_out, bit
-    )
-    dx_high = list(dx_high)
-    g0, dx_high[0], dx_high[1], mlp1 = after(g0, dx_high[0], dx_high[1], mlp1)
-    dx_low = send_low(g0, g1, odd)
-    half = in0_keep.shape[0] // 2
-    mix0 = jnp.concatenate(
-        [
-            sum_rows(in0_keep[:half], in0_send[:half], dp, sections, width),
-            sum_rows(in0_keep[half:], in0_send[half:], dp, sections, width, True),
-        ]
-    )
-    activations = assemble((x1, x2, x3, x4), act_low, act_high)
-    input_grads = assemble((g0, g1, g2, g3), dx_low, dx_high)
+    mixer_weights = (mix_gain, mix_in, conv_weight, conv_bias, mix_out)
+    mlp_weights = (mlp_gain, mlp_up, up_bias, mlp_down, down_bias)
+
+    stack, *stash0, final0 = mixer_forward(0, x0, None, masks, init, *mixer_weights)
+    stack, pre0 = mlp_forward(0, stack, 0, *mlp_weights)
+    stack, *stash1, final1 = mixer_forward(1, stack, 1, masks, init, *mixer_weights)
+    stack, pre1 = mlp_forward(1, stack, 2, *mlp_weights)
+
+    seq = tokens.shape[1]
+    dims = (sections, seq, width)
+    stacked = [(0, part) for part in range(4)]
+
+    def cuts(*shares):
+        edges = [seq * share // 16 for share in shares]
+        return [(a, b - a) for a, b in zip(edges, edges[1:])]
+
+    def every(span, buffer=0):
+        return [(part, part, *span, buffer) for part in range(4)]
+
+    spans = cuts(0, 4, 10, 14, 16)
+    back_mixer = (mix_gain, mix_in, conv_weight, mix_out, bit)
+    back_mlp = (mlp_gain, mlp_up, mlp_down, bit)
+    cargo = Cargo(1, [stack], stacked, [None], every(spans[0]), dims)
+    up1, g3, dbu1, dbd1, dgain_mlp1, acts = mlp_backward(1, stack, 2, g4, pre1, *back_mlp, False, cargo)
+    mlp1 = lax.psum_scatter(up1, "dp", scatter_dimension=0, tiled=True)
+    cargo = Cargo(2, [stack], stacked, [acts], every(spans[1]), dims)
+    in1, g2, small1, dgain_mix1, acts = mixer_backward(
+        1, stack, 1, g3, stash1, masks, init, *back_mixer, False, cargo
+    )
+    mix1 = lax.psum_scatter(in1, "dp", scatter_dimension=0, tiled=True)
+    cargo = Cargo(3, [stack], stacked, [acts], every(spans[2]), dims)
+    up0_keep, up0_send, g1, dbu0, dbd0, dgain_mlp0, acts = mlp_backward(
+        0, stack, 0, g2, pre0, *back_mlp, True, cargo
+    )
+    (early, late), (early1, late1) = cuts(0, 4, 16), cuts(0, 8, 16)
+    jobs = every(spans[3]) + [(4, 3, *early, 1), (5, 2, *early, 1), (6, 1, *early1, 1)]
+    cargo = Cargo(
+        4, [stack, g3, g2, g1], stacked + [(1, None), (2, None), (3, None)], [acts, None], jobs, dims
+    )
+    in0_keep, in0_send, g0, small0, dgain_mix0, acts, dxs = mixer_backward(
+        0, x0, None, g1, stash0, masks, init, *back_mixer, True, cargo
+    )
+    jobs = [(3, 0, 0, seq, 0), (0, 3, *late, 0), (1, 2, *late, 0), (2, 1, *late1, 0)]
+    cargo = Cargo(5, [g3, g2, g1, g0], None, [dxs], jobs, dims)
+    dxs, mlp0, mix0 = finish(cargo, (up0_keep, in0_keep), (up0_send, in0_send), dp, width)
+    activations = lax.dynamic_update_index_in_dim(acts, own(stack, 0), section, 0)[None]
+    own_dx = jnp.where(section < 2, jnp.where(section == 0, g0, g1), jnp.where(section == 2, g2, g3))
+    input_grads = lax.dynamic_update_index_in_dim(dxs, own_dx, section, 0)[None]
+    parts = (sum_rest([mlp0], dp, width), sum_rest([mix0], dp, width), [mlp1], [mix1])
+    joined = [jnp.concatenate([add_up(part) for part in parts], axis=1).astype(BF16)]
+    total = sum_section(joined, sections)
+    sizes = [part[0].shape[1] for part in parts]
+    mlp0, mix0, mlp1, mix1 = jnp.split(total, [sum(sizes[:k]) for k in range(1, 4)], axis=1)
 
     devices = dp * sections
     mix_small = jnp.stack([small0, small1])
@@ -878,11 +1022,17 @@
         jnp.stack([dbu0[0], dbu1[0]]),
         mix_small[:, :5].reshape(10, -1),
     ]
+    final = jnp.concatenate([final0, final1]).reshape(2, sections, -1).transpose(1, 0, 2)
+    final = jnp.tile(final.reshape(sections, -1), (dp, 1))
     packed = jnp.concatenate(
-        [a.reshape(a.shape[0], devices, -1).transpose(1, 0, 2).reshape(devices, -1) for a in lines],
+        [a.reshape(a.shape[0], devices, -1).transpose(1, 0, 2).reshape(devices, -1) for a in lines]
+        + [final],
         axis=1,
     )
-    summed = sum_small(packed, dp, sections)
+    arrived = lax.all_to_all(packed, ("dp", "section"), split_axis=0, concat_axis=0, tiled=True)
+    near = lax.dynamic_slice_in_dim(arrived, lax.axis_index("dp") * sections, sections, 0)
+    final_states = near[:, -final.shape[1] :].reshape(sections, 2, -1).transpose(1, 0, 2)
+    summed = jnp.sum(arrived[:, : -final.shape[1]], axis=0)
     pieces, at = [], 0
     for a in lines:
         size = a.size // devices
@@ -891,17 +1041,16 @@
     mix_gain_grad, mlp_gain_grad, down_bias_grad, up_bias_grad, conv = pieces
     conv = conv.reshape(2, 5, -1)
 
-    mix_big = jnp.stack([mix0, mix1])
-    mlp_big = jnp.stack([mlp0, mlp1])
-    share = mix_big.shape[2]
+    share = width // devices
+    mix_big = jnp.stack([mix0, mix1]).reshape(2, share, count, 3 * tile)
     mix_in_grad = (
-        mix_big[..., : 2 * tile].reshape(2, count, share, 2, tile).transpose(0, 2, 3, 1, 4)
+        mix_big[..., : 2 * tile].reshape(2, share, count, 2, tile).transpose(0, 1, 3, 2, 4)
         .reshape(2, share, -1)
     )
-    mix_out_grad = mix_big[..., 2 * tile :].transpose(0, 1, 3, 2).reshape(2, -1, share)
-    wide = mlp_big.shape[3] // 2
-    mlp_up_grad = mlp_big[..., :wide].transpose(0, 2, 1, 3).reshape(2, share, -1)
-    mlp_down_grad = mlp_big[..., wide:].transpose(0, 1, 3, 2).reshape(2, -1, share)
+    mix_out_grad = mix_big[..., 2 * tile :].reshape(2, share, -1).transpose(0, 2, 1)
+    mlp_big = jnp.stack([mlp0, mlp1]).reshape(2, share, -1, 2, TILE_F)
+    mlp_up_grad = mlp_big[:, :, :, 0].reshape(2, share, -1)
+    mlp_down_grad = mlp_big[:, :, :, 1].reshape(2, share, -1).transpose(0, 2, 1)
     return (
         activations, input_grads, final_states, mix_gain_grad, mix_in_grad, conv[:, :4], conv[:, 4],
         mix_out_grad, mlp_gain_grad, mlp_up_grad, up_bias_grad, mlp_down_grad, down_bias_grad,

time: 622 us -> 382 us (0.61)
  starting transfers between devices: 169 us -> 8 us
  waiting for transfers between devices: 139 us -> 27.7 us
  Pallas kernels: 233 us -> 283 us
  other arithmetic: 27 us -> 8.23 us
  local copies, waits for them, and re-layouts: 51.4 us -> 33.7 us
  between operations: 1.97 us -> 14.7 us
    ppermute x42 -> x3, starting transfers between devices: 162 us -> 4.39 us  [permute(): return lax.ppermute(x, axis, pairs)]
    ppermute x42 -> x3, waiting for transfers between devices: 136 us -> 27 us  [permute(): return lax.ppermute(x, axis, pairs)]
    pallas_call x10 -> x9, Pallas kernels: 233 us -> 283 us  [the longest x4 145 us: call(): pl.pallas_call(carrying, grid=grid, in_specs=list(in_specs) + [ANYWHERE]...]
    dynamic_slice x6 -> x1, local copies, waits for them, and re-layouts: 10 us -> 0.01 us  [body(): lax.dynamic_slice_in_dim(arrived, lax.axis_index('dp') * sections, sectio...]
    select_n x4 -> x0, other arithmetic: 8.5 us -> none  [the longest x2 4.28 us: send_low(): two = jnp.where(odd, second, first)]
    convert_element_type x29 -> x0, other arithmetic: 6.76 us -> none  [part(): return functools.reduce(jnp.add, pieces).astype(addends[0].dtype)]
  transfers between devices with their start and end apart: 43 -> 6, of which waited for: 16 -> 2; matrix products, arithmetic and copies ran while one was open for 10% -> 3% of each run, Pallas kernels for 31% -> 39%
where the time goes in v2:
time: 382 us; the launch traced here: 375 us
  Pallas kernels  283 us (74%)
  local copies, waits for them, and re-layouts  33.7 us (9%)
  waiting for transfers between devices  27.7 us (7%)
  between operations  14.7 us (4%)
  other arithmetic  8.23 us (2%)
  starting transfers between devices  8 us (2%)
    pallas_call x4, Pallas kernels, call(): pl.pallas_call(carrying, grid=grid, in_specs=list(in_specs) + [ANYWHERE]...  145 us
    pallas_call x1, Pallas kernels, finish(): pl.pallas_call(functools.partial(last_kernel, cargo.jobs, first_step(dp,...  74 us
    pallas_call x2, Pallas kernels, mixer_forward(): pl.pallas_call(mixer_forward_kernel, grid=(count,), in_specs=[source_spec...  42.8 us
    ppermute x3, waiting for transfers between devices, permute(): return lax.ppermute(x, axis, pairs)  27 us
    pallas_call x2, Pallas kernels, mlp_forward(): pl.pallas_call(mlp_forward_kernel, grid=(inner // tile,), in_specs=[sourc...  21 us
  transfers between devices with their start and end apart: 6, of which 2 were waited for; matrix products, arithmetic and copies ran while one was open for 3% of the time, Pallas kernels for 39%

profile of v2, /device:TPU:0, one launch (start us, length us, event | category | flops | bytes accessed | tf_op | source)
XLA Modules:
  0.0 374.9 jit_solution(8324010575646934240)
XLA Ops:
  7.2 0.7 subtract_convert_fusion
  8.0 0.8 maximum_multiply_fusion
  9.2 0.6 constant_dynamic-slice_fusion.1.init_ref.refs_9_
  9.8 2.3 dynamic-slice_bitcast_fusion.1.x_ref.refs_0_
  12.1 1.3 broadcast_in_dim.36.gain_ref.refs_2_
  13.4 1.3 broadcast_in_dim.37.bg_ref.bc_ref
  14.7 1.3 broadcast_in_dim.40.gain_ref.refs_2_
  16.0 1.3 broadcast_in_dim.41.bu_ref
  17.3 1.3 broadcast_in_dim.42.bd_ref
  18.6 1.7 broadcast_in_dim.39.mask_ref.refs_8_
  20.3 21.4 %mixer_forward.2 = (bf16[4,1024,512]{2,1,0:T(8,128)(2,1)}, bf16[4,1024,512]{2,1,0:T(8,128)(2,1)}, bf16[1024,1024]{1,0:T(8,128)(2,1)}, bf16[1024,1024]{1,0:T(8,12...) custom-call(bf16[1024,512]{1,0:T(8,128)(2,1)} %dynamic-slice_bitcast_fusion.1.x_ref.refs_0_, ...), custom_call_target="tpu_custom_call" | custom-call | flops 16499999744 | bytes 4194304 | tf_op jit(solution)/shard_map/mixer_forward/pallas_call | solution.py:653
  41.7 10.5 %mlp_forward.2 = (bf16[4,1024,512]{2,1,0:T(8,128)(2,1)}, bf16[1024,2048]{1,0:T(8,128)(2,1)}) custom-call(bf16[4,1024,512]{2,1,0:T(8,128)(2,1)} %get-tuple-element.57.x_ref, f32[2,1,512]{2,1,0:T(1,128)} %broadcast_in_dim.40.gain_ref.refs_2_, bf16[2,512,2048]{2,1,0:T(8,128)(2,1)} %refs_3_.6, ...), custom_call_target="tpu_custom_call", output_to_operand_aliasing={{0}: (0, {})} | custom-call | flops 11000000512 | bytes 4194304 | tf_op jit(solution)/shard_map/mlp_forward/pallas_call | solution.py:728
  52.2 21.4 %mixer_forward.3 = (bf16[4,1024,512]{2,1,0:T(8,128)(2,1)}, bf16[4,1024,512]{2,1,0:T(8,128)(2,1)}, bf16[1024,1024]{1,0:T(8,128)(2,1)}, bf16[1024,1024]{1,0:T(8,12...) custom-call(bf16[4,1024,512]{2,1,0:T(8,128)(2,1)} %get-tuple-element.58.x_ref, ...), custom_call_target="tpu_custom_call", output_to_operand_aliasing={{0}: (0, {})} | custom-call | flops 16499999744 | bytes 4194304 | tf_op jit(solution)/shard_map/mixer_forward/pallas_call | solution.py:653
  73.7 10.5 %mlp_forward.3 = (bf16[4,1024,512]{2,1,0:T(8,128)(2,1)}, bf16[1024,2048]{1,0:T(8,128)(2,1)}) custom-call(bf16[4,1024,512]{2,1,0:T(8,128)(2,1)} %get-tuple-element.59.x_ref, f32[2,1,512]{2,1,0:T(1,128)} %broadcast_in_dim.40.gain_ref.refs_2_, bf16[2,512,2048]{2,1,0:T(8,128)(2,1)} %refs_3_.6, ...), custom_call_target="tpu_custom_call", output_to_operand_aliasing={{0}: (0, {})} | custom-call | flops 11000000512 | bytes 4194304 | tf_op jit(solution)/shard_map/mlp_forward/pallas_call | solution.py:728
  84.2 2.3 dynamic-slice_bitcast_fusion.refs_1_
  86.4 28.3 %mlp_backward.2 = (bf16[512,4096]{1,0:T(8,128)(2,1)}, bf16[1024,512]{1,0:T(8,128)(2,1)}, f32[1,2048]{1,0:T(1,128)}, f32[1,512]{1,0:T(1,128)}, f32[1,512]{1,0:T(1,128)}, /*index=5*/bf16[4,1024,512]{2,1,0:T(8,128)(2,1)}) custom-call(bf16[4,1024,512]{2,1,0:T(8,128)(2,1)} %get-tuple-element.60.refs_0_.refs_7_.refs_15_, ...), custom_call_target="tpu_custom_call" | custom-call | flops 22000001024 | bytes 4194304 | tf_op jit(solution)/shard_map/mlp_backward/pallas_call | solution.py:597
  114.7 45.8 %mixer_backward.2 = (bf16[512,3072]{1,0:T(8,128)(2,1)}, bf16[1024,512]{1,0:T(8,128)(2,1)}, f32[4,8,512]{2,1,0:T(8,128)}, f32[1,512]{1,0:T(1,128)}, bf16[4,1024,512]{2,1,0:T(8,128)(2,1)}) custom-call(bf16[4,1024,512]{2,1,0:T(8,128)(2,1)} %get-tuple-element.60.refs_0_.refs_7_.refs_15_, ...), custom_call_target="tpu_custom_call", output_to_operand_aliasing={{4}: (16, {})} | custom-call | flops 32999999488 | bytes 4194304 | tf_op jit(solution)/shard_map/mixer_backward/pallas_call | solution.py:597
  160.6 0.7 reduce-scatter.3.cloned.1.call-update
  161.3 25.9 %mlp_backward.3 = (bf16[256,4096]{1,0:T(8,128)(2,1)}, bf16[256,4096]{1,0:T(8,128)(2,1)}, bf16[1024,512]{1,0:T(8,128)(2,1)}, f32[1,2048]{1,0:T(1,128)}, f32[1,512...) custom-call(bf16[4,1024,512]{2,1,0:T(8,128)(2,1)} %get-tuple-element.60.refs_0_.r, ...), custom_call_target="tpu_custom_call", output_to_operand_aliasing={{6}: (8, {})} | custom-call | flops 22000001024 | bytes 4194304 | tf_op jit(solution)/shard_map/mlp_backward/pallas_call | solution.py:597
  187.3 44.8 %mixer_backward.3 = (bf16[256,3072]{1,0:T(8,128)(2,1)}, bf16[256,3072]{1,0:T(8,128)(2,1)}, bf16[1024,512]{1,0:T(8,128)(2,1)}, f32[4,8,512]{2,1,0:T(8,128)}, f32[...) custom-call(bf16[1024,512]{1,0:T(8,128)(2,1)} %dynamic-slice_bitcast, ...), custom_call_target="tpu_custom_call", output_to_operand_aliasing={{5}: (19, {})} | custom-call | flops 32999999488 | bytes 4194304 | tf_op jit(solution)/shard_map/mixer_backward/pallas_call | solution.py:597
  232.1 0.9 copy.72
  234.2 0.7 pad_maximum_fusion.3
  235.4 0.9 copy.78
  236.2 3.5 all-to-all-start
  239.9 74.0 %finish.1 = (bf16[4,1024,512]{2,1,0:T(8,128)(2,1)}, bf16[64,4096]{1,0:T(8,128)(2,1)}, bf16[64,3072]{1,0:T(8,128)(2,1)}) custom-call(bf16[1024,512]{1,0:T(8,128)(2,1)} %get-tuple-element.62.refs_1_.refs_16_.refs_0_, bf16[1024,512]{1,0:T(8,128)(2,1)} %get-tuple-element.68.refs_1_.refs_17_, ...), custom_call_target="tpu_custom_call", output_to_operand_aliasing={{0}: (8, {})} | custom-call | tf_op jit(solution)/shard_map/finish/pallas_call | solution.py:878
  313.9 3.2 bitcast_dynamic-update-slice_fusion
  317.2 1.3 pad_maximum_fusion
  318.5 1.0 dynamic-slice_bitcast_fusion.4
  319.5 1.8 collective-permute-start
  321.3 2.6 collective-permute-start.2
  324.1 0.6 slice.107
  324.7 0.6 slice.108
  325.4 0.6 reshape.176
  326.0 0.6 reshape.180
  326.7 0.6 reshape.182
  327.3 0.6 reshape.181
  328.0 0.7 slice.104
  328.6 11.7 %collective-permute-done = bf16[16,14336]{1,0:T(8,128)(2,1)S(1)} collective-permute-done((bf16[16,14336]{1,0:T(8,128)(2,1)}, bf16[16,14336]{1,0:T(8,128)(2,1)S(1)}, u32[]{:S(2)}, u32[]{:S(2)}) %collective-permute-start) | collective-permute-done | bytes 458784 | tf_op jit(solution)/shard_map/ppermute | solution.py:797
  340.3 15.3 %collective-permute-done.1 = bf16[16,14336]{1,0:T(8,128)(2,1)} collective-permute-done((bf16[16,14336]{1,0:T(8,128)(2,1)}, bf16[16,14336]{1,0:T(8,128)(2,1)}, u32[]{:S(2)}, u32[]{:S(2)}) %collective-permute-start.1) | collective-permute-done | bytes 458784 | tf_op jit(solution)/shard_map/ppermute | solution.py:797
  355.6 1.4 fusion.1
  357.4 0.2 stack.65
  357.7 0.2 stack.66
  358.0 0.9 reshape_squeeze.7
  358.9 0.9 reshape_squeeze.6
  359.8 0.8 reshape.178
  360.7 0.7 reshape.179
  361.4 4.6 %copy.105 = bf16[1,4,1024,512]{3,2,1,0:T(8,128)(2,1)} copy(bf16[1,4,1024,512]{3,2,1,0:T(8,128)(2,1)} %get-tuple-element.130) | data formatting | bytes 8388608
  366.0 2.0 copy.106
  (96 shorter events, 3.0 us)
Async XLA Ops:
  7.2 2.0 copy-start
  7.2 309.9 %reduce-scatter.5.cloned.1.call-start = ((), (), s32[]{:S(2)}) async-start(), calls=%async_computation.4 | async-start | bytes 3538944 | tf_op jit(solution)/shard_map/reduce_scatter | solution.py:989
  160.6 156.6 %reduce-scatter.3.cloned.1.call-start = ((), (), s32[]{:S(2)}) async-start(), calls=%async_computation.3 | async-start | bytes 4718592 | tf_op jit(solution)/shard_map/reduce_scatter | solution.py:984
  187.2 45.8 %copy-start.9 = (f32[4,8,512]{2,1,0:T(8,128)S(1)}, f32[4,8,512]{2,1,0:T(8,128)}, u32[]{:S(2)}) copy-start(f32[4,8,512]{2,1,0:T(8,128)} %get-tuple-element.94) | copy-start | bytes 196612
  187.2 46.2 %copy-start.10 = (f32[1,2048]{1,0:T(1,128)S(1)}, f32[1,2048]{1,0:T(1,128)}, u32[]{:S(2)}) copy-start(f32[1,2048]{1,0:T(1,128)} %get-tuple-element.92) | copy-start | bytes 24580
  187.2 46.2 %copy-start.11 = (f32[1,2048]{1,0:T(1,128)S(1)}, f32[1,2048]{1,0:T(1,128)}, u32[]{:S(2)}) copy-start(f32[1,2048]{1,0:T(1,128)} %get-tuple-element.91) | copy-start | bytes 24580
  187.2 46.5 %copy-start.15 = (f32[1,512]{1,0:T(1,128)S(1)}, f32[1,512]{1,0:T(1,128)}, u32[]{:S(2)}) copy-start(f32[1,512]{1,0:T(1,128)} %get-tuple-element.90) | copy-start | bytes 6148
  187.3 46.5 %copy-start.16 = (f32[1,512]{1,0:T(1,128)S(1)}, f32[1,512]{1,0:T(1,128)}, u32[]{:S(2)}) copy-start(f32[1,512]{1,0:T(1,128)} %get-tuple-element.88) | copy-start | bytes 6148
  187.3 46.5 %copy-start.17 = (f32[1,512]{1,0:T(1,128)S(1)}, f32[1,512]{1,0:T(1,128)}, u32[]{:S(2)}) copy-start(f32[1,512]{1,0:T(1,128)} %get-tuple-element.89) | copy-start | bytes 6148
  187.3 46.5 %copy-start.18 = (f32[1,512]{1,0:T(1,128)S(1)}, f32[1,512]{1,0:T(1,128)}, u32[]{:S(2)}) copy-start(f32[1,512]{1,0:T(1,128)} %get-tuple-element.87) | copy-start | bytes 6148
  187.3 46.9 %copy-start.14 = (f32[1,512]{1,0:T(1,128)S(1)}, f32[1,512]{1,0:T(1,128)}, u32[]{:S(2)}) copy-start(f32[1,512]{1,0:T(1,128)} %get-tuple-element.86) | copy-start | bytes 6148
  187.3 47.8 %copy-start.12 = (f32[1,1024]{1,0:T(1,128)S(1)}, f32[1,1024]{1,0:T(1,128)}, u32[]{:S(2)}) copy-start(f32[1,1024]{1,0:T(1,128)} %get-tuple-element.95) | copy-start | bytes 12292
  187.3 47.8 %copy-start.13 = (f32[1,1024]{1,0:T(1,128)S(1)}, f32[1,1024]{1,0:T(1,128)}, u32[]{:S(2)}) copy-start(f32[1,1024]{1,0:T(1,128)} %get-tuple-element.96) | copy-start | bytes 12292
  236.2 80.9 %all-to-all-start = ((f32[32,1,1376]{2,1,0:T(1,128)}), f32[32,1,1376]{2,1,0:T(1,128)S(1)}, u32[]{:S(2)}, u32[]{:S(2)}) async-start(f32[32,1,1376]{2,1,0:T(1,128)} %copy.78), calls=%async_computation | async-start | bytes 360448 | tf_op jit(solution)/shard_map/all_to_all | solution.py:1032
  239.8 74.0 %copy-start.3 = (bf16[1024,512]{1,0:T(8,128)(2,1)S(1)}, bf16[1024,512]{1,0:T(8,128)(2,1)}, u32[]{:S(2)}) copy-start(bf16[1024,512]{1,0:T(8,128)(2,1)} %get-tuple-element.62.refs_1_.refs_16_.refs_0_) | copy-start | bytes 3145732
  239.8 74.0 %copy-start.4 = (bf16[1024,512]{1,0:T(8,128)(2,1)S(1)}, bf16[1024,512]{1,0:T(8,128)(2,1)}, u32[]{:S(2)}) copy-start(bf16[1024,512]{1,0:T(8,128)(2,1)} %get-tuple-element.68.refs_1_.refs_17_) | copy-start | bytes 3145732
  239.8 74.0 %copy-start.5 = (bf16[1024,512]{1,0:T(8,128)(2,1)S(1)}, bf16[1024,512]{1,0:T(8,128)(2,1)}, u32[]{:S(2)}) copy-start(bf16[1024,512]{1,0:T(8,128)(2,1)} %get-tuple-element.71.refs_1_.refs_18_.refs_2_) | copy-start | bytes 3145732
  239.8 74.0 %copy-start.6 = (bf16[1024,512]{1,0:T(8,128)(2,1)S(1)}, bf16[1024,512]{1,0:T(8,128)(2,1)}, u32[]{:S(2)}) copy-start(bf16[1024,512]{1,0:T(8,128)(2,1)} %get-tuple-element.78.refs_3_) | copy-start | bytes 3145732
  313.8 3.3 copy-start.7
  313.9 3.3 copy-start.8
  319.5 20.8 %collective-permute-start = (bf16[16,14336]{1,0:T(8,128)(2,1)}, bf16[16,14336]{1,0:T(8,128)(2,1)S(1)}, u32[]{:S(2)}, u32[]{:S(2)}) collective-permute-start(bf16[16,14336]{1,0:T(8,128)(2,1)} %get-tuple-element.101), channel_id=1, source_target_pairs={{0,1},{1,0},{2,3},{3,2},{4,5},{5,4},{6,7},{7,6},{8,9},{9,8},{10,11... | collective-permute-start | bytes 1376264 | tf_op jit(solution)/shard_map/ppermute | solution.py:797
  321.3 34.3 %collective-permute-start.1 = (bf16[16,14336]{1,0:T(8,128)(2,1)}, bf16[16,14336]{1,0:T(8,128)(2,1)}, u32[]{:S(2)}, u32[]{:S(2)}) collective-permute-start(bf16[16,14336]{1,0:T(8,128)(2,1)} %get-tuple-element.103), channel_id=1, source_target_pairs={{0,2},{1,3},{2,0},{3,1},{4,6},{5,7},{6,4},{7,5},{8,10},{9,11},{10,... | collective-permute-start | bytes 1376264 | tf_op jit(solution)/shard_map/ppermute | solution.py:797
  321.3 34.3 %collective-permute-start.2 = (bf16[16,14336]{1,0:T(8,128)(2,1)S(1)}, bf16[16,14336]{1,0:T(8,128)(2,1)}, u32[]{:S(2)}, u32[]{:S(2)}) collective-permute-start(bf16[16,14336]{1,0:T(8,128)(2,1)S(1)} %get-tuple-element.102), channel_id=1, source_target_pairs={{0,3},{1,2},{2,1},{3,0},{4,7},{5,6},{6,5},{7,4},{8,11},{9,10},{10,... | collective-permute-start | bytes 1376264 | tf_op jit(solution)/shard_map/ppermute | solution.py:797
  361.4 4.6 %copy-start.2 = (bf16[1,4,1024,512]{3,2,1,0:T(8,128)(2,1)S(1)}, bf16[1,4,1024,512]{3,2,1,0:T(8,128)(2,1)}, u32[]{:S(2)}) copy-start(bf16[1,4,1024,512]{3,2,1,0:T(8,128)(2,1)} %get-tuple-element.131) | copy-start | bytes 12582916
  361.4 6.7 %copy-start.1 = (f32[2,4,1024]{2,1,0:T(4,128)S(1)}, f32[2,4,1024]{2,1,0:T(4,128)}, u32[]{:S(2)}) copy-start(f32[2,4,1024]{2,1,0:T(4,128)} %param.16) | copy-start | bytes 98308
Sparse Core Ops, SparseCore 0:
  160.7 46.4 reduce-scatter.4
  210.9 71.1 reduce-scatter.2

commit v3 on v2

--- a/solution.py
+++ b/solution.py
@@ -10,7 +10,7 @@
 EPSILON = 1e-06
 LANES = 128
 GROUP = 8
-TILE_C = 256
+TILE_C = 512
 TILE_F = 512
 BIG = 1024
 F32 = jnp.float32
@@ -40,13 +40,18 @@
 
     def at(index, carry):
         for tile in range(natural.shape[0]):
-            first = natural[tile, pl.ds(2 * index, GROUP, stride=stride), :]
-            second = natural[tile, pl.ds(2 * index + 1, GROUP, stride=stride), :]
-            both = jnp.concatenate([first, second], axis=0).astype(BF16)
-            target[pl.ds(pl.multiple_of(index * 16, 16), 16), pl.ds(tile * LANES, LANES)] = both
+            block = jnp.stack(
+                [
+                    natural[tile, pl.ds(pl.multiple_of(s * stride + index * GROUP, GROUP), GROUP), :]
+                    for s in range(GROUP)
+                ]
+            )
+            rows = pl.ds(pl.multiple_of(index * GROUP * GROUP, GROUP * GROUP), GROUP * GROUP)
+            mixed = jnp.swapaxes(block, 0, 1).reshape(GROUP * GROUP, LANES)
+            target[rows, pl.ds(tile * LANES, LANES)] = mixed.astype(BF16)
         return carry
 
-    lax.fori_loop(0, stride // 2, at, 0)
+    lax.fori_loop(0, stride // GROUP, at, 0)
 
 
 def to_tokens(chunked, natural):
@@ -54,11 +59,15 @@
 
     def at(index, carry):
         for tile in range(natural.shape[0]):
-            rows = pl.ds(pl.multiple_of(index * GROUP, GROUP), GROUP)
-            natural[tile, pl.ds(index, GROUP, stride=stride), :] = chunked[rows, pl.ds(tile * LANES, LANES)]
+            rows = pl.ds(pl.multiple_of(index * GROUP * GROUP, GROUP * GROUP), GROUP * GROUP)
+            block = chunked[rows, pl.ds(tile * LANES, LANES)].reshape(GROUP, GROUP, LANES)
+            mixed = jnp.swapaxes(block, 0, 1)
+            for s in range(GROUP):
+                to = pl.ds(pl.multiple_of(s * stride + index * GROUP, GROUP), GROUP)
+                natural[tile, to, :] = mixed[s]
         return carry
 
-    lax.fori_loop(0, stride, at, 0)
+    lax.fori_loop(0, stride // GROUP, at, 0)
 
 
 def transpose_into(source, target):
@@ -83,10 +92,10 @@
     return jnp.concatenate([natural[tile, rows, :] for tile in range(natural.shape[0])], axis=1)
 
 
-def norm_into(x_ref, gain_ref, target):
+def norm_into(x_ref, gain, target):
     def at(rows):
         source = x_ref[rows, :].astype(F32)
-        result = source * inverse_rms(source) * gain_ref[...]
+        result = source * inverse_rms(source) * gain
         if len(target.shape) == 3:
             put_tiles(target, rows, result)
         else:
@@ -121,9 +130,9 @@
 
 
 def mixer_forward_kernel(
-    x_ref, gain_ref, wg_ref, wc_ref, kg_ref, kc_ref, bg_ref, bc_ref, wo_ref, mask_ref, init_ref,
+    layer, begin, x_ref, gain_ref, wg_ref, wc_ref, kg_ref, kc_ref, bg_ref, bc_ref, wo_ref, keep_ref, init_ref,
     y_ref, p_ref, z_ref, cand_ref, h_ref, final_ref,
-    normed, natural, total, proj, local, decay,
+    normed, natural, total, proj, local, decay, mask_ref,
 ):
     step = pl.program_id(0)
     seq = x_ref.shape[0]
@@ -131,7 +140,9 @@
 
     @pl.when(step == 0)
     def _():
-        norm_into(x_ref, gain_ref, natural)
+        windows_into(keep_ref, mask_ref)
+        begin()
+        norm_into(x_ref, gain_ref[layer : layer + 1, :], natural)
         to_chunks(natural, normed)
         total[...] = jnp.zeros_like(total)
 
@@ -160,7 +171,7 @@
             lanes = pl.ds(tile * LANES, LANES)
 
             def convolve(shift, taps, bias):
-                value = bias[0:1, lanes]
+                value = bias[layer : layer + 1, lanes]
                 for k in range(4):
                     at = pl.ds(pl.multiple_of(base + HALO - GROUP * k, GROUP), STEP)
                     term = proj[at, pl.ds(shift + tile * LANES, LANES)]
@@ -194,7 +205,7 @@
     entries = []
     for tile, (state, product) in enumerate(ends):
         lanes = pl.ds(tile * LANES, LANES)
-        current = init_ref[0:1, lanes]
+        current = init_ref[layer : layer + 1, lanes]
         starts = []
         for g in range(GROUP):
             starts.append(current)
@@ -225,8 +236,7 @@
         rows_loop(seq, 128, finish)
 
 
-def norm_backward(x_ref, g_ref, gain_ref, grad_normed, dx_ref, dgain_ref):
-    gain = gain_ref[...]
+def norm_backward(x_ref, g_ref, gain, grad_normed, dx_ref, dgain_ref):
 
     def at(index, carry):
         rows = pl.ds(pl.multiple_of(index * 64, 64), 64)
@@ -257,11 +267,11 @@
 
 
 def mixer_backward_kernel(
-    x_ref, g_ref, gain_ref, wg_ref, wc_ref, kg_ref, kc_ref, wo_ref, mask_ref, init_ref,
+    layer, begin, x_ref, g_ref, gain_ref, wg_ref, wc_ref, kg_ref, kc_ref, wo_ref, keep_ref, init_ref,
     p_ref, z_ref, cand_ref, h_ref, bit_ref, *rest,
 ):
-    *dw, dx_ref, small_ref, dgain_ref = rest[:-9]
-    (normed_t, upstream, upstream_t, natural, total, local, decay, dconv, dproj) = rest[-9:]
+    *dw, dx_ref, small_ref, dgain_ref = rest[:-10]
+    (normed_t, upstream, upstream_t, natural, total, local, decay, dconv, dproj, mask_ref) = rest[-10:]
     step = pl.program_id(0)
     seq = x_ref.shape[0]
     width = wg_ref.shape[1]
@@ -269,7 +279,9 @@
 
     @pl.when(step == 0)
     def _():
-        norm_into(x_ref, gain_ref, natural)
+        windows_into(keep_ref, mask_ref)
+        begin()
+        norm_into(x_ref, gain_ref[layer : layer + 1, :], natural)
         to_chunks(natural, upstream)
         transpose_into(upstream, normed_t)
 
@@ -321,7 +333,7 @@
         entries.append(jnp.concatenate(starts[::-1], axis=0))
 
     last_rows = h_ref[pl.ds(seq - 16, 16), :].astype(F32)[GROUP:]
-    before = previous_chunk(last_rows, init_ref[0:1, :])
+    before = previous_chunk(last_rows, init_ref[layer : layer + 1, :])
 
     def gates(index, carry):
         base = pl.multiple_of(index * STEP, STEP)
@@ -401,26 +413,27 @@
     @pl.when(step == pl.num_programs(0) - 1)
     def _():
         to_tokens(total, natural)
-        norm_backward(x_ref, g_ref, gain_ref, natural, dx_ref, dgain_ref)
+        norm_backward(x_ref, g_ref, gain_ref[layer : layer + 1, :], natural, dx_ref, dgain_ref)
 
 
 def mlp_forward_kernel(
-    x_ref, gain_ref, wu_ref, bu_ref, wd_ref, bd_ref, y_ref, u_ref, normed, total
+    layer, begin, x_ref, gain_ref, wu_ref, bu_ref, wd_ref, bd_ref, y_ref, u_ref, normed, total
 ):
     step = pl.program_id(0)
     seq = x_ref.shape[0]
 
     @pl.when(step == 0)
     def _():
-        norm_into(x_ref, gain_ref, normed)
+        begin()
+        norm_into(x_ref, gain_ref[layer : layer + 1, :], normed)
 
         def start(rows):
-            total[rows, :] = x_ref[rows, :].astype(F32) + bd_ref[...]
+            total[rows, :] = x_ref[rows, :].astype(F32) + bd_ref[layer : layer + 1, :]
 
         rows_loop(seq, 128, start)
 
     def at(rows):
-        pre = dot_nn(normed[rows, :], wu_ref[...]) + bu_ref[...]
+        pre = dot_nn(normed[rows, :], wu_ref[...]) + bu_ref[layer : layer + 1, :]
         u_ref[rows, :] = pre.astype(BF16)
         inner = ROOT_2_PI * (pre + CUBIC * (pre * pre * pre))
         active = (0.5 * pre * (1.0 + jnp.tanh(inner))).astype(BF16)
@@ -436,8 +449,18 @@
         rows_loop(seq, 128, finish)
 
 
+def gelu_parts(pre):
+    square = pre * pre
+    bent = jnp.tanh(pre * (ROOT_2_PI + (ROOT_2_PI * CUBIC) * square))
+    half = 0.5 * pre
+    slope = 0.5 + 0.5 * bent + half * (1.0 - bent * bent) * (
+        ROOT_2_PI + (3.0 * ROOT_2_PI * CUBIC) * square
+    )
+    return (half + half * bent).astype(BF16), slope
+
+
 def mlp_backward_kernel(
-    x_ref, g_ref, gain_ref, wu_ref, wd_ref, u_ref, bit_ref, *rest,
+    layer, begin, x_ref, g_ref, gain_ref, wu_ref, wd_ref, u_ref, bit_ref, *rest,
 ):
     *dw, dx_ref, dbu_ref, dbd_ref, dgain_ref = rest[:-5]
     normed_t, upstream_t, total, active, dpre = rest[-5:]
@@ -447,7 +470,8 @@
 
     @pl.when(step == 0)
     def _():
-        norm_into(x_ref, gain_ref, active)
+        begin()
+        norm_into(x_ref, gain_ref[layer : layer + 1, :], active)
         transpose_into(active, normed_t)
         transpose_into(g_ref, upstream_t)
 
@@ -461,13 +485,7 @@
     def at(index, carry):
         rows = pl.ds(pl.multiple_of(index * BIG, BIG), BIG)
         pre = u_ref[rows, :].astype(F32)
-        square = pre * pre
-        bent = jnp.tanh(pre * (ROOT_2_PI + (ROOT_2_PI * CUBIC) * square))
-        half = 0.5 * pre
-        active[rows, :] = (half + half * bent).astype(BF16)
-        slope = 0.5 + 0.5 * bent + half * (1.0 - bent * bent) * (
-            ROOT_2_PI + (3.0 * ROOT_2_PI * CUBIC) * square
-        )
+        active[rows, :], slope = gelu_parts(pre)
         low = (dot_nt(g_ref[rows, :], wd_ref[...]) * slope).astype(BF16)
         dpre[rows, :] = low
         total[rows, :] += dot_nt(low, wu_ref[...])
@@ -480,7 +498,7 @@
 
     @pl.when(step == pl.num_programs(0) - 1)
     def _():
-        norm_backward(x_ref, g_ref, gain_ref, total, dx_ref, dgain_ref)
+        norm_backward(x_ref, g_ref, gain_ref[layer : layer + 1, :], total, dx_ref, dgain_ref)
 
 
 def shape(dims, kind):
@@ -496,25 +514,27 @@
 ANYWHERE = pl.BlockSpec(memory_space=pl.ANY)
 MESH = pl.DeviceIdType.MESH
 SECTIONS = 4
-
-
-def meet_sections(section):
+FAR = 2
+
+
+def greet_sections(section):
     barrier = pltpu.get_barrier_semaphore()
     for by in range(1, SECTIONS):
         other = (section + by) % SECTIONS
         pl.semaphore_signal(barrier, inc=1, device_id={"section": other}, device_id_type=MESH)
-    pl.semaphore_wait(barrier, SECTIONS - 1)
 
 
 def delivery(jobs, sources, buffers, send_sems, recv_sems):
     section = lax.axis_index("section")
 
+    def sends(job):
+        return functools.reduce(jnp.logical_or, [section == sender for sender in job[5]])
+
     def copy(number, sender):
-        source, part, first, count, buffer = jobs[number]
+        source, part, first, count, buffer, _ = jobs[number]
         rows = pl.ds(first, count)
         return pltpu.make_async_remote_copy(
-            src_ref=sources[source][0].at[sources[source][1], rows] if sources[source][1] is not None
-            else sources[source][0].at[rows],
+            src_ref=sources[source].at[rows],
             dst_ref=buffers[buffer].at[sender, rows],
             send_sem=send_sems.at[number],
             recv_sem=recv_sems.at[number, sender],
@@ -522,34 +542,36 @@
             device_id_type=MESH,
         )
 
-    def start():
-        for number, job in enumerate(jobs):
-
-            @pl.when(section != job[1])
+    def start(first=0, last=len(jobs)):
+        for number, job in list(enumerate(jobs))[first:last]:
+
+            @pl.when(sends(job))
             def _(number=number):
                 copy(number, section).start()
 
     def wait():
         for number, job in enumerate(jobs):
 
-            @pl.when(section != job[1])
+            @pl.when(sends(job))
             def _(number=number):
                 copy(number, section).wait_send()
 
             @pl.when(section == job[1])
             def _(number=number, job=job):
-                for sender in range(SECTIONS):
-                    if sender != job[1]:
-                        copy(number, sender).wait_recv()
+                for sender in job[5]:
+                    copy(number, sender).wait_recv()
 
     return start, wait
 
 
+def after(value, *others):
+    return lax.optimization_barrier((value,) + others)
+
+
 class Cargo:
-    def __init__(self, collective_id, arrays, sources, buffers, jobs, dims):
+    def __init__(self, collective_id, arrays, buffers, jobs, dims):
         self.collective_id = collective_id
         self.arrays = list(arrays)
-        self.sources = sources
         self.old = [b for b in buffers if b is not None]
         self.buffers = buffers
         self.jobs = jobs
@@ -560,7 +582,7 @@
     aliases = dict(aliases or {})
     if cargo is None:
         return pl.pallas_call(
-            kernel, grid=grid, in_specs=in_specs, out_specs=out_specs, out_shape=out_shape,
+            functools.partial(kernel, lambda: None), grid=grid, in_specs=in_specs, out_specs=out_specs, out_shape=out_shape,
             scratch_shapes=scratch_shapes, compiler_params=PARAMS, cost_estimate=cost_estimate, name=name,
             input_output_aliases=aliases,
         )(*args)
@@ -573,16 +595,18 @@
         outs, refs = refs[:n_out], refs[n_out:]
         buffers, refs = refs[:n_buffer], refs[n_buffer:]
         own, (send_sems, recv_sems) = refs[:-2], refs[-2:]
-        sources = [(arrays[a], at) for a, at in cargo.sources]
-        start, wait = delivery(cargo.jobs, sources, buffers, send_sems, recv_sems)
+        start, wait = delivery(cargo.jobs, arrays, buffers, send_sems, recv_sems)
         step = pl.program_id(0)
 
         @pl.when(step == 0)
         def _():
-            meet_sections(lax.axis_index("section"))
+            greet_sections(lax.axis_index("section"))
+
+        def begin():
+            pl.semaphore_wait(pltpu.get_barrier_semaphore(), SECTIONS - 1)
             start()
 
-        kernel(*ins, *outs, *own)
+        kernel(begin, *ins, *outs, *own)
 
         @pl.when(step == pl.num_programs(0) - 1)
         def _():
@@ -599,7 +623,7 @@
         grid=grid,
         in_specs=list(in_specs) + [ANYWHERE] * (n_array + n_old),
         out_specs=list(out_specs) + [ANYWHERE] * n_buffer,
-        out_shape=list(out_shape) + [shape(cargo.dims, BF16)] * n_buffer,
+        out_shape=list(out_shape) + (cargo.dims if isinstance(cargo.dims, list) else [shape(cargo.dims, BF16)] * n_buffer),
         scratch_shapes=list(scratch_shapes)
         + [pltpu.SemaphoreType.DMA((jobs,)), pltpu.SemaphoreType.DMA((jobs, SECTIONS))],
         compiler_params=pltpu.CompilerParams(
@@ -622,12 +646,6 @@
     return pl.BlockSpec(dims, lambda i: (0,) * len(dims))
 
 
-def source_spec(stack, at):
-    if at is None:
-        return whole(stack.shape)
-    return pl.BlockSpec((None,) + stack.shape[1:], lambda i: (at, 0, 0))
-
-
 def mixer_specs(layer, width, hidden, tile):
     count = hidden // tile
     return dict(
@@ -635,45 +653,46 @@
         cand=pl.BlockSpec((None, width, tile), lambda i: (layer, 0, count + i)),
         tap_gate=pl.BlockSpec((None, 4, tile), lambda i: (layer, 0, i)),
         tap_cand=pl.BlockSpec((None, 4, tile), lambda i: (layer, 0, count + i)),
-        bias_gate=pl.BlockSpec((None, 1, tile), lambda i: (layer, 0, i)),
-        bias_cand=pl.BlockSpec((None, 1, tile), lambda i: (layer, 0, count + i)),
+        bias_gate=pl.BlockSpec((2, tile), lambda i: (0, i)),
+        bias_cand=pl.BlockSpec((2, tile), lambda i: (0, count + i)),
         out=pl.BlockSpec((None, tile, width), lambda i: (layer, i, 0)),
-        gain=pl.BlockSpec((None, 1, width), lambda i: (layer, 0, 0)),
-        init=pl.BlockSpec((None, 1, tile), lambda i: (layer, 0, i)),
-    )
-
-
-def mixer_forward(layer, stack, at, masks, init, gain, weight_in, taps, bias, weight_out):
-    seq, width = stack.shape[-2:]
-    hidden = init.shape[2]
+        gain=whole((2, width)),
+        init=pl.BlockSpec((2, tile), lambda i: (0, i)),
+    )
+
+
+def mixer_forward(layer, x, masks, init, gain, weight_in, taps, bias, weight_out, cargo=None):
+    seq, width = x.shape
+    hidden = init.shape[1]
     tile = TILE_C
     count = hidden // tile
     spec = mixer_specs(layer, width, hidden, tile)
     column = pl.BlockSpec((seq, tile), lambda i: (0, i))
-    return pl.pallas_call(
-        mixer_forward_kernel,
+    return call(
+        functools.partial(mixer_forward_kernel, layer),
+        cargo,
         grid=(count,),
         in_specs=[
-            source_spec(stack, at), spec["gain"], spec["gate"], spec["cand"], spec["tap_gate"], spec["tap_cand"],
+            whole(x.shape), spec["gain"], spec["gate"], spec["cand"], spec["tap_gate"], spec["tap_cand"],
             spec["bias_gate"], spec["bias_cand"], spec["out"], whole(masks.shape), spec["init"],
         ],
         out_specs=[
-            pl.BlockSpec((None, seq, width), lambda i: (2 * layer, 0, 0)), pl.BlockSpec((1, seq, 2 * tile), lambda i: (i, 0, 0)), column, column, column,
+            whole(x.shape), pl.BlockSpec((1, seq, 2 * tile), lambda i: (i, 0, 0)), column, column, column,
             pl.BlockSpec((1, tile), lambda i: (0, i)),
         ],
         out_shape=[
-            shape((4, seq, width), BF16), shape((count, seq, 2 * tile), BF16), shape((seq, hidden), BF16),
+            shape(x.shape, BF16), shape((count, seq, 2 * tile), BF16), shape((seq, hidden), BF16),
             shape((seq, hidden), BF16), shape((seq, hidden), BF16), shape((1, hidden), F32),
         ],
         scratch_shapes=[
             pltpu.VMEM((seq, width), BF16), pltpu.VMEM((width // LANES, seq, LANES), F32), pltpu.VMEM((seq, width), F32),
             pltpu.VMEM((seq + HALO, 2 * tile), F32), pltpu.VMEM((seq, tile), F32), pltpu.VMEM((seq, tile), F32),
+            pltpu.VMEM((3, seq + HALO, LANES), F32),
         ],
-        compiler_params=PARAMS,
         cost_estimate=cost(seq, 15),
-        input_output_aliases={} if at is None else {0: 0},
         name="mixer_forward",
-    )(stack, gain, weight_in, weight_in, taps, taps, bias, bias, weight_out, masks, init)
+        args=(x, gain, weight_in, weight_in, taps, taps, bias, bias, weight_out, masks, init),
+    )
 
 
 def grad_outputs(width, tile, total, split):
@@ -685,20 +704,20 @@
     )
 
 
-def mixer_backward(layer, stack, at, g, stash, masks, init, gain, weight_in, taps, weight_out, bit, split, cargo):
+def mixer_backward(layer, x, g, stash, masks, init, gain, weight_in, taps, weight_out, bit, split, cargo=None):
     seq, width = g.shape
-    hidden = init.shape[2]
+    hidden = init.shape[1]
     tile = TILE_C
     count = hidden // tile
     spec = mixer_specs(layer, width, hidden, tile)
     column = pl.BlockSpec((seq, tile), lambda i: (0, i))
     dw_specs, dw_shapes = grad_outputs(width, 3 * tile, 3 * hidden, split)
     return call(
-        mixer_backward_kernel,
+        functools.partial(mixer_backward_kernel, layer),
         cargo,
         grid=(count,),
         in_specs=[
-            source_spec(stack, at), whole(g.shape), spec["gain"], spec["gate"], spec["cand"], spec["tap_gate"],
+            whole(x.shape), whole(g.shape), spec["gain"], spec["gate"], spec["cand"], spec["tap_gate"],
             spec["tap_cand"], spec["out"], whole(masks.shape), spec["init"],
             pl.BlockSpec((1, seq, 2 * tile), lambda i: (i, 0, 0)), column, column, column, SCALAR,
         ],
@@ -713,52 +732,49 @@
             pltpu.VMEM((width, seq), BF16), pltpu.VMEM((seq, width), BF16), pltpu.VMEM((width, seq), BF16),
             pltpu.VMEM((width // LANES, seq, LANES), F32), pltpu.VMEM((seq, width), F32), pltpu.VMEM((seq, tile), F32),
             pltpu.VMEM((seq, tile), F32), pltpu.VMEM((seq + HALO, 2 * tile), F32),
-            pltpu.VMEM((seq, 2 * tile), BF16),
+            pltpu.VMEM((seq, 2 * tile), BF16), pltpu.VMEM((3, seq + HALO, LANES), F32),
         ],
         cost_estimate=cost(seq, 30),
         name="mixer_backward",
-        args=(stack, g, gain, weight_in, weight_in, taps, taps, weight_out, masks, init, *stash, bit),
-    )
-
-
-def mlp_forward(layer, stack, at, gain, weight_up, bias_up, weight_down, bias_down):
-    seq, width = stack.shape[-2:]
+        args=(x, g, gain, weight_in, weight_in, taps, taps, weight_out, masks, init, *stash, bit),
+    )
+
+
+def mlp_forward(layer, x, gain, weight_up, bias_up, weight_down, bias_down, cargo=None):
+    seq, width = x.shape
     inner = weight_up.shape[2]
     tile = TILE_F
-    return pl.pallas_call(
-        mlp_forward_kernel,
+    return call(
+        functools.partial(mlp_forward_kernel, layer),
+        cargo,
         grid=(inner // tile,),
         in_specs=[
-            source_spec(stack, at), pl.BlockSpec((None, 1, width), lambda i: (layer, 0, 0)),
+            whole(x.shape), whole(gain.shape),
             pl.BlockSpec((None, width, tile), lambda i: (layer, 0, i)),
-            pl.BlockSpec((None, 1, tile), lambda i: (layer, 0, i)),
+            pl.BlockSpec((2, tile), lambda i: (0, i)),
             pl.BlockSpec((None, tile, width), lambda i: (layer, i, 0)),
-            pl.BlockSpec((None, 1, width), lambda i: (layer, 0, 0)),
+            whole(bias_down.shape),
         ],
-        out_specs=[
-            pl.BlockSpec((None, seq, width), lambda i: (2 * layer + 1, 0, 0)),
-            pl.BlockSpec((seq, tile), lambda i: (0, i)),
-        ],
-        out_shape=[shape(stack.shape, BF16), shape((seq, inner), BF16)],
+        out_specs=[whole(x.shape), pl.BlockSpec((seq, tile), lambda i: (0, i))],
+        out_shape=[shape(x.shape, BF16), shape((seq, inner), BF16)],
         scratch_shapes=[pltpu.VMEM((seq, width), BF16), pltpu.VMEM((seq, width), F32)],
-        compiler_params=PARAMS,
         cost_estimate=cost(seq, 10),
-        input_output_aliases={0: 0},
         name="mlp_forward",
-    )(stack, gain, weight_up, bias_up, weight_down, bias_down)
-
-
-def mlp_backward(layer, stack, at, g, pre, gain, weight_up, weight_down, bit, split, cargo):
+        args=(x, gain, weight_up, bias_up, weight_down, bias_down),
+    )
+
+
+def mlp_backward(layer, x, g, pre, gain, weight_up, weight_down, bit, split, cargo=None):
     seq, width = g.shape
     inner = weight_up.shape[2]
     tile = TILE_F
     dw_specs, dw_shapes = grad_outputs(width, 2 * tile, 2 * inner, split)
     return call(
-        mlp_backward_kernel,
+        functools.partial(mlp_backward_kernel, layer),
         cargo,
         grid=(inner // tile,),
         in_specs=[
-            source_spec(stack, at), whole(g.shape), pl.BlockSpec((None, 1, width), lambda i: (layer, 0, 0)),
+            whole(x.shape), whole(g.shape), whole(gain.shape),
             pl.BlockSpec((None, width, tile), lambda i: (layer, 0, i)),
             pl.BlockSpec((None, tile, width), lambda i: (layer, i, 0)),
             pl.BlockSpec((seq, tile), lambda i: (0, i)), SCALAR,
@@ -776,41 +792,59 @@
         ],
         cost_estimate=cost(seq, 20),
         name="mlp_backward",
-        args=(stack, g, gain, weight_up, weight_down, pre, bit),
+        args=(x, g, gain, weight_up, weight_down, pre, bit),
     )
 
 
 def chunk_masks(resets):
     seq = resets.shape[0]
-    keep = (1 - resets).astype(F32)
-    windows = [keep]
-    for k in (1, 2):
-        windows.append(windows[-1] * jnp.concatenate([jnp.ones((k,), F32), keep[:-k]]))
-    stacked = jnp.stack(windows)
-    cut = stacked.reshape(3, GROUP, seq // GROUP).transpose(0, 2, 1)
-    ahead = jnp.concatenate([cut[:, :4, 1:], jnp.zeros((3, 4, 1), F32)], axis=2)
-    rows = jnp.concatenate([cut, ahead], axis=1).reshape(3, seq + 4 * GROUP, 1)
-    return jnp.broadcast_to(rows, (3, seq + 4 * GROUP, LANES))
+    cut = (1 - resets).astype(F32).reshape(GROUP, seq // GROUP).T
+    ends = jnp.zeros((3, 1), F32)
+    before = jnp.concatenate([ends, cut[-3:, :-1]], axis=1)
+    ahead = jnp.concatenate([cut[:3, 1:], ends], axis=1)
+    rows = jnp.concatenate([before, cut, ahead]).reshape(seq + 2 * HALO, 1)
+    return jnp.broadcast_to(rows, (seq + 2 * HALO, LANES))
+
+
+def windows_into(keep_ref, mask_ref):
+    count = mask_ref.shape[1]
+    first = keep_ref[pl.ds(HALO, count), :]
+    second = first * keep_ref[pl.ds(HALO - GROUP, count), :]
+    mask_ref[0] = first
+    mask_ref[1] = second
+    mask_ref[2] = second * keep_ref[pl.ds(HALO - 2 * GROUP, count), :]
 
 
 def permute(x, axis, pairs):
     return lax.ppermute(x, axis, pairs)
 
 
-def last_kernel(jobs, split, dp, n_array, *refs):
+def last_kernel(jobs, split, dp, inner, n_array, *refs):
     arrays, refs = refs[:n_array], refs[n_array:]
-    (keeps, sends), refs = (refs[0:2], refs[2:4]), refs[5:]
-    buffer, outs, refs = refs[0], refs[1:3], refs[3:]
-    kept, got, parts, landed, sums = refs[0:2], refs[2:4], refs[4:6], refs[6:8], refs[8:10]
-    send_sems, recv_sems, local_sems, core_sems, part_sems = refs[10:]
+    keeps, sends, refs = refs[0:3], refs[3:6], refs[6:]
+    if inner:
+        later, refs = refs[0:2], refs[2:]
+    cotangent, wu_any, wd_any, gain_ref, bu_ref, bd_ref, refs = *refs[:6], refs[6:]
+    buffers, refs = refs[2:4], refs[4:]
+    acts, dxs = buffers
+    outs, refs = (refs[:5], refs[5:]) if inner else (refs[:3], refs[3:])
+    wu, wd, x_own, g_own, normed, total, grad, y_own, d_own, dgain, redo_sems = refs[-11:]
+    refs = refs[:-11]
+    kept, got, parts, landed, refs = refs[0:3], refs[3:6], refs[6:9], refs[9:12], refs[12:]
+    if inner:
+        level, first, second, third, refs = refs[0:5], refs[5:10], refs[10:15], refs[15:20], refs[20:]
+        z_sems, refs = refs[0], refs[1:]
+    else:
+        sums, refs = refs[0:3], refs[3:]
+    send_sems, recv_sems, local_sems, core_sems, part_sems = refs
     section = lax.axis_index("section")
     where = lax.axis_index("dp")
     bit = (where // split) % 2
     partner = where + split * (1 - 2 * bit)
-    top = dp // 4 if split * 4 < dp else 0
     steps = [step for step in bits_of(dp) if step != split][-2:]
     low_bit, high_bit = (where // steps[0]) % 2, (where // steps[1]) % 2
     mine = low_bit + 2 * high_bit
+    near_bit, far_bit = section % 2, section // 2
 
     def flipped(mask):
         low, high = mask % 2, mask // 2
@@ -818,6 +852,23 @@
         new_high = high_bit + high * (1 - 2 * high_bit)
         device = where + steps[0] * (new_low - low_bit) + steps[1] * (new_high - high_bit)
         return new_low + 2 * new_high, device
+
+    def near_copy(n):
+        return pltpu.make_async_remote_copy(
+            src_ref=level[n].at[:, 1 - near_bit], dst_ref=first[n], send_sem=z_sems.at[0, n], recv_sem=z_sems.at[1, n],
+            device_id={"section": section + 1 - 2 * near_bit}, device_id_type=MESH,
+        )
+
+    def far_copy(n):
+        return pltpu.make_async_remote_copy(
+            src_ref=second[n].at[1 - far_bit], dst_ref=third[n], send_sem=z_sems.at[2, n], recv_sem=z_sems.at[3, n],
+            device_id={"section": section + 2 - 4 * far_bit}, device_id_type=MESH,
+        )
+
+    def near_sum(n):
+        for half in range(2):
+            both = level[n][half, near_bit].astype(F32) + first[n][half].astype(F32)
+            second[n][half] = both.astype(second[n].dtype)
 
     barrier = pltpu.get_barrier_semaphore()
     for by in range(1, SECTIONS):
@@ -826,30 +877,96 @@
     pl.semaphore_signal(barrier, inc=1, device_id={"dp": partner}, device_id_type=MESH)
     for mask in (1, 2, 3):
         pl.semaphore_signal(barrier, inc=1, device_id={"dp": flipped(mask)[1]}, device_id_type=MESH)
+    loads = [pltpu.make_async_copy(keeps[n], kept[n], local_sems.at[n]) for n in range(3)]
+    if inner:
+        loads += [pltpu.make_async_copy(later[n], level[3 + n], local_sems.at[3 + n]) for n in range(2)]
+    for load in loads:
+        load.start()
     pl.semaphore_wait(barrier, SECTIONS + 3)
 
-    start, wait = delivery(jobs, [(a, None) for a in arrays], [buffer], send_sems, recv_sems)
-    swaps, loads = [], []
-    for n in range(2):
+    start, wait = delivery(jobs, arrays, buffers, send_sems, recv_sems)
+    redoes = section == SECTIONS - 1
+
+    def fetch(row):
+        return (
+            pltpu.make_async_copy(acts.at[row], x_own, redo_sems.at[0]),
+            pltpu.make_async_copy(cotangent.at[row], g_own, redo_sems.at[1]),
+        )
+
+    def fetch_weights():
+        return (
+            pltpu.make_async_copy(wu_any.at[1], wu, redo_sems.at[2]),
+            pltpu.make_async_copy(wd_any.at[1], wd, redo_sems.at[3]),
+        )
+
+    def put(row):
+        return (
+            pltpu.make_async_copy(y_own, acts.at[row], redo_sems.at[4]),
+            pltpu.make_async_copy(d_own, dxs.at[row], redo_sems.at[5]),
+        )
+
+    @pl.when(redoes)
+    def _():
+        for one in fetch(0) + fetch_weights():
+            one.start()
+
+    def redo(row):
+        for one in fetch(row) + (fetch_weights() if row == 0 else put(row - 1)):
+            one.wait()
+        gain = gain_ref[1:2, :]
+        norm_into(x_own, gain, normed)
+
+        def begin_total(rows):
+            total[rows, :] = x_own[rows, :].astype(F32) + bd_ref[1:2, :]
+
+        rows_loop(total.shape[0], 128, begin_total)
+        grad[...] = jnp.zeros_like(grad)
+
+        def tile(index, carry):
+            cut = pl.ds(pl.multiple_of(index * TILE_F, TILE_F), TILE_F)
+            up, down = wu[:, cut], wd[cut, :]
+            pre = dot_nn(normed[...], up) + bu_ref[1:2, cut]
+            active, slope = gelu_parts(pre)
+            total[...] += dot_nn(active, down)
+            low = (dot_nt(g_own[...], down) * slope).astype(BF16)
+            grad[...] += dot_nt(low, up)
+            return carry
+
+        lax.fori_loop(0, wu.shape[1] // TILE_F, tile, 0)
+
+        def end_total(rows):
+            y_own[rows, :] = total[rows, :].astype(BF16)
+
+        rows_loop(total.shape[0], 128, end_total)
+        norm_backward(x_own, g_own, gain, grad, d_own, dgain)
+        for one in put(row) + (fetch(row + 1) if row + 1 < FAR else ()):
+            one.start()
+
+    swaps = []
+    for n in range(3):
         swap = pltpu.make_async_remote_copy(
             src_ref=sends[n], dst_ref=got[n], send_sem=core_sems.at[0, n], recv_sem=core_sems.at[1, n],
             device_id={"dp": partner}, device_id_type=MESH,
         )
         swap.start()
-        load = pltpu.make_async_copy(keeps[n], kept[n], local_sems.at[n])
-        load.start()
         swaps.append(swap)
-        loads.append(load)
-    start()
+    start(0, -1)
+    for load in loads:
+        load.wait()
+    near = {}
+    if inner:
+        for n in (3, 4):
+            near[n] = near_copy(n)
+            near[n].start()
     moves = []
-    for n in range(2):
-        loads[n].wait()
+    for n in range(3):
         swaps[n].wait()
         rows = kept[n].shape[0] // 4
         for mask in (1, 2, 3):
             quarter, device = flipped(mask)
             taken = pl.ds(pl.multiple_of(quarter * rows, rows), rows)
-            parts[n][mask - 1] = (kept[n][taken, :].astype(F32) + got[n][taken, :].astype(F32)).astype(BF16)
+            pair = kept[n][taken, :].astype(F32) + got[n][taken, :].astype(F32)
+            parts[n][mask - 1] = pair.astype(parts[n].dtype)
             move = pltpu.make_async_remote_copy(
                 src_ref=parts[n].at[mask - 1], dst_ref=landed[n].at[mask - 1],
                 send_sem=part_sems.at[0, n, mask - 1], recv_sem=part_sems.at[1, n, mask - 1],
@@ -857,42 +974,110 @@
             )
             move.start()
             moves.append(move)
-    for n in range(2):
+    pl.when(redoes)(functools.partial(redo, 0))
+    for n in range(3):
         rows = kept[n].shape[0] // 4
         taken = pl.ds(pl.multiple_of(mine * rows, rows), rows)
-        total = kept[n][taken, :].astype(F32) + got[n][taken, :].astype(F32)
+        summed = kept[n][taken, :].astype(F32) + got[n][taken, :].astype(F32)
         for mask in (1, 2, 3):
             moves[3 * n + mask - 1].wait()
-            total = total + landed[n][mask - 1].astype(F32)
-        sums[n][...] = total.astype(BF16)
-        store = pltpu.make_async_copy(sums[n], outs[n], local_sems.at[n])
-        store.start()
-        store.wait()
+            summed = summed + landed[n][mask - 1].astype(F32)
+        if inner:
+            share = rows // SECTIONS
+            for part in range(SECTIONS):
+                level[n][part // 2, part % 2] = summed[part * share : (part + 1) * share].astype(level[n].dtype)
+            near[n] = near_copy(n)
+            near[n].start()
+        else:
+            sums[n][...] = summed.astype(sums[n].dtype)
+            store = pltpu.make_async_copy(sums[n], outs[n], local_sems.at[n])
+            store.start()
+            store.wait()
+    if not inner:
+        start(len(jobs) - 1)
+    pl.when(redoes)(functools.partial(redo, 1))
+    if inner:
+        far = {}
+        for n in (3, 4, 0, 1, 2):
+            near[n].wait()
+            near_sum(n)
+            far[n] = far_copy(n)
+            far[n].start()
+        start(len(jobs) - 1)
+        for n in (3, 4, 0, 1, 2):
+            far[n].wait()
+            block = n // 3
+            final = second[n][far_bit].astype(F32) + third[n][...].astype(F32)
+            if n == 2:
+                outs[4][...] = final
+            elif n in (1, 4):
+                cand = outs[0].shape[2] // 2
+                for at in range(0, final.shape[1], 3 * TILE_C):
+                    to = at // 3
+                    outs[0][block, :, pl.ds(to, TILE_C)] = final[:, at : at + TILE_C]
+                    outs[0][block, :, pl.ds(cand + to, TILE_C)] = final[:, at + TILE_C : at + 2 * TILE_C]
+                    outs[1][block, :, pl.ds(to, TILE_C)] = final[:, at + 2 * TILE_C : at + 3 * TILE_C]
+            else:
+                for at in range(0, final.shape[1], 2 * TILE_F):
+                    outs[2][block, :, pl.ds(at // 2, TILE_F)] = final[:, at : at + TILE_F]
+                    outs[3][block, :, pl.ds(at // 2, TILE_F)] = final[:, at + TILE_F : at + 2 * TILE_F]
+
+    @pl.when(redoes)
+    def _():
+        for one in put(1):
+            one.wait()
+
     wait()
 
 
-def finish(cargo, keeps, sends, dp, width):
-    quarters = [(k.shape[0] // 4, k.shape[1]) for k in keeps]
+def finish(cargo, keeps, sends, later, redo, dp, width):
+    inner = later is not None
+    columns = [k.shape[1] for k in keeps]
+    kinds = [k.dtype for k in keeps]
+    rows = keeps[0].shape[0] // 4
+    share = rows // SECTIONS
     n_array = len(cargo.arrays)
     jobs = len(cargo.jobs)
+    lots = list(zip(columns + columns[:2], kinds + kinds[:2]))
+    if inner:
+        later = [a.reshape(2, 2, share, -1) for a in later]
+        wide = columns[1] // 3
+        outs = [shape((2, share, c), F32) for c in (2 * wide, wide, columns[0] // 2, columns[0] // 2)]
+        outs += [shape((share, columns[2]), F32)]
+        out_specs = [pl.BlockSpec(memory_space=pltpu.VMEM)] * 5
+        extra = [pltpu.VMEM((2, 2, share, c), kind) for c, kind in lots]
+        extra += [pltpu.VMEM((2, share, c), kind) for c, kind in lots] * 2
+        extra += [pltpu.VMEM((share, c), kind) for c, kind in lots]
+        extra += [pltpu.SemaphoreType.DMA((4, 5))]
+    else:
+        later = []
+        outs = [shape((rows, c), kind) for c, kind in zip(columns, kinds)]
+        out_specs = [ANYWHERE] * 3
+        extra = [pltpu.VMEM((rows, c), kind) for c, kind in zip(columns, kinds)]
+    n_in = n_array + 6 + len(later)
     return pl.pallas_call(
-        functools.partial(last_kernel, cargo.jobs, first_step(dp, width), dp, n_array),
-        in_specs=[ANYWHERE] * (n_array + 5),
-        out_specs=[ANYWHERE] * 3,
-        out_shape=[shape(cargo.dims, BF16)] + [shape(q, BF16) for q in quarters],
-        scratch_shapes=[pltpu.VMEM(k.shape, BF16) for k in keeps] * 2
-        + [pltpu.VMEM((3,) + q, BF16) for q in quarters] * 2
-        + [pltpu.VMEM(q, BF16) for q in quarters]
+        functools.partial(last_kernel, cargo.jobs, first_step(dp, width), dp, inner, n_array),
+        in_specs=[ANYWHERE] * (n_in + 3) + [pl.BlockSpec(memory_space=pltpu.VMEM)] * 3 + [ANYWHERE] * 2,
+        out_specs=[ANYWHERE] * 2 + out_specs,
+        out_shape=[shape(cargo.dims, BF16)] * 2 + outs,
+        scratch_shapes=[pltpu.VMEM(k.shape, k.dtype) for k in keeps] * 2
+        + [pltpu.VMEM((3, rows, c), kind) for c, kind in zip(columns, kinds)] * 2
+        + extra
         + [
             pltpu.SemaphoreType.DMA((jobs,)), pltpu.SemaphoreType.DMA((jobs, SECTIONS)),
-            pltpu.SemaphoreType.DMA((2,)), pltpu.SemaphoreType.DMA((2, 2)), pltpu.SemaphoreType.DMA((2, 2, 3)),
-        ],
+            pltpu.SemaphoreType.DMA((5,)), pltpu.SemaphoreType.DMA((2, 3)), pltpu.SemaphoreType.DMA((2, 3, 3)),
+        ]
+        + [pltpu.VMEM(redo[1].shape[1:], BF16), pltpu.VMEM(redo[2].shape[1:], BF16)]
+        + [pltpu.VMEM(cargo.dims[1:], BF16)] * 3 + [pltpu.VMEM(cargo.dims[1:], F32)] * 2
+        + [pltpu.VMEM(cargo.dims[1:], BF16)] * 2
+        + [pltpu.VMEM((1, width), F32), pltpu.SemaphoreType.DMA((6,))],
         compiler_params=pltpu.CompilerParams(
             vmem_limit_bytes=56 * 1024 * 1024, collective_id=cargo.collective_id, has_side_effects=True
         ),
-        input_output_aliases={n_array + 4: 0},
+        input_output_aliases={n_in + 6: 0, n_in + 7: 1},
+        cost_estimate=cost(1024, 100),
         name="finish",
-    )(*cargo.arrays, *keeps, *sends, cargo.old[0])
+    )(*cargo.arrays, *keeps, *sends, *later, *redo, *cargo.old)
 
 
 def add_up(pieces):
@@ -906,7 +1091,7 @@
 
     def part(which):
         taken = [lax.dynamic_index_in_dim(b, which, 0, keepdims=False) for b in blocks]
-        return add_up(taken).astype(BF16)
+        return add_up(taken).astype(addends[0].dtype)
 
     result = [part(own)]
     for mask in range(1, 1 << len(steps)):
@@ -951,66 +1136,65 @@
     x0 = own(tokens, 0)
     g4 = own(cotangent, 0)
     masks = chunk_masks(own(resets, 0))
-    init = own(init_states, 1)[:, None, :]
-    mix_gain = mix_gain[:, None, :]
-    mlp_gain = mlp_gain[:, None, :]
-    conv_bias = conv_bias[:, None, :]
-    up_bias = up_bias[:, None, :]
-    down_bias = down_bias[:, None, :]
+    init = own(init_states, 1)
     mixer_weights = (mix_gain, mix_in, conv_weight, conv_bias, mix_out)
     mlp_weights = (mlp_gain, mlp_up, up_bias, mlp_down, down_bias)
-
-    stack, *stash0, final0 = mixer_forward(0, x0, None, masks, init, *mixer_weights)
-    stack, pre0 = mlp_forward(0, stack, 0, *mlp_weights)
-    stack, *stash1, final1 = mixer_forward(1, stack, 1, masks, init, *mixer_weights)
-    stack, pre1 = mlp_forward(1, stack, 2, *mlp_weights)
-
     seq = tokens.shape[1]
     dims = (sections, seq, width)
-    stacked = [(0, part) for part in range(4)]
-
-    def cuts(*shares):
-        edges = [seq * share // 16 for share in shares]
-        return [(a, b - a) for a, b in zip(edges, edges[1:])]
-
-    def every(span, buffer=0):
-        return [(part, part, *span, buffer) for part in range(4)]
-
-    spans = cuts(0, 4, 10, 14, 16)
+    sent = {}
+
+    def some(source, part, share, buffer=0, senders=None):
+        if senders is None:
+            senders = tuple(k for k in range(sections) if k != part)
+        kind = (buffer, part, senders)
+        first = sent.get(kind, 0)
+        sent[kind] = first + share
+        return (source, part, seq * first // 32, seq * share // 32, buffer, senders)
+
+    distant, close = tuple(range(FAR)), tuple(range(FAR, sections - 1))
+
+    x1, *stash0, final0 = mixer_forward(0, x0, masks, init, *mixer_weights)
+    x2, pre0 = mlp_forward(0, x1, *mlp_weights)
+    cargo = Cargo(1, [x1, x2], [None], [some(0, 0, 5), some(1, 1, 5)], dims)
+    x3, *stash1, final1, acts = mixer_forward(1, x2, masks, init, *mixer_weights, cargo)
+    cargo = Cargo(2, [x1, x2, x3], [acts], [some(0, 0, 2), some(1, 1, 2), some(2, 2, 6)], dims)
+    x4, pre1, acts = mlp_forward(1, x3, *mlp_weights, cargo)
+
     back_mixer = (mix_gain, mix_in, conv_weight, mix_out, bit)
     back_mlp = (mlp_gain, mlp_up, mlp_down, bit)
-    cargo = Cargo(1, [stack], stacked, [None], every(spans[0]), dims)
-    up1, g3, dbu1, dbd1, dgain_mlp1, acts = mlp_backward(1, stack, 2, g4, pre1, *back_mlp, False, cargo)
+    xs = [x1, x2, x3, x4]
+    jobs = [some(0, 0, 7), some(1, 1, 7), some(2, 2, 7), some(2, 3, 7, 0, distant), some(3, 3, 7, 0, close)]
+    quarters = jnp.concatenate([final0, final1, jnp.zeros((GROUP - 2, final0.shape[1]), F32)])
+    quarters = jnp.split(quarters, sections, axis=1)
+    jobs += [some(4 + part, part, 32, 2)[:2] + (0, GROUP, 1) + some(4 + part, part, 32, 3)[5:] for part in range(sections)]
+    shapes = [shape(dims, BF16), shape((sections,) + quarters[0].shape, F32)]
+    up1, g3, dbu1, dbd1, dgain_mlp1, acts, ends = mlp_backward(
+        1, x3, g4, pre1, *back_mlp, False, Cargo(3, xs + quarters, [acts, None], jobs, shapes)
+    )
+    here = lax.broadcasted_iota(jnp.int32, (sections, 1, 1), 0) == section
+    ends = jnp.where(here, lax.dynamic_index_in_dim(jnp.stack(quarters), section, 0), ends)
+    final_states = ends[:, :2].transpose(1, 0, 2)
     mlp1 = lax.psum_scatter(up1, "dp", scatter_dimension=0, tiled=True)
-    cargo = Cargo(2, [stack], stacked, [acts], every(spans[1]), dims)
+    jobs = [some(0, 0, 9), some(1, 1, 9), some(2, 2, 9), some(2, 3, 9, 0, distant), some(3, 3, 9, 0, close)]
     in1, g2, small1, dgain_mix1, acts = mixer_backward(
-        1, stack, 1, g3, stash1, masks, init, *back_mixer, False, cargo
+        1, x2, g3, stash1, masks, init, *back_mixer, False, Cargo(4, xs, [acts], jobs, dims)
     )
     mix1 = lax.psum_scatter(in1, "dp", scatter_dimension=0, tiled=True)
-    cargo = Cargo(3, [stack], stacked, [acts], every(spans[2]), dims)
+    jobs = [some(0, 0, 7), some(1, 1, 7), some(2, 2, 7), some(2, 3, 7, 0, distant), some(3, 3, 8, 0, close)]
     up0_keep, up0_send, g1, dbu0, dbd0, dgain_mlp0, acts = mlp_backward(
-        0, stack, 0, g2, pre0, *back_mlp, True, cargo
-    )
-    (early, late), (early1, late1) = cuts(0, 4, 16), cuts(0, 8, 16)
-    jobs = every(spans[3]) + [(4, 3, *early, 1), (5, 2, *early, 1), (6, 1, *early1, 1)]
-    cargo = Cargo(
-        4, [stack, g3, g2, g1], stacked + [(1, None), (2, None), (3, None)], [acts, None], jobs, dims
-    )
+        0, x1, g2, pre0, *back_mlp, True, Cargo(5, xs, [acts], jobs, dims)
+    )
+    jobs = [some(0, 0, 2), some(1, 1, 2), some(2, 2, 3), some(2, 3, 9, 0, distant), some(3, 3, 8, 0, close)]
+    jobs += [some(4, 3, 16, 1, close), some(5, 2, 6, 1), some(6, 1, 14, 1)]
+    cargo = Cargo(6, xs + [g3, g2, g1], [acts, None], jobs, dims)
+    g1, mlp1 = after(g1, mlp1)
     in0_keep, in0_send, g0, small0, dgain_mix0, acts, dxs = mixer_backward(
-        0, x0, None, g1, stash0, masks, init, *back_mixer, True, cargo
-    )
-    jobs = [(3, 0, 0, seq, 0), (0, 3, *late, 0), (1, 2, *late, 0), (2, 1, *late1, 0)]
-    cargo = Cargo(5, [g3, g2, g1, g0], None, [dxs], jobs, dims)
-    dxs, mlp0, mix0 = finish(cargo, (up0_keep, in0_keep), (up0_send, in0_send), dp, width)
-    activations = lax.dynamic_update_index_in_dim(acts, own(stack, 0), section, 0)[None]
-    own_dx = jnp.where(section < 2, jnp.where(section == 0, g0, g1), jnp.where(section == 2, g2, g3))
-    input_grads = lax.dynamic_update_index_in_dim(dxs, own_dx, section, 0)[None]
-    parts = (sum_rest([mlp0], dp, width), sum_rest([mix0], dp, width), [mlp1], [mix1])
-    joined = [jnp.concatenate([add_up(part) for part in parts], axis=1).astype(BF16)]
-    total = sum_section(joined, sections)
-    sizes = [part[0].shape[1] for part in parts]
-    mlp0, mix0, mlp1, mix1 = jnp.split(total, [sum(sizes[:k]) for k in range(1, 4)], axis=1)
-
+        0, x0, g1, stash0, masks, init, *back_mixer, True, cargo
+    )
+    jobs = [some(3, 0, 32, 1, (2, 3)), some(3, 0, 16, 1, (1,)), some(2, 1, 18, 1), some(0, 3, 16, 1, close), some(1, 2, 26, 1)]
+    jobs += [some(3, 0, 16, 1, (1,))]
+    cargo = Cargo(7, [g3, g2, g1, g0], [acts, dxs], jobs, dims)
+    redo = (cotangent, mlp_up, mlp_down, mlp_gain, up_bias, down_bias)
     devices = dp * sections
     mix_small = jnp.stack([small0, small1])
     count, tile = mix_small.shape[1], mix_small.shape[3] // 2
@@ -1022,17 +1206,48 @@
         jnp.stack([dbu0[0], dbu1[0]]),
         mix_small[:, :5].reshape(10, -1),
     ]
-    final = jnp.concatenate([final0, final1]).reshape(2, sections, -1).transpose(1, 0, 2)
-    final = jnp.tile(final.reshape(sections, -1), (dp, 1))
     packed = jnp.concatenate(
-        [a.reshape(a.shape[0], devices, -1).transpose(1, 0, 2).reshape(devices, -1) for a in lines]
-        + [final],
-        axis=1,
-    )
-    arrived = lax.all_to_all(packed, ("dp", "section"), split_axis=0, concat_axis=0, tiled=True)
-    near = lax.dynamic_slice_in_dim(arrived, lax.axis_index("dp") * sections, sections, 0)
-    final_states = near[:, -final.shape[1] :].reshape(sections, 2, -1).transpose(1, 0, 2)
-    summed = jnp.sum(arrived[:, : -final.shape[1]], axis=0)
+        [a.reshape(a.shape[0], devices, -1).transpose(1, 0, 2).reshape(devices, -1) for a in lines], axis=1
+    )
+    share = width // devices
+    length = packed.shape[1]
+    packed = jnp.pad(packed, ((0, 0), (0, share * LANES - length))).reshape(-1, 2, SPLIT, LANES)
+
+    def half(which):
+        return lax.dynamic_index_in_dim(packed, which, 1, keepdims=False).reshape(-1, LANES)
+
+    halves = ((up0_keep, in0_keep, half(bit[0])), (up0_send, in0_send, half(1 - bit[0])))
+    inner = dp == 8 and first_step(dp, width) == 1
+    if inner:
+        acts, dxs, mix_in_grad, mix_out_grad, mlp_up_grad, mlp_down_grad, summed = finish(
+            cargo, *halves, (mlp1, mix1), redo, dp, width
+        )
+    else:
+        acts, dxs, mlp0, mix0, summed = finish(cargo, *halves, None, redo, dp, width)
+        parts = [sum_rest([part], dp, width) for part in (mlp0, mix0, summed)] + [[mlp1], [mix1]]
+        mlp0, mix0, summed, mlp1, mix1 = [
+            sum_section([add_up(part).astype(part[0].dtype)], sections) for part in parts
+        ]
+        mix_big = jnp.stack([mix0, mix1]).reshape(2, share, -1, 3, TILE_C)
+        mix_in_grad = mix_big[:, :, :, :2].transpose(0, 1, 3, 2, 4).reshape(2, share, -1)
+        mix_out_grad = mix_big[:, :, :, 2].reshape(2, share, -1)
+        mlp_big = jnp.stack([mlp0, mlp1]).reshape(2, share, -1, 2, TILE_F)
+        mlp_up_grad = mlp_big[:, :, :, 0].reshape(2, share, -1)
+        mlp_down_grad = mlp_big[:, :, :, 1].reshape(2, share, -1)
+    mix_out_grad = mix_out_grad.transpose(0, 2, 1)
+    mlp_down_grad = mlp_down_grad.transpose(0, 2, 1)
+
+    def with_own(buffer, parts):
+        mine = jnp.where(
+            section < 2, jnp.where(section == 0, parts[0], parts[1]), jnp.where(section == 2, parts[2], parts[3])
+        )
+        here = lax.broadcasted_iota(jnp.int32, (sections, 1, 1), 0) == section
+        return jnp.where(here, mine[None], buffer)[None]
+
+    activations = with_own(acts, xs)
+    input_grads = with_own(dxs, [g0, g1, g2, g3])
+
+    summed = summed.reshape(-1)[:length]
     pieces, at = [], 0
     for a in lines:
         size = a.size // devices
@@ -1041,16 +1256,6 @@
     mix_gain_grad, mlp_gain_grad, down_bias_grad, up_bias_grad, conv = pieces
     conv = conv.reshape(2, 5, -1)
 
-    share = width // devices
-    mix_big = jnp.stack([mix0, mix1]).reshape(2, share, count, 3 * tile)
-    mix_in_grad = (
-        mix_big[..., : 2 * tile].reshape(2, share, count, 2, tile).transpose(0, 1, 3, 2, 4)
-        .reshape(2, share, -1)
-    )
-    mix_out_grad = mix_big[..., 2 * tile :].reshape(2, share, -1).transpose(0, 2, 1)
-    mlp_big = jnp.stack([mlp0, mlp1]).reshape(2, share, -1, 2, TILE_F)
-    mlp_up_grad = mlp_big[:, :, :, 0].reshape(2, share, -1)
-    mlp_down_grad = mlp_big[:, :, :, 1].reshape(2, share, -1).transpose(0, 2, 1)
     return (
         activations, input_grads, final_states, mix_gain_grad, mix_in_grad, conv[:, :4], conv[:, 4],
         mix_out_grad, mlp_gain_grad, mlp_up_grad, up_bias_grad, mlp_down_grad, down_bias_grad,

time: 382 us -> 342 us (0.90); the launches traced: 375 us -> 341 us
  waiting for transfers between devices: 27.7 us -> 0.06 us
  local copies, waits for them, and re-layouts: 33.7 us -> 17 us
  Pallas kernels: 283 us -> 294 us
  starting transfers between devices: 8 us -> 0.26 us
  other arithmetic: 8.23 us -> 15.4 us
    pallas_call x4 -> x2, Pallas kernels: 63.8 us -> 28.3 us  [call(): pl.pallas_call(functools.partial(kernel, lambda: None), grid=grid, in_spe...]
    pallas_call x1, Pallas kernels: 74 us -> 107 us  [finish(): pl.pallas_call(functools.partial(last_kernel, cargo.jobs, first_step(dp,...]
    ppermute x3 -> x0, waiting for transfers between devices: 27 us -> none  [permute(): return lax.ppermute(x, axis, pairs)]
    pallas_call x4 -> x6, Pallas kernels: 145 us -> 159 us  [call(): pl.pallas_call(carrying, grid=grid, in_specs=list(in_specs) + [ANYWHERE]...]
    broadcast_in_dim x7 -> x3, local copies, waits for them, and re-layouts: 8.33 us -> 1.12 us  [the longest x2 1.12 us: chunk_masks(): return jnp.broadcast_to(rows, (seq + 2 * HALO, LANES))]
    broadcast_in_dim x0 -> x2, other arithmetic: none -> 6.13 us  [the longest x1 6.11 us: with_own(): return jnp.where(here, mine[None], buffer)[None]]
    ppermute x3 -> x0, starting transfers between devices: 4.39 us -> none  [permute(): return lax.ppermute(x, axis, pairs)]
    select_n x0 -> x2, other arithmetic: none -> 3.88 us  [with_own(): jnp.where(section < 2, jnp.where(section == 0, parts[0], parts[1]), jnp.w...]
  transfers between devices with their start and end apart: 6 -> 2, of which waited for: 2 -> 0; matrix products, arithmetic and copies ran while one was open for 3% -> 3% of each run, Pallas kernels for 39% -> 27%
where the time goes in v3:
time: 342 us; the launch traced here: 341 us
  Pallas kernels  294 us (86%)
  local copies, waits for them, and re-layouts  17 us (5%)
  other arithmetic  15.4 us (5%)
  between operations  14.5 us (4%)
    pallas_call x6, Pallas kernels, call(): pl.pallas_call(carrying, grid=grid, in_specs=list(in_specs) + [ANYWHERE]...  159 us
    pallas_call x1, Pallas kernels, finish(): pl.pallas_call(functools.partial(last_kernel, cargo.jobs, first_step(dp,...  107 us
    pallas_call x2, Pallas kernels, call(): pl.pallas_call(functools.partial(kernel, lambda: None), grid=grid, in_spe...  28.3 us
  transfers between devices with their start and end apart: 2, of which 0 were waited for; matrix products, arithmetic and copies ran while one was open for 3% of the time, Pallas kernels for 27%

profile of v3, /device:TPU:0, one launch (start us, length us, event | category | flops | bytes accessed | tf_op | source)
XLA Modules:
  0.0 341.5 jit_solution(12692311600762058433)
XLA Ops:
  7.2 0.7 subtract_convert_fusion
  8.0 0.6 copy.63
  8.8 0.1 copy.47
  8.9 0.1 broadcast_in_dim.61
  9.0 3.0 dynamic-slice_bitcast_fusion
  12.0 1.0 broadcast_in_dim.62.keep_ref.refs_9_.refs_8_
  13.0 17.8 %mixer_forward.2 = (bf16[1024,512]{1,0:T(8,128)(2,1)}, bf16[2,1024,1024]{2,1,0:T(8,128)(2,1)}, bf16[1024,1024]{1,0:T(8,128)(2,1)}, bf16[1024,1024]{1,0:T(8,128)(...) custom-call(bf16[1024,512]{1,0:T(8,128)(2,1)} %get-tuple-element.176.x_ref.refs_0_, f32[2,512]{1,0:T(2,128)} %refs_2_.11, ...), custom_call_target="tpu_custom_call" | custom-call | flops 16499999744 | bytes 4194304 | tf_op jit(solution)/shard_map/mixer_forward/pallas_call | solution.py:584
  30.8 10.5 %mlp_forward.2 = (bf16[1024,512]{1,0:T(8,128)(2,1)}, bf16[1024,2048]{1,0:T(8,128)(2,1)}) custom-call(bf16[1024,512]{1,0:T(8,128)(2,1)} %get-tuple-element.66.x_ref.refs_11_.refs_6_.refs_7_.refs_15_.refs_0_, f32[2,512]{1,0:T(2,128)} %refs_15_.1, bf16[2,512,2048]{2,1,0:T(8,128)(2,1)} %refs_13_.1, f32[2,2048]{1,0:T(2,128)} %refs_16_.1, ...), custom_call_target="tpu_custom_call" | custom-call | flops 11000000512 | bytes 4194304 | tf_op jit(solution)/shard_map/mlp_forward/pallas_call | solution.py:584
  41.3 23.1 %mixer_forward.3 = (bf16[1024,512]{1,0:T(8,128)(2,1)}, bf16[2,1024,1024]{2,1,0:T(8,128)(2,1)}, bf16[1024,1024]{1,0:T(8,128)(2,1)}, bf16[1024,1024]{1,0:T(8,128)(...) custom-call(bf16[1024,512]{1,0:T(8,128)(2,1)} %get-tuple-element.67.refs_0_.refs_12_.refs_7_.refs, ...), custom_call_target="tpu_custom_call" | custom-call | flops 16499999744 | bytes 4194304 | tf_op jit(solution)/shard_map/mixer_forward/pallas_call | solution.py:621
  64.5 0.7 maximum_maximum_fusion
  65.2 0.6 slice_bitcast_fusion
  65.8 13.5 %mlp_forward.3 = (bf16[1024,512]{1,0:T(8,128)(2,1)}, bf16[1024,2048]{1,0:T(8,128)(2,1)}, bf16[4,1024,512]{2,1,0:T(8,128)(2,1)}) custom-call(bf16[1024,512]{1,0:T(8,128)(2,1)} %get-tuple-element.68.refs_0_.refs_8_.refs_9_.refs_17_, f32[2,512]{1,0:T(2,128)} %refs_15_.1, bf16[2,512,2048]{2,1,0:T(8,128)(2,1)} %refs_13_.1, ...), custom_call_target="tpu_custom_call", output_to_operand_aliasing={{2}: (9, {})} | custom-call | flops 11000000512 | bytes 4194304 | tf_op jit(solution)/shard_map/mlp_forward/pallas_call | solution.py:621
  79.3 28.7 %mlp_backward.2 = (bf16[512,4096]{1,0:T(8,128)(2,1)}, bf16[1024,512]{1,0:T(8,128)(2,1)}, f32[1,2048]{1,0:T(1,128)}, f32[1,512]{1,0:T(1,128)}, f32[1,512]{1,0:T(1...) custom-call(bf16[1024,512]{1,0:T(8,128)(2,1)} %get-tuple-element.68.refs_0_.refs_8_.r, ...), custom_call_target="tpu_custom_call", output_to_operand_aliasing={{5}: (15, {})} | custom-call | flops 22000001024 | bytes 4194304 | tf_op jit(solution)/shard_map/mlp_backward/pallas_call | solution.py:621
  108.1 0.2 reduce-scatter.5.cloned.1.call-start
  108.3 33.9 %mixer_backward.2 = (bf16[512,3072]{1,0:T(8,128)(2,1)}, bf16[1024,512]{1,0:T(8,128)(2,1)}, f32[2,8,1024]{2,1,0:T(8,128)}, f32[1,512]{1,0:T(1,128)}, bf16[4,1024,512]{2,1,0:T(8,128)(2,1)}) custom-call(bf16[1024,512]{1,0:T(8,128)(2,1)} %get-tuple-element.67.refs_0_.refs_12_.refs_7_.refs_8_.refs_16_, ...), custom_call_target="tpu_custom_call", output_to_operand_aliasing={{4}: (19, {})} | custom-call | flops 32999999488 | bytes 4194304 | tf_op jit(solution)/shard_map/mixer_backward/pallas_call | solution.py:621
  142.3 26.3 %mlp_backward.3 = (bf16[256,4096]{1,0:T(8,128)(2,1)}, bf16[256,4096]{1,0:T(8,128)(2,1)}, bf16[1024,512]{1,0:T(8,128)(2,1)}, f32[1,2048]{1,0:T(1,128)}, f32[1,512...) custom-call(bf16[1024,512]{1,0:T(8,128)(2,1)} %get-tuple-element.66.x_ref.refs_1, ...), custom_call_target="tpu_custom_call", output_to_operand_aliasing={{6}: (11, {})} | custom-call | flops 22000001024 | bytes 4194304 | tf_op jit(solution)/shard_map/mlp_backward/pallas_call | solution.py:621
  168.7 0.8 fusion.4
  169.5 0.6 copy.58
  170.2 0.7 pad_maximum_fusion
  170.9 0.1 reshape.117
  171.0 0.1 reshape.118
  171.1 0.7 pad_maximum_fusion.3
  172.0 0.7 pad_maximum_fusion.2
  172.7 0.1 reshape.113
  173.0 2.5 select_select_fusion.1
  175.5 33.6 %mixer_backward.3 = (bf16[256,3072]{1,0:T(8,128)(2,1)}, bf16[256,3072]{1,0:T(8,128)(2,1)}, bf16[1024,512]{1,0:T(8,128)(2,1)}, f32[2,8,1024]{2,1,0:T(8,128)}, f32...) custom-call(bf16[1024,512]{1,0:T(8,128)(2,1)} %get-tuple-element.176, ...), custom_call_target="tpu_custom_call", output_to_operand_aliasing={{5}: (22, {})} | custom-call | flops 32999999488 | bytes 4194304 | tf_op jit(solution)/shard_map/mixer_backward/pallas_call | solution.py:621
  209.1 0.8 pad_maximum_fusion.1
  210.1 0.9 copy.52
  211.1 0.1 reshape.119
  211.2 0.1 reshape_reshape.6
  211.3 0.1 copy.54
  211.4 0.1 reshape.120
  211.5 0.1 concatenate.20
  211.7 0.7 constant_dynamic-slice_fusion
  212.4 1.4 select_select_fusion
  213.9 107.1 %finish.1 = (bf16[4,1024,512]{2,1,0:T(8,128)(2,1)}, bf16[4,1024,512]{2,1,0:T(8,128)(2,1)}, f32[2,16,2048]{2,1,0:T(8,128)}, f32[2,16,1024]{2,1,0:T(8,128)}, f32[2...) custom-call(bf16[1024,512]{1,0:T(8,128)(2,1)} %get-tuple-element.75., ...), custom_call_target="tpu_custom_call", output_to_operand_aliasing={{0}: (18, {}), {1}: (19, {})} | custom-call | flops 109999996928 | bytes 4194304 | tf_op jit(solution)/shard_map/finish/pallas_call | solution.py:1058
  321.0 0.8 slice.64
  321.7 0.8 slice.60
  322.6 0.6 slice.62
  323.1 0.6 slice.61
  323.7 0.8 slice.48
  324.5 0.6 reshape.127
  325.1 0.6 fusion.5
  325.8 6.1 %select_bitcast_fusion = (bf16[1,4,1024,512]{3,2,1,0:T(8,128)(2,1)}, bf16[1,4,1024,512]{3,2,1,0:T(8,128)(2,1)}) fusion(bf16[4,1024,512]{2,1,0:T(8,128)(2,1)} %get-tuple-element.112, pred[4]{0:T(512)(128)(4,1)S(1)} %copy-done.16, bf16[1024,512]{1,0:T(8,128)(2,1)S(1)} %select_select_fusion, bf16[4,1024,512]{2,1,0:T(8,128)(2,1)} %get-tuple-element.111, ...), kind=kLoop, calls=%fused_computation | loop fusion | flops 4194304 | bytes 18874372 | tf_op jit(solution)/shard_map/broadcast_in_dim | solution.py:1245
  331.9 0.7 copy.75
  332.6 0.7 copy.76
  333.2 0.7 copy.77
  333.9 0.7 copy.78
  (67 shorter events, 1.3 us)
Async XLA Ops:
  7.2 0.8 copy-start
  7.2 168.3 %reduce-scatter.3.cloned.1.call-start = ((), (), s32[]{:S(2)}) async-start(), calls=%async_computation.2 | async-start | bytes 4718592 | tf_op jit(solution)/shard_map/reduce_scatter | solution.py:1177
  41.3 23.2 %copy-start.14 = (f32[1,1024]{1,0:T(1,128)S(1)}, f32[1,1024]{1,0:T(1,128)}, u32[]{:S(2)}) copy-start(f32[1,1024]{1,0:T(1,128)} %get-tuple-element.72) | copy-start | bytes 12292
  108.1 105.8 %reduce-scatter.5.cloned.1.call-start = ((), (), s32[]{:S(2)}) async-start(), calls=%async_computation.3 | async-start | bytes 3538944 | tf_op jit(solution)/shard_map/reduce_scatter | solution.py:1182
  142.2 26.5 %copy-start.15 = (pred[4]{0:T(512)(128)(4,1)}, pred[4]{0:T(512)(128)(4,1)S(1)}, u32[]{:S(2)}) copy-start(pred[4]{0:T(512)(128)(4,1)S(1)} %iota_compare_fusion.2) | copy-start | bytes 16
  142.3 27.9 %copy-start.12 = (f32[2,8,1024]{2,1,0:T(8,128)S(1)}, f32[2,8,1024]{2,1,0:T(8,128)}, u32[]{:S(2)}) copy-start(f32[2,8,1024]{2,1,0:T(8,128)} %get-tuple-element.104) | copy-start | bytes 196612
  142.3 27.9 %copy-start.13 = (f32[1,2048]{1,0:T(1,128)S(1)}, f32[1,2048]{1,0:T(1,128)}, u32[]{:S(2)}) copy-start(f32[1,2048]{1,0:T(1,128)} %get-tuple-element.102) | copy-start | bytes 24580
  142.3 28.8 %copy-start.19 = (f32[1,512]{1,0:T(1,128)S(1)}, f32[1,512]{1,0:T(1,128)}, u32[]{:S(2)}) copy-start(f32[1,512]{1,0:T(1,128)} %get-tuple-element.100) | copy-start | bytes 6148
  142.3 29.7 %copy-start.18 = (f32[1,512]{1,0:T(1,128)S(1)}, f32[1,512]{1,0:T(1,128)}, u32[]{:S(2)}) copy-start(f32[1,512]{1,0:T(1,128)} %get-tuple-element.98) | copy-start | bytes 6148
  142.3 30.7 %copy-start.4 = (bf16[1024,512]{1,0:T(8,128)(2,1)S(1)}, bf16[1024,512]{1,0:T(8,128)(2,1)}, u32[]{:S(2)}) copy-start(bf16[1024,512]{1,0:T(8,128)(2,1)} %get-tuple-element.66.x_ref.refs_11_.refs_6_.refs_7_.refs_15_.refs_0_) | copy-start | bytes 3145732
  142.3 30.7 %copy-start.5 = (bf16[1024,512]{1,0:T(8,128)(2,1)S(1)}, bf16[1024,512]{1,0:T(8,128)(2,1)}, u32[]{:S(2)}) copy-start(bf16[1024,512]{1,0:T(8,128)(2,1)} %get-tuple-element.67.refs_0_.refs_12_.refs_7_.refs_8_.refs_16_) | copy-start | bytes 3145732
  142.3 30.7 %copy-start.7 = (bf16[1024,512]{1,0:T(8,128)(2,1)S(1)}, bf16[1024,512]{1,0:T(8,128)(2,1)}, u32[]{:S(2)}) copy-start(bf16[1024,512]{1,0:T(8,128)(2,1)} %get-tuple-element.68.refs_0_.refs_8_.refs_9_.refs_17_) | copy-start | bytes 3145732
  175.5 33.6 %copy-start.17 = (f32[1,512]{1,0:T(1,128)S(1)}, f32[1,512]{1,0:T(1,128)}, u32[]{:S(2)}) copy-start(f32[1,512]{1,0:T(1,128)} %get-tuple-element.96) | copy-start | bytes 6148
  209.1 3.4 copy-start.3
  209.1 3.4 copy-start.6
  213.9 111.8 %copy-start.2 = (bf16[1024,512]{1,0:T(8,128)(2,1)S(1)}, bf16[1024,512]{1,0:T(8,128)(2,1)}, u32[]{:S(2)}) copy-start(bf16[1024,512]{1,0:T(8,128)(2,1)} %select_select_fusion.1) | copy-start | bytes 3145732
  213.9 111.8 %copy-start.16 = (pred[4]{0:T(512)(128)(4,1)S(1)}, pred[4]{0:T(512)(128)(4,1)}, u32[]{:S(2)}) copy-start(pred[4]{0:T(512)(128)(4,1)} %copy-done.15) | copy-start | bytes 16
  325.7 6.2 %copy-start.10 = (f32[2,16,2048]{2,1,0:T(8,128)S(1)}, f32[2,16,2048]{2,1,0:T(8,128)}, u32[]{:S(2)}) copy-start(f32[2,16,2048]{2,1,0:T(8,128)} %get-tuple-element.194) | copy-start | bytes 786436
  325.7 6.9 %copy-start.11 = (f32[2,16,1024]{2,1,0:T(8,128)S(1)}, f32[2,16,1024]{2,1,0:T(8,128)}, u32[]{:S(2)}) copy-start(f32[2,16,1024]{2,1,0:T(8,128)} %get-tuple-element.116) | copy-start | bytes 393220
  325.7 7.5 %copy-start.9 = (f32[2,16,2048]{2,1,0:T(8,128)S(1)}, f32[2,16,2048]{2,1,0:T(8,128)}, u32[]{:S(2)}) copy-start(f32[2,16,2048]{2,1,0:T(8,128)} %get-tuple-element.199) | copy-start | bytes 786436
  325.7 8.2 %copy-start.8 = (f32[2,16,2048]{2,1,0:T(8,128)S(1)}, f32[2,16,2048]{2,1,0:T(8,128)}, u32[]{:S(2)}) copy-start(f32[2,16,2048]{2,1,0:T(8,128)} %get-tuple-element.118) | copy-start | bytes 786436
  325.8 8.9 %copy-start.1 = (f32[2,4,1024]{2,1,0:T(4,128)S(1)}, f32[2,4,1024]{2,1,0:T(4,128)}, u32[]{:S(2)}) copy-start(f32[2,4,1024]{2,1,0:T(4,128)} %param.16) | copy-start | bytes 98308
Sparse Core Ops, SparseCore 0:
  108.2 51.6 reduce-scatter.2
  163.6 46.2 reduce-scatter.4
